TPU v7x, 32 devices: a whole 2x2x4 slice. The times are simulated.
32 devices in a mesh: group: 2 (over y), seq: 8 (over z, x), exp: 2 (over core).
Axes of the slice: x: 2, y: 2, z: 4, core: 2. Of those that a mesh axis runs over, the one named last changes fastest.
Arguments:
- tokens: bfloat16 [4096, 2048], P(('group', 'seq'), 'exp'), parts along dimension 0, may hold values from -20 to 20
- upstream: bfloat16 [4096, 2048], P(('group', 'seq'), 'exp'), parts along dimension 0, may hold values from -6 to 6
- slot_params: bfloat16 [64, 2048], P(('group', 'seq'), 'exp'), parts along dimension 0, may hold values from -3 to 3
- slot_outputs: bfloat16 [64, 2048], P(('group', 'seq', 'exp')), parts along dimension 0, may hold values from -6 to 6
- slot_input_grads: bfloat16 [64, 2048], P(('group', 'seq', 'exp')), parts along dimension 0, may hold values from -384 to 384
Outputs:
- token_grads: bfloat16 [4096, 2048], P(('group', 'seq'), 'exp'), parts along dimension 0
- param_grads: float32 [64, 2048], P(('group', 'seq'), 'exp'), parts along dimension 0
- slot_output_grads: float32 [64, 2048], P(('group', 'seq', 'exp')), parts along dimension 0
There are 2 independent parts, one for each index of `group`. A program takes and returns all parts, laid end to end along the dimension named above; each array names one. Nothing has to cross between parts.
All inputs are finite; a program needn't handle non-finite values.
Results may differ from a plain program's by a relative error of at most 0.0052.
Values may be sent and summed in bfloat16 or wider, within the bound.
No kernel may reach another device: no remote copies, remote signals or barrier semaphores. Data moves between devices by JAX's collectives and lax.ppermute only.
A program may use at most 64 MiB of HBM per device.

v0:
```python
import jax
import jax.numpy as jnp
from jax import lax
from jax.sharding import PartitionSpec as P


def contract_last(left, right):
    return lax.dot_general(
        left, right, (((1,), (1,)), ((), ())), preferred_element_type=jnp.float32
    )


def contract_first(left, right):
    return lax.dot_general(
        left, right, (((0,), (0,)), ((), ())), preferred_element_type=jnp.float32
    )


def shards(tokens, upstream, slot_params, slot_outputs, slot_input_grads):
    half = tokens.shape[1]
    side = lax.axis_index("exp")
    params = lax.all_gather(slot_params, "seq", axis=0, tiled=True)
    outs_all, grads_all = (
        lax.all_gather(slot_outputs, ("seq", "exp"), axis=0, tiled=True),
        lax.all_gather(slot_input_grads, ("seq", "exp"), axis=0, tiled=True),
    )
    outs_half = lax.dynamic_slice_in_dim(outs_all, side * half, half, 1)
    grads_half = lax.dynamic_slice_in_dim(grads_all, side * half, half, 1)
    logit_part = contract_last(tokens, params)
    comb_part = contract_last(upstream, outs_half)
    disp_part = contract_last(tokens, grads_half)
    logits = lax.psum(logit_part, "exp")
    d_comb, d_disp = lax.psum((comb_part, disp_part), "exp")
    row_top = jnp.max(logits, axis=1, keepdims=True)
    row_exp = jnp.exp(logits - row_top)
    combine = row_exp / jnp.sum(row_exp, axis=1, keepdims=True)
    col_top = lax.pmax(jnp.max(logits, axis=0), "seq")
    col_exp = jnp.exp(logits - col_top[None, :])
    col_sum = lax.psum(jnp.sum(col_exp, axis=0), "seq")
    dispatch = col_exp / col_sum[None, :]
    combine_b = combine.astype(jnp.bfloat16)
    dispatch_b = dispatch.astype(jnp.bfloat16)
    columns = combine_b
    slot_sums = lax.psum_scatter(
        contract_first(columns, upstream), "seq", scatter_dimension=0, tiled=True
    )
    slot_output_grads = lax.all_to_all(slot_sums, "exp", split_axis=0, concat_axis=1, tiled=True)
    row_inner = jnp.sum(combine * d_comb, axis=1, keepdims=True)
    col_inner = lax.psum(jnp.sum(dispatch * d_disp, axis=0), "seq")
    d_logit = combine * (d_comb - row_inner) + dispatch * (d_disp - col_inner[None, :])
    d_logit_b = d_logit.astype(jnp.bfloat16)
    token_grads = jnp.dot(dispatch_b, grads_half, preferred_element_type=jnp.float32)
    token_grads = token_grads + jnp.dot(d_logit_b, params, preferred_element_type=jnp.float32)
    columns = d_logit_b
    param_grads = lax.psum_scatter(
        contract_first(columns, tokens), "seq", scatter_dimension=0, tiled=True
    )
    return (token_grads.astype(jnp.bfloat16), param_grads, slot_output_grads)


def solution(mesh):
    in_specs = (
        P(("group", "seq"), "exp"),
        P(("group", "seq"), "exp"),
        P(("group", "seq"), "exp"),
        P(("group", "seq", "exp"), None),
        P(("group", "seq", "exp"), None),
    )
    out_specs = (
        P(("group", "seq"), "exp"),
        P(("group", "seq"), "exp"),
        P(("group", "seq", "exp"), None),
    )
    return jax.shard_map(shards, mesh=mesh, in_specs=in_specs, out_specs=out_specs, check_vma=False)
```

profile of v0, /device:TPU:0, one launch (start us, length us, event | category | flops | bytes accessed | tf_op | source)
XLA Modules:
  0.0 243.1 jit_solution(1687349543499199279)
XLA Ops:
  7.2 0.0 copy-start
  7.2 0.0 all-reduce.9.cloned.1.call-start
  7.2 23.8 %all-gather.1 = bf16[16,2,2048]{2,1,0:T(2,128)(2,1)S(1)} all-gather(bf16[1,2,2048]{2,1,0:T(2,128)(2,1)} %bitcast.19), channel_id=1, replica_groups=mesh['group'=2,'seq'=8,'exp'=2] {'seq','exp'}, dimensions={0}, use_global_device_ids=true | all-gather | bytes 139264 | tf_op jit(solution)/shard_map/all_gather | solution.py:25
  31.0 0.1 reshape.18
  31.1 0.0 copy-start.5
  31.1 0.7 copy-done.5
  31.8 30.5 %all-gather = bf16[8,4,1024]{2,1,0:T(4,128)(2,1)S(1)} all-gather(bf16[1,4,1024]{2,1,0:T(4,128)(2,1)S(1)} %bitcast.20), channel_id=1, replica_groups=mesh['group'=2,'seq'=8,'exp'=2] {'seq'}, dimensions={0}, use_global_device_ids=true | all-gather | bytes 73728 | tf_op jit(solution)/shard_map/all_gather | solution.py:22
  62.3 0.0 copy-start.6
  62.3 0.7 copy-done.6
  63.0 17.5 %all-gather.2 = bf16[16,2,2048]{2,1,0:T(2,128)(2,1)S(1)} all-gather(bf16[1,2,2048]{2,1,0:T(2,128)(2,1)S(1)} %bitcast.21), channel_id=1, replica_groups=mesh['group'=2,'seq'=8,'exp'=2] {'seq','exp'}, dimensions={0}, use_global_device_ids=true | all-gather | bytes 139264 | tf_op jit(solution)/shard_map/all_gather | solution.py:24
  80.4 0.1 reshape.20
  80.5 0.0 copy-done
  80.5 0.0 copy-start.1
  80.5 0.9 fusion.19
  81.4 0.9 convolution_bitcast_fusion
  82.3 0.0 copy-done.1
  82.3 0.9 convolution_bitcast_fusion.1
  83.1 0.0 all-reduce.9.cloned.1.call-update
  83.2 0.0 all-reduce.7.cloned.1.call-start
  83.2 0.0 copy-start.7
  83.2 0.6 copy-done.7
  83.9 0.6 dynamic-slice
  85.1 15.0 %all-reduce.9.cloned.1.call-done = (f32[256,32]{0,1:T(8,128)}, f32[256,32]{0,1:T(8,128)}, f32[256,32]{0,1:T(8,128)}) async-done(((f32[256,32]{0,1:T(8,128)}, f32[256,32]{0,1:T(8,128)}, f32[256,32]{0,1:T(8,128)}), (f32[256,32]{0,1:T(8,128)}, f32[256,32]{0,1:T(8,128)}, f32[256,32]{0,1:T(8,128)})) %all-reduce.9.cloned.1.call-update) | async-done | bytes 98320 | tf_op jit(solution)/shard_map/psum | solution.py:32
  100.1 0.0 copy-start.2
  100.1 1.0 fusion.17
  101.0 21.6 %pmax.7 = f32[32]{0:T(128)S(1)} all-reduce(f32[32]{0:T(128)S(1)} %get-tuple-element.8), channel_id=1, replica_groups=mesh['group'=2,'seq'=8,'exp'=2] {'seq'}, use_global_device_ids=true, to_apply=%region_2.0 | all-reduce | flops 32 | bytes 256 | tf_op jit(solution)/shard_map/pmax | solution.py:37
  122.7 0.0 copy-done.2
  122.7 0.2 fusion.8
  122.9 17.1 %psum.36 = f32[32]{0:T(128)S(1)} all-reduce(f32[32]{0:T(128)S(1)} %get-tuple-element.6), channel_id=1, replica_groups=mesh['group'=2,'seq'=8,'exp'=2] {'seq'}, use_global_device_ids=true, to_apply=%region_4.0 | all-reduce | flops 32 | bytes 256 | tf_op jit(solution)/shard_map/psum | solution.py:39
  140.0 0.4 fusion.3
  140.4 0.0 copy-start.3
  140.4 0.0 copy-start.4
  140.4 0.8 fusion.9
  141.2 0.0 copy-done.3
  141.2 0.0 copy-done.4
  141.2 0.2 multiply_reduce_fusion.1
  141.4 19.1 %psum.39 = f32[32]{0:T(128)S(1)} all-reduce(f32[32]{0:T(128)S(1)} %get-tuple-element.4), channel_id=1, replica_groups=mesh['group'=2,'seq'=8,'exp'=2] {'seq'}, use_global_device_ids=true, to_apply=%region_11.0 | all-reduce | flops 32 | bytes 256 | tf_op jit(solution)/shard_map/psum | solution.py:49
  160.6 0.9 fusion.18
  161.5 0.0 all-reduce.7.cloned.1.call-update
  161.5 1.2 fusion
  162.7 67.0 %all-reduce.7.cloned.1.call-done = (f32[32,1024]{1,0:T(8,128)}, f32[32,1024]{1,0:T(8,128)}) async-done(((f32[32,1024]{1,0:T(8,128)}, f32[32,1024]{1,0:T(8,128)}), (f32[32,1024]{1,0:T(8,128)}, f32[32,1024]{1,0:T(8,128)})) %all-reduce.7.cloned.1.call-update) | async-done | bytes 262160
  229.7 1.4 constant_dynamic-slice_fusion.1
  231.1 0.8 constant_dynamic-slice_fusion
  231.9 3.7 %all_to_all.19 = f32[2,2,1024]{2,1,0:T(2,128)S(1)} all-to-all(f32[2,2,1024]{2,1,0:T(2,128)S(1)} %all_to_all.14), channel_id=1, replica_groups=mesh['group'=2,'seq'=8,'exp'=2] {'exp'}, dimensions={0} | all-to-all | bytes 32768 | tf_op jit(solution)/shard_map/all_to_all | solution.py:47
  235.6 0.6 copy.16
  (2 shorter events, 0.0 us)
Async XLA Ops:
  7.2 73.3 %copy-start = (bf16[256,1024]{1,0:T(8,128)(2,1)S(1)}, bf16[256,1024]{1,0:T(8,128)(2,1)}, u32[]{:S(2)}) copy-start(bf16[256,1024]{1,0:T(8,128)(2,1)} %param.5) | copy-start | bytes 1572868
  7.2 92.9 %all-reduce.9.cloned.1.call-start = ((), (), s32[]{:S(2)}) async-start(), calls=%async_computation.2 | async-start | bytes 196608 | tf_op jit(solution)/shard_map/psum | solution.py:32
  31.1 0.7 copy-start.5
  62.3 0.7 copy-start.6
  80.5 1.8 copy-start.1
  83.2 146.6 %all-reduce.7.cloned.1.call-start = ((), (), s32[]{:S(2)}) async-start(), calls=%async_computation.1 | async-start | bytes 524288
  83.2 0.7 copy-start.7
  100.1 22.6 %copy-start.2 = (f32[256,32]{0,1:T(8,128)S(1)}, f32[256,32]{0,1:T(8,128)}, u32[]{:S(2)}) copy-start(f32[256,32]{0,1:T(8,128)} %get-tuple-element.11) | copy-start | bytes 98308
  140.4 0.9 copy-start.3
  140.4 0.8 copy-start.4
Sparse Core Ops, SparseCore 0:
  83.3 16.7 all-reduce.8
  161.6 68.0 all-reduce.6
where the time goes:
time: 244 us; the launch traced here: 243 us
  blocking collectives  133 us (55%)
  waiting for transfers between devices  82 us (34%)
  between operations  14.8 us (6%)
  matrix products  5.94 us (2%)
  local copies, waits for them, and re-layouts  5.5 us (2%)
    unnamed x3, waiting for transfers between devices  67.1 us
    all_gather x1, blocking collectives, shards(): params = lax.all_gather(slot_params, 'seq', axis=0, tiled=True)  30.5 us
    all_gather x1, blocking collectives, shards(): lax.all_gather(slot_input_grads, ('seq', 'exp'), axis=0, tiled=True)  23.8 us
    pmax x1, blocking collectives, shards(): col_top = lax.pmax(jnp.max(logits, axis=0), 'seq')  21.6 us
    psum x1, blocking collectives, shards(): col_inner = lax.psum(jnp.sum(dispatch * d_disp, axis=0), 'seq')  19.1 us
    all_gather x1, blocking collectives, shards(): lax.all_gather(slot_outputs, ('seq', 'exp'), axis=0, tiled=True)  17.5 us
    psum x1, blocking collectives, shards(): col_sum = lax.psum(jnp.sum(col_exp, axis=0), 'seq')  17.1 us
    psum x1, waiting for transfers between devices, shards(): logits = lax.psum(logit_part, 'exp')  15 us
  transfers between devices with their start and end apart: 2, of which 2 were waited for; matrix products, arithmetic and copies ran while one was open for 1% of the time, Pallas kernels for 0%

commit v1 on v0

v1 whole, which is shorter than its diff:
```python
import functools

import jax
import jax.numpy as jnp
from jax import lax
from jax.experimental import pallas as pl
from jax.experimental.pallas import tpu as pltpu
from jax.sharding import PartitionSpec as P

F32 = jnp.float32
BF16 = jnp.bfloat16


def dot_nt(left, right):
    return lax.dot_general(left, right, (((1,), (1,)), ((), ())), preferred_element_type=F32)


def dot_tn(left, right):
    return lax.dot_general(left, right, (((0,), (0,)), ((), ())), preferred_element_type=F32)


def call(kernel, outs, name, seq, scratch=()):
    return pl.pallas_call(
        kernel,
        out_shape=outs,
        scratch_shapes=list(scratch),
        compiler_params=pltpu.CompilerParams(vmem_limit_bytes=(16 if seq <= 16 else 48) << 20),
        name=name,
    )


def split16(value):
    high = value.astype(BF16).astype(F32)
    return high, (value - high).astype(BF16).astype(F32)


def pack_kernel(params_ref, outs_ref, grads_ref, chunks_ref):
    half = params_ref.shape[1]
    quarter = half // 2
    params = params_ref[...].astype(F32)
    outs = outs_ref[...].astype(F32)
    grads = grads_ref[...].astype(F32)
    for core in range(2):
        span = slice(core * half, (core + 1) * half)
        rows = jnp.concatenate([params, outs[:, span], grads[:, span]], axis=0)
        chunk = jnp.concatenate([rows[:, :quarter], rows[:, quarter:]], axis=0).astype(BF16)
        for dest in range(chunks_ref.shape[0] // 2):
            chunks_ref[2 * dest + core] = chunk


def partial_kernel(slots_ref, tokens_ref, upstream_ref, part_ref):
    side = lax.axis_index("exp")
    devices, _, quarter = slots_ref.shape
    n_slots = part_ref.shape[0] // 3
    rows = slots_ref[...].reshape(devices * 16, quarter)

    def halves(right_ref):
        first = dot_nt(rows, right_ref[:, :quarter]).reshape(devices, 16, -1)
        second = dot_nt(rows, right_ref[:, quarter:]).reshape(devices, 16, -1)
        return first[:, :8] + second[:, 8:]

    by_tokens = halves(tokens_ref)
    by_upstream = halves(upstream_ref)
    for chip in range(devices // 2):
        a, b = 2 * chip, 2 * chip + 1
        own = jnp.where(side == 0, by_tokens[a], by_tokens[b])
        base = 4 * chip
        part_ref[base : base + 4, :] = own[0:4]
        for device, at in ((a, base), (b, base + 2)):
            part_ref[n_slots + at : n_slots + at + 2, :] = by_upstream[device][4:6]
            part_ref[2 * n_slots + at : 2 * n_slots + at + 2, :] = by_tokens[device][6:8]


def local_kernel(
    mine_ref, other_ref, tokens_ref, upstream_ref, send_ref, col_ref, row_ref, disp_ref, up_ref, tok_ref
):
    n_slots = col_ref.shape[0]
    seq, _, width = send_ref.shape
    half = tokens_ref.shape[1]
    extra = width - half
    groups = n_slots // 16 + 1
    both = mine_ref[...] + other_ref[...]
    logits, d_comb, d_disp = both[:n_slots], both[n_slots : 2 * n_slots], both[2 * n_slots :]
    row_exp = jnp.exp(logits - jnp.max(logits, axis=0, keepdims=True))
    combine = row_exp / jnp.sum(row_exp, axis=0, keepdims=True)
    row_part = combine * (d_comb - jnp.sum(combine * d_comb, axis=0, keepdims=True))
    top_high, top_low = split16(jnp.max(logits, axis=1, keepdims=True))
    col_exp = jnp.exp(logits - (top_high + top_low))
    sum_high, sum_low = split16(jnp.sum(col_exp, axis=1, keepdims=True))
    inner_high, inner_low = split16(jnp.sum(col_exp * d_disp, axis=1, keepdims=True))
    centre = (inner_high + inner_low) / (sum_high + sum_low)
    col_part = col_exp * (d_disp - centre)
    col_ref[...] = col_exp
    row_ref[...] = row_part
    disp_ref[...] = d_disp

    up_ref[...] = jnp.zeros_like(up_ref)
    tok_ref[...] = jnp.zeros_like(tok_ref)
    for chip in range(seq):
        span = slice(4 * chip, 4 * chip + 4)
        base = 16 * chip
        up_ref[base : base + 4, :] = combine[span]
        tok_ref[base + 4 : base + 8, :] = row_part[span]
        tok_ref[base + 8 : base + 12, :] = col_part[span]
        tok_ref[base + 12 : base + 16, :] = col_exp[span]
    sums = jnp.dot(up_ref[...].astype(BF16), upstream_ref[...], preferred_element_type=F32)
    sums = sums + jnp.dot(tok_ref[...].astype(BF16), tokens_ref[...], preferred_element_type=F32)
    send_ref[:, :, :half] = sums.astype(BF16).reshape(seq, 16, half)

    lane = lax.broadcasted_iota(jnp.int32, (n_slots, extra), 1)
    stats = jnp.zeros((n_slots, extra), F32)
    for j, stat in enumerate((top_high, top_low, sum_high, sum_low, inner_high, inner_low)):
        stats = jnp.where(lane == j * groups, stat, stats)
    every = jnp.zeros((16, extra), F32)
    for group in range(groups - 1):
        every = every + pltpu.roll(stats[16 * group : 16 * group + 16], group + 1, 1)
    for chip in range(seq):
        own = stats[4 * chip : 4 * chip + 4]
        block = every + jnp.concatenate([own, own, own, own], axis=0)
        send_ref[chip, :, half:] = block.astype(BF16)


def column_stats(stats, groups):
    extra = stats.shape[-1]
    axis = stats.ndim - 1
    pair = stats + pltpu.roll(stats, extra - groups, axis)
    return pair, pltpu.roll(pair, extra - 2 * groups, axis), pltpu.roll(pair, extra - 4 * groups, axis)


def merge_stats(got_ref, half, groups):
    seq = got_ref.shape[0]
    tops, totals, inners = [], [], []
    for chip in range(seq):
        top, total, inner = column_stats(got_ref[chip, :, half:].astype(F32), groups)
        tops.append(top)
        totals.append(total)
        inners.append(inner)
    high = functools.reduce(jnp.maximum, tops)
    scales = [jnp.exp(top - high) for top in tops]
    total = sum(scale * value for scale, value in zip(scales, totals))
    inner = sum(scale * value for scale, value in zip(scales, inners))
    weights = [scale / total for scale in scales]
    centres = [value / whole for value, whole in zip(inners, totals)]
    return high, total, inner / total, weights, centres


def sums_kernel(got_ref, params_ref, keep_ref, give_ref, *, groups):
    side = lax.axis_index("exp")
    half = params_ref.shape[1]
    _, _, centre, weights, centres = merge_stats(got_ref, half, groups)
    row = lax.broadcasted_iota(jnp.int32, centre.shape, 0)
    acc = jnp.zeros((16, half), F32)
    for chip, (weight, own) in enumerate(zip(weights, centres)):
        factor = jnp.where(row < 8, 1.0, jnp.where(row < 12, weight, weight * (own - centre)))
        acc = acc + factor[:, 0:1] * got_ref[chip, :, :half].astype(F32)
    params_ref[...] = acc[4:8] + acc[8:12] + acc[12:16]
    keep_ref[...] = jnp.where(side == 0, acc[0:2], acc[2:4])
    give_ref[...] = jnp.where(side == 0, acc[2:4], acc[0:2])


def tokens_kernel(got_ref, slots_ref, col_ref, row_ref, disp_ref, out_ref, left_ref, *, groups):
    side = lax.axis_index("exp")
    me = lax.axis_index("seq")
    half = out_ref.shape[1]
    quarter = half // 2
    devices = slots_ref.shape[0]
    n_slots = col_ref.shape[0]
    high, total, centre, _, _ = merge_stats(got_ref, half, groups)
    mine = got_ref[pl.ds(me, 1), :, half:][0].astype(F32)
    top, _, _ = column_stats(mine, groups)
    weight = jnp.exp(top - high) / total
    left_ref[...] = jnp.zeros_like(left_ref)
    for group in range(n_slots // 16):
        span = slice(16 * group, 16 * group + 16)
        dispatch = col_ref[span] * weight[:, group + 1 : group + 2]
        d_logit = row_ref[span] + dispatch * (disp_ref[span] - centre[:, group + 1 : group + 2])
        for j in range(4):
            chip = 4 * group + j
            ours = d_logit[4 * j : 4 * j + 4]
            left_ref[2 * chip, 0:4] = jnp.where(side == 0, ours, 0.0)
            left_ref[2 * chip + 1, 0:4] = jnp.where(side == 1, ours, 0.0)
            left_ref[2 * chip, 6:8] = dispatch[4 * j : 4 * j + 2]
            left_ref[2 * chip + 1, 6:8] = dispatch[4 * j + 2 : 4 * j + 4]
    left = left_ref[...]
    zero = jnp.zeros_like(left)
    right = slots_ref[...].reshape(devices * 16, quarter)
    for part, order in ((0, (left, zero)), (1, (zero, left))):
        rows = jnp.concatenate(order, axis=1).reshape(devices * 16, -1).astype(BF16)
        out_ref[:, part * quarter : (part + 1) * quarter] = dot_tn(rows, right).astype(out_ref.dtype)


def shards(seq, tokens, upstream, slot_params, slot_outputs, slot_input_grads):
    patches, half = tokens.shape
    n_slots = slot_params.shape[0] * seq
    groups = n_slots // 16 + 1
    extra = -(-6 * groups // 128) * 128
    sds = jax.ShapeDtypeStruct

    chunks = call(pack_kernel, sds((2 * seq, 16, half // 2), BF16), "pack", seq)(
        slot_params, slot_outputs, slot_input_grads
    )
    slots = lax.all_to_all(chunks, ("seq", "exp"), split_axis=0, concat_axis=0, tiled=True)
    part = call(partial_kernel, sds((3 * n_slots, patches), F32), "partial", seq)(slots, tokens, upstream)
    other = lax.ppermute(part, "exp", [(0, 1), (1, 0)])
    by_slot = sds((n_slots, patches), F32)
    send, col, row, disp = call(
        local_kernel,
        (sds((seq, 16, half + extra), BF16), by_slot, by_slot, by_slot),
        "local",
        seq,
        [pltpu.VMEM((16 * seq, patches), F32), pltpu.VMEM((16 * seq, patches), F32)],
    )(part, other, tokens, upstream)
    got = lax.all_to_all(send, "seq", split_axis=0, concat_axis=0, tiled=True)
    pair = sds((2, half), F32)
    param_grads, keep, give = call(
        functools.partial(sums_kernel, groups=groups), (sds((4, half), F32), pair, pair), "sums", seq
    )(got)
    taken = lax.ppermute(give, "exp", [(0, 1), (1, 0)])
    token_grads = call(
        functools.partial(tokens_kernel, groups=groups),
        sds((patches, half), BF16),
        "token_grads",
        seq,
        [pltpu.VMEM((2 * seq, 8, patches), F32)],
    )(got, slots, col, row, disp)
    side = lax.axis_index("exp")
    slot_output_grads = jnp.where(
        side == 0, jnp.concatenate([keep, taken], axis=1), jnp.concatenate([taken, keep], axis=1)
    )
    return token_grads, param_grads, slot_output_grads


def solution(mesh):
    in_specs = (
        P(("group", "seq"), "exp"),
        P(("group", "seq"), "exp"),
        P(("group", "seq"), "exp"),
        P(("group", "seq", "exp"), None),
        P(("group", "seq", "exp"), None),
    )
    out_specs = (
        P(("group", "seq"), "exp"),
        P(("group", "seq"), "exp"),
        P(("group", "seq", "exp"), None),
    )
    return jax.shard_map(
        functools.partial(shards, mesh.shape["seq"]),
        mesh=mesh,
        in_specs=in_specs,
        out_specs=out_specs,
        check_vma=False,
    )
```

time: 244 us -> 40.1 us (0.16)
  blocking collectives: 133 us -> 30.6 us
  waiting for transfers between devices: 82 us -> 1.29 us
  between operations: 14.8 us -> 0.68 us
  matrix products: 5.94 us -> 0 us
  Pallas kernels: 0 us -> 3.21 us
    all_gather x3 -> x0, blocking collectives: 71.7 us -> none  [the longest x1 30.5 us: shards(): params = lax.all_gather(slot_params, 'seq', axis=0, tiled=True)]
    unnamed x3 -> x0, waiting for transfers between devices: 67.1 us -> none
    psum x2 -> x0, blocking collectives: 36.3 us -> none  [the longest x1 19.1 us: shards(): col_inner = lax.psum(jnp.sum(dispatch * d_disp, axis=0), 'seq')]
    all_to_all x1 -> x2, blocking collectives: 3.72 us -> 30.6 us  [the longest x1 17.2 us: shards(): lax.all_to_all(chunks, ('seq', 'exp'), split_axis=0, concat_axis=0, tiled...]
    pmax x1 -> x0, blocking collectives: 21.6 us -> none  [shards(): col_top = lax.pmax(jnp.max(logits, axis=0), 'seq')]
    psum x1 -> x0, waiting for transfers between devices: 15 us -> none  [shards(): logits = lax.psum(logit_part, 'exp')]
    dot_general x7 -> x0, matrix products: 5.94 us -> none  [the longest x3 2.62 us: contract_last(): lax.dot_general(left, right, (((1,), (1,)), ((), ())), preferred_element_...]
    pallas_call x0 -> x5, Pallas kernels: none -> 3.21 us  [the longest x1 1.37 us: shards(): call(functools.partial(tokens_kernel, groups=groups), sds((patches, half)...]
  transfers between devices with their start and end apart: 2 -> 2, of which waited for: 2 -> 1; matrix products, arithmetic and copies ran while one was open for 1% -> 0% of each run, Pallas kernels for 0% -> 3%
where the time goes in v1:
time: 40.1 us; the launch traced here: 39.6 us
  blocking collectives  30.6 us (76%)
  Pallas kernels  3.21 us (8%)
  local copies, waits for them, and re-layouts  3.19 us (8%)
  waiting for transfers between devices  1.29 us (3%)
  between operations  0.68 us (2%)
  other arithmetic  0.62 us (2%)
    all_to_all x1, blocking collectives, shards(): lax.all_to_all(chunks, ('seq', 'exp'), split_axis=0, concat_axis=0, tiled...  17.2 us
    all_to_all x1, blocking collectives, shards(): got = lax.all_to_all(send, 'seq', split_axis=0, concat_axis=0, tiled=True)  13.4 us
    unnamed x10, local copies, waits for them, and re-layouts  3.19 us
    pallas_call x1, Pallas kernels, shards(): call(functools.partial(tokens_kernel, groups=groups), sds((patches, half)...  1.37 us
    ppermute x1, waiting for transfers between devices, shards(): other = lax.ppermute(part, 'exp', [(0, 1), (1, 0)])  1.29 us
    pallas_call x1, Pallas kernels, shards(): call(functools.partial(sums_kernel, groups=groups), (sds((4, half), F32),...  0.87 us
  transfers between devices with their start and end apart: 2, of which 1 were waited for; matrix products, arithmetic and copies ran while one was open for 0% of the time, Pallas kernels for 3%

profile of v1, /device:TPU:0, one launch (start us, length us, event | category | flops | bytes accessed | tf_op | source)
XLA Modules:
  0.0 39.6 jit_solution(5507803977327792775)
XLA Ops:
  0.6 0.0 copy-start
  0.6 0.0 copy-start.2
  0.7 0.7 %copy-done.2 = bf16[4,1024]{1,0:T(4,128)(2,1)S(1)} copy-done((bf16[4,1024]{1,0:T(4,128)(2,1)S(1)}, bf16[4,1024]{1,0:T(4,128)(2,1)}, u32[]{:S(2)}) %copy-start.2) | copy-done | bytes 8216
  1.4 0.0 copy-start.3
  1.4 0.7 %copy-done.3 = bf16[2,2048]{1,0:T(2,128)(2,1)S(1)} copy-done((bf16[2,2048]{1,0:T(2,128)(2,1)S(1)}, bf16[2,2048]{1,0:T(2,128)(2,1)}, u32[]{:S(2)}) %copy-start.3) | copy-done | bytes 8216
  2.1 0.0 copy-start.4
  2.1 0.7 %copy-done.4 = bf16[2,2048]{1,0:T(2,128)(2,1)S(1)} copy-done((bf16[2,2048]{1,0:T(2,128)(2,1)S(1)}, bf16[2,2048]{1,0:T(2,128)(2,1)}, u32[]{:S(2)}) %copy-start.4) | copy-done | bytes 8216
  2.8 17.2 %all_to_all.10.slots_ref = bf16[16,16,512]{2,1,0:T(8,128)(2,1)S(1)} all-to-all(bf16[16,16,512]{2,1,0:T(8,128)(2,1)S(1)} %pack.1), channel_id=1, replica_groups=mesh['group'=2,'seq'=8,'exp'=2] {'seq','exp'}, dimensions={0} | all-to-all | bytes 524288 | tf_op jit(solution)/shard_map/all_to_all | solution.py:202
  20.0 0.0 copy-done
  20.0 0.0 copy-start.1
  20.0 1.0 %copy-done.1 = bf16[256,1024]{1,0:T(8,128)(2,1)S(1)} copy-done((bf16[256,1024]{1,0:T(8,128)(2,1)S(1)}, bf16[256,1024]{1,0:T(8,128)(2,1)}, u32[]{:S(2)}) %copy-start.1) | copy-done | bytes 524312
  21.1 0.5 %partial.1.mine_ref = f32[96,256]{1,0:T(8,128)S(1)} custom-call(bf16[16,16,512]{2,1,0:T(8,128)(2,1)S(1)} %all_to_all.10.slots_ref, bf16[256,1024]{1,0:T(8,128)(2,1)S(1)} %copy-done, bf16[256,1024]{1,0:T(8,128)(2,1)S(1)} %copy-done.1), custom_call_target="tpu_custom_call" | custom-call | tf_op jit(solution)/shard_map/partial/pallas_call | solution.py:203
  21.6 0.1 collective-permute-start
  21.6 1.3 %collective-permute-done.other_ref = f32[96,256]{1,0:T(8,128)S(1)} collective-permute-done((f32[96,256]{1,0:T(8,128)S(1)}, f32[96,256]{1,0:T(8,128)S(1)}, u32[]{:S(2)}, u32[]{:S(2)}) %collective-permute-start) | collective-permute-done | bytes 98336 | tf_op jit(solution)/shard_map/ppermute | solution.py:204
  22.9 0.5 %local.1 = (bf16[8,16,1152]{2,1,0:T(8,128)(2,1)S(1)}, f32[32,256]{1,0:T(8,128)S(1)}, f32[32,256]{1,0:T(8,128)S(1)}, f32[32,256]{1,0:T(8,128)S(1)}) custom-call(f32[96,256]{1,0:T(8,128)S(1)} %partial.1.mine_ref, f32[96,256]{1,0:T(8,128)S(1)} %collective-permute-done.other_ref, bf16[256,1024]{1,0:T(8,128)(2,1)S(1)} %copy-done, bf16[256,1024]{1,0:T(8,128)(2,1)S(1)} %copy-done.1), custom_call_target="tpu_custom_call" | custom-call | tf_op jit(solution)/shard_map/local/pallas_call | solution.py:206
  23.4 13.4 %all_to_all.11.got_ref = bf16[8,16,1152]{2,1,0:T(8,128)(2,1)S(1)} all-to-all(bf16[8,16,1152]{2,1,0:T(8,128)(2,1)S(1)} %get-tuple-element.10), channel_id=1, replica_groups=mesh['group'=2,'seq'=8,'exp'=2] {'seq'}, dimensions={0} | all-to-all | bytes 589824 | tf_op jit(solution)/shard_map/all_to_all | solution.py:213
  36.8 0.9 %sums.1 = (f32[4,1024]{1,0:T(4,128)}, f32[2,1024]{1,0:T(2,128)S(1)}, f32[2,1024]{1,0:T(2,128)S(1)}) custom-call(bf16[8,16,1152]{2,1,0:T(8,128)(2,1)S(1)} %all_to_all.11.got_ref), custom_call_target="tpu_custom_call" | custom-call | tf_op jit(solution)/shard_map/sums/pallas_call | solution.py:215
  37.6 0.0 collective-permute-start.1
  37.6 1.4 %token_grads.1 = bf16[256,1024]{1,0:T(8,128)(2,1)} custom-call(bf16[8,16,1152]{2,1,0:T(8,128)(2,1)S(1)} %all_to_all.11.got_ref, bf16[16,16,512]{2,1,0:T(8,128)(2,1)S(1)} %all_to_all.10.slots_ref, f32[32,256]{1,0:T(8,128)S(1)} %get-tuple-element.11.col_ref, f32[32,256]{1,0:T(8,128)S(1)} %get-tuple-element.12.row_ref, f32[32,256]{1,0:T(8,128)S(1)} %get-tuple-element.13.disp_ref), custom_call_target="tpu_custom_call" | custom-call | tf_op jit(solution)/shard_map/token_grads/pallas_call | solution.py:219
  39.0 0.0 collective-permute-done.1
  39.0 0.6 %maximum_select_fusion = f32[2,2048]{1,0:T(2,128)} fusion(f32[2,1024]{1,0:T(2,128)S(1)} %collective-permute-done.1, f32[2,1024]{1,0:T(2,128)S(1)} %get-tuple-element.15, pred[]{:T(512)S(6)} %eq.3), kind=kLoop, calls=%fused_computation | loop fusion | flops 12288 | bytes 32769 | tf_op jit(solution)/shard_map/jit(_where)/select_n | solution.py:227
  (1 shorter events, 0.0 us)
Async XLA Ops:
  0.6 19.4 %copy-start = (bf16[256,1024]{1,0:T(8,128)(2,1)S(1)}, bf16[256,1024]{1,0:T(8,128)(2,1)}, u32[]{:S(2)}) copy-start(bf16[256,1024]{1,0:T(8,128)(2,1)} %tokens_ref.3) | copy-start | bytes 1572868
  0.6 0.8 %copy-start.2 = (bf16[4,1024]{1,0:T(4,128)(2,1)S(1)}, bf16[4,1024]{1,0:T(4,128)(2,1)}, u32[]{:S(2)}) copy-start(bf16[4,1024]{1,0:T(4,128)(2,1)} %params_ref.1) | copy-start | bytes 24580
  1.4 0.7 %copy-start.3 = (bf16[2,2048]{1,0:T(2,128)(2,1)S(1)}, bf16[2,2048]{1,0:T(2,128)(2,1)}, u32[]{:S(2)}) copy-start(bf16[2,2048]{1,0:T(2,128)(2,1)} %outs_ref.1) | copy-start | bytes 24580
  2.1 0.7 %copy-start.4 = (bf16[2,2048]{1,0:T(2,128)(2,1)S(1)}, bf16[2,2048]{1,0:T(2,128)(2,1)}, u32[]{:S(2)}) copy-start(bf16[2,2048]{1,0:T(2,128)(2,1)} %grads_ref.1) | copy-start | bytes 24580
  20.0 1.0 %copy-start.1 = (bf16[256,1024]{1,0:T(8,128)(2,1)S(1)}, bf16[256,1024]{1,0:T(8,128)(2,1)}, u32[]{:S(2)}) copy-start(bf16[256,1024]{1,0:T(8,128)(2,1)} %upstream_ref.3) | copy-start | bytes 1572868
  21.6 1.4 %collective-permute-start = (f32[96,256]{1,0:T(8,128)S(1)}, f32[96,256]{1,0:T(8,128)S(1)}, u32[]{:S(2)}, u32[]{:S(2)}) collective-permute-start(f32[96,256]{1,0:T(8,128)S(1)} %partial.1.mine_ref), channel_id=1, source_target_pairs={{0,1},{1,0},{2,3},{3,2},{4,5},{5,4},{6,7},{7,6},{8,9},{9,8},{10,11... | collective-permute-start | bytes 294920 | tf_op jit(solution)/shard_map/ppermute | solution.py:204
  37.6 1.4 %collective-permute-start.1 = (f32[2,1024]{1,0:T(2,128)S(1)}, f32[2,1024]{1,0:T(2,128)S(1)}, u32[]{:S(2)}, u32[]{:S(2)}) collective-permute-start(f32[2,1024]{1,0:T(2,128)S(1)} %get-tuple-element.16), channel_id=1, source_target_pairs={{0,1},{1,0},{2,3},{3,2},{4,5},{5,4},{6,7},{7,6},{8,9},{9,8},{10,11... | collective-permute-start | bytes 24584 | tf_op jit(solution)/shard_map/ppermute | solution.py:218

commit v2 on v1

v2 whole, which is shorter than its diff:
```python
import functools

import jax
import jax.numpy as jnp
from jax import lax
from jax.experimental import pallas as pl
from jax.experimental.pallas import tpu as pltpu
from jax.sharding import PartitionSpec as P

F32 = jnp.float32
BF16 = jnp.bfloat16


def dot_nt(left, right):
    return lax.dot_general(left, right, (((1,), (1,)), ((), ())), preferred_element_type=F32)


def dot_tn(left, right):
    return lax.dot_general(left, right, (((0,), (0,)), ((), ())), preferred_element_type=F32)


def call(kernel, outs, name, seq, scratch=(), **specs):
    return pl.pallas_call(
        kernel,
        out_shape=outs,
        scratch_shapes=list(scratch),
        compiler_params=pltpu.CompilerParams(vmem_limit_bytes=(16 if seq <= 16 else 48) << 20),
        name=name,
        **specs,
    )


def split16(value):
    high = value.astype(BF16).astype(F32)
    return high, (value - high).astype(BF16).astype(F32)


def fetch_kernel(
    params_ref, outs_ref, grads_ref, upstream_ref, mine_ref, give_ref, held_ref, params, outs, grads, sems
):
    side = lax.axis_index("exp")
    half = params_ref.shape[1]
    sources, targets = (params_ref, outs_ref, grads_ref, upstream_ref), (params, outs, grads, held_ref)
    copies = [pltpu.make_async_copy(*pair, sems.at[i]) for i, pair in enumerate(zip(sources, targets))]
    for copy in copies:
        copy.start()
    for copy in copies[:3]:
        copy.wait()
    both = jnp.concatenate([outs[...].astype(F32), grads[...].astype(F32)], axis=0)
    first, second = both[:, :half], both[:, half:]
    mine_ref[0:4, :] = params[...].astype(F32)
    mine_ref[4:8, :] = jnp.where(side == 0, first, second)
    give_ref[...] = jnp.where(side == 0, second, first).astype(BF16)
    copies[3].wait()


def pack_kernel(mine_ref, taken_ref, chunks_ref):
    side = lax.axis_index("exp")
    half = mine_ref.shape[1]
    mine = mine_ref[...]
    own, taken = mine[4:8], taken_ref[...].astype(F32)
    first, second = jnp.where(side == 0, own, taken), jnp.where(side == 0, taken, own)
    outs = jnp.concatenate([first[0:2], second[0:2]], axis=0)
    left = jnp.concatenate([mine[0:4], first[2:4], second[2:4]], axis=0).astype(BF16)
    right = jnp.concatenate([outs[:, : half // 2], outs[:, half // 2 :]], axis=0).astype(BF16)
    for dest in range(chunks_ref.shape[0]):
        chunks_ref[dest, :, :half] = left
        chunks_ref[dest, :, half:] = right


def partial_kernel(slots_ref, tokens_ref, upstream_ref, part_ref):
    seq, _, width = slots_ref.shape
    half = tokens_ref.shape[1]
    quarter = half // 2
    n_slots = 4 * seq
    by_tokens = dot_nt(slots_ref[:, :, :half].reshape(8 * seq, half), tokens_ref[...])
    outs = slots_ref[:, :, half:].reshape(8 * seq, quarter)
    first = dot_nt(outs, upstream_ref[:, :quarter])
    second = dot_nt(outs, upstream_ref[:, quarter:])
    for chip in range(seq):
        at = 4 * chip
        base = 8 * chip
        part_ref[at : at + 4, :] = by_tokens[base : base + 4]
        part_ref[n_slots + at : n_slots + at + 4, :] = first[base : base + 4] + second[base + 4 : base + 8]
        part_ref[2 * n_slots + at : 2 * n_slots + at + 4, :] = by_tokens[base + 4 : base + 8]


def local_kernel(
    mine_ref, other_ref, tokens_ref, upstream_ref, send_ref, col_ref, row_ref, disp_ref, one_ref, two_ref, three_ref
):
    n_slots = col_ref.shape[0]
    seq, _, width = send_ref.shape
    half = tokens_ref.shape[1]
    extra = width - 2 * half
    groups = n_slots // 8 + 1
    both = mine_ref[...] + other_ref[...]
    logits, d_comb, d_disp = both[:n_slots], both[n_slots : 2 * n_slots], both[2 * n_slots :]
    row_exp = jnp.exp(logits - jnp.max(logits, axis=0, keepdims=True))
    combine = row_exp / jnp.sum(row_exp, axis=0, keepdims=True)
    row_part = combine * (d_comb - jnp.sum(combine * d_comb, axis=0, keepdims=True))
    top_high, top_low = split16(jnp.max(logits, axis=1, keepdims=True))
    col_exp = jnp.exp(logits - (top_high + top_low))
    sum_high, sum_low = split16(jnp.sum(col_exp, axis=1, keepdims=True))
    inner_high, inner_low = split16(jnp.sum(col_exp * d_disp, axis=1, keepdims=True))
    centre = (inner_high + inner_low) / (sum_high + sum_low)
    col_part = col_exp * (d_disp - centre)
    col_ref[...] = col_exp
    row_ref[...] = row_part
    disp_ref[...] = d_disp

    zero = jnp.zeros((4, col_ref.shape[1]), F32)
    for chip in range(seq):
        span = slice(4 * chip, 4 * chip + 4)
        upper, lower = slice(8 * chip, 8 * chip + 4), slice(8 * chip + 4, 8 * chip + 8)
        one_ref[upper, :] = combine[span]
        one_ref[lower, :] = zero
        two_ref[upper, :] = zero
        two_ref[lower, :] = col_part[span]
        three_ref[upper, :] = row_part[span]
        three_ref[lower, :] = col_exp[span]
    left = jnp.dot(one_ref[...].astype(BF16), upstream_ref[...], preferred_element_type=F32)
    left = left + jnp.dot(two_ref[...].astype(BF16), tokens_ref[...], preferred_element_type=F32)
    right = jnp.dot(three_ref[...].astype(BF16), tokens_ref[...], preferred_element_type=F32)
    send_ref[:, :, :half] = left.astype(BF16).reshape(seq, 8, half)
    send_ref[:, :, half : 2 * half] = right.astype(BF16).reshape(seq, 8, half)

    lane = lax.broadcasted_iota(jnp.int32, (n_slots, extra), 1)
    stats = jnp.zeros((n_slots, extra), F32)
    for j, stat in enumerate((top_high, top_low, sum_high, sum_low, inner_high, inner_low)):
        stats = jnp.where(lane == j * groups, stat, stats)
    every = jnp.zeros((8, extra), F32)
    for group in range(groups - 1):
        every = every + pltpu.roll(stats[8 * group : 8 * group + 8], group + 1, 1)
    for chip in range(seq):
        own = stats[4 * chip : 4 * chip + 4]
        send_ref[chip, :, 2 * half :] = (every + jnp.concatenate([own, own], axis=0)).astype(BF16)


def outs_kernel(got_ref, keep_ref, give_ref):
    side = lax.axis_index("exp")
    half = keep_ref.shape[1]
    acc = got_ref[0, :, :half].astype(F32)
    for chip in range(1, got_ref.shape[0]):
        acc = acc + got_ref[chip, :, :half].astype(F32)
    keep_ref[...] = jnp.where(side == 0, acc[0:2], acc[2:4])
    give_ref[...] = jnp.where(side == 0, acc[2:4], acc[0:2])


def column_stats(stats, groups):
    extra = stats.shape[1]
    pair = stats + pltpu.roll(stats, extra - groups, 1)
    return pair, pltpu.roll(pair, extra - 2 * groups, 1), pltpu.roll(pair, extra - 4 * groups, 1)


def sums_kernel(got_ref, col_ref, row_ref, disp_ref, params_ref, left_ref, rows_ref):
    me = lax.axis_index("seq")
    half = params_ref.shape[1]
    seq = got_ref.shape[0]
    n_slots = col_ref.shape[0]
    groups = n_slots // 8 + 1
    blocks = [column_stats(got_ref[chip, :, 2 * half :].astype(F32), groups) for chip in range(seq)]
    high = functools.reduce(jnp.maximum, [top for top, _, _ in blocks])
    scales = [jnp.exp(top - high) for top, _, _ in blocks]
    total = sum(scale * value for scale, (_, value, _) in zip(scales, blocks))
    centre = sum(scale * value for scale, (_, _, value) in zip(scales, blocks)) / total
    upper = lax.broadcasted_iota(jnp.int32, centre.shape, 0) < 4
    acc = jnp.zeros((8, half), F32)
    for chip, (scale, (_, own_total, own_inner)) in enumerate(zip(scales, blocks)):
        weight = scale / total
        by_left = jnp.where(upper, 0.0, weight)
        by_right = jnp.where(upper, 1.0, weight * (own_inner / own_total - centre))
        acc = acc + by_left[:, 0:1] * got_ref[chip, :, :half].astype(F32)
        acc = acc + by_right[:, 0:1] * got_ref[chip, :, half : 2 * half].astype(F32)
    params_ref[...] = acc[0:4] + acc[4:8]

    top, _, _ = column_stats(got_ref[pl.ds(me, 1), :, 2 * half :][0].astype(F32), groups)
    weight = jnp.exp(top - high) / total
    for group in range(groups - 1):
        span = slice(8 * group, 8 * group + 8)
        dispatch = col_ref[span] * weight[:, group + 1 : group + 2]
        d_logit = row_ref[span] + dispatch * (disp_ref[span] - centre[:, group + 1 : group + 2])
        for j in range(2):
            at = 16 * group + 8 * j
            rows_ref[at : at + 4, :] = d_logit[4 * j : 4 * j + 4]
            rows_ref[at + 4 : at + 8, :] = dispatch[4 * j : 4 * j + 4]
    left_ref[...] = rows_ref[...].astype(BF16)


def tokens_kernel(left_ref, slots_ref, keep_ref, taken_ref, out_ref, sums_ref):
    side = lax.axis_index("exp")
    half = out_ref.shape[1]
    right = slots_ref[:, :, :half].reshape(left_ref.shape[0], half)
    out_ref[...] = dot_tn(left_ref[...], right).astype(out_ref.dtype)
    keep, taken = keep_ref[...], taken_ref[...]
    sums_ref[:, :half] = jnp.where(side == 0, keep, taken)
    sums_ref[:, half:] = jnp.where(side == 0, taken, keep)


def shards(seq, tokens, upstream, slot_params, slot_outputs, slot_input_grads):
    patches, half = tokens.shape
    n_slots = slot_params.shape[0] * seq
    extra = -(-6 * (n_slots // 8 + 1) // 128) * 128
    sds = jax.ShapeDtypeStruct
    cores = [(0, 1), (1, 0)]

    mine, give, upstream = call(
        fetch_kernel,
        (sds((8, half), F32), sds((4, half), BF16), pltpu.VMEM(upstream.shape, BF16)),
        "fetch",
        seq,
        [
            pltpu.VMEM(slot_params.shape, BF16),
            pltpu.VMEM(slot_outputs.shape, BF16),
            pltpu.VMEM(slot_input_grads.shape, BF16),
            pltpu.SemaphoreType.DMA((4,)),
        ],
        in_specs=[pl.BlockSpec(memory_space=pl.ANY)] * 4,
    )(*(pltpu.with_memory_space_constraint(x, pltpu.HBM) for x in (slot_params, slot_outputs, slot_input_grads, upstream)))
    taken = lax.ppermute(give, "exp", cores)
    chunks = call(pack_kernel, sds((seq, 8, half + half // 2), BF16), "pack", seq)(mine, taken)
    slots = lax.all_to_all(chunks, "seq", split_axis=0, concat_axis=0, tiled=True)
    part = call(partial_kernel, sds((3 * n_slots, patches), F32), "partial", seq)(slots, tokens, upstream)
    other = lax.ppermute(part, "exp", cores)
    by_slot = sds((n_slots, patches), F32)
    send, col, row, disp = call(
        local_kernel,
        (sds((seq, 8, 2 * half + extra), BF16), by_slot, by_slot, by_slot),
        "local",
        seq,
        [pltpu.VMEM((8 * seq, patches), F32)] * 3,
    )(part, other, tokens, upstream)
    got = lax.all_to_all(send, "seq", split_axis=0, concat_axis=0, tiled=True)
    pair = sds((2, half), F32)
    keep, give = call(outs_kernel, (pair, pair), "outs", seq)(got)
    taken = lax.ppermute(give, "exp", cores)
    param_grads, left = call(
        sums_kernel,
        (sds((4, half), F32), sds((8 * seq, patches), BF16)),
        "sums",
        seq,
        [pltpu.VMEM((8 * seq, patches), F32)],
    )(got, col, row, disp)
    token_grads, slot_output_grads = call(
        tokens_kernel, (sds((patches, half), BF16), sds((2, 2 * half), F32)), "token_grads", seq
    )(left, slots, keep, taken)
    return token_grads, param_grads, slot_output_grads


def solution(mesh):
    in_specs = (
        P(("group", "seq"), "exp"),
        P(("group", "seq"), "exp"),
        P(("group", "seq"), "exp"),
        P(("group", "seq", "exp"), None),
        P(("group", "seq", "exp"), None),
    )
    out_specs = (
        P(("group", "seq"), "exp"),
        P(("group", "seq"), "exp"),
        P(("group", "seq", "exp"), None),
    )
    return jax.shard_map(
        functools.partial(shards, mesh.shape["seq"]),
        mesh=mesh,
        in_specs=in_specs,
        out_specs=out_specs,
        check_vma=False,
    )
```

time: 40.1 us -> 36.7 us (0.915)
  local copies, waits for them, and re-layouts: 3.19 us -> 0.01 us
  blocking collectives: 30.6 us -> 28.5 us
  waiting for transfers between devices: 1.29 us -> 2.37 us
  Pallas kernels: 3.21 us -> 4.24 us
  other arithmetic: 0.62 us -> 0 us
  starting transfers between devices: 0.07 us -> 0.66 us
    unnamed x10 -> x2, local copies, waits for them, and re-layouts: 3.19 us -> 0.01 us
    all_to_all x1, blocking collectives: 17.2 us -> 15.2 us  [shards(): lax.all_to_all(chunks, 'seq', split_axis=0, concat_axis=0, tiled=True)]
    ppermute x2 -> x3, waiting for transfers between devices: 1.29 us -> 2.37 us  [the longest x1 1.29 us: shards(): other = lax.ppermute(part, 'exp', cores)]
    pallas_call x4 -> x6, Pallas kernels: 2.73 us -> 3.8 us  [the longest x1 1.18 us: shards(): call(fetch_kernel, (sds((8, half), F32), sds((4, half), BF16), pltpu.VMEM...]
    select_n x1 -> x0, other arithmetic: 0.62 us -> none  [shards(): jnp.where(side == 0, jnp.concatenate([keep, taken], axis=1), jnp.concaten...]
    ppermute x2 -> x3, starting transfers between devices: 0.07 us -> 0.66 us  [the longest x2 0.59 us: shards(): taken = lax.ppermute(give, 'exp', cores)]
  transfers between devices with their start and end apart: 2 -> 3, of which waited for: 1 -> 3; matrix products, arithmetic and copies ran while one was open for 0% -> 0% of each run, Pallas kernels for 3% -> 2%
where the time goes in v2:
time: 36.7 us; the launch traced here: 36.5 us
  blocking collectives  28.5 us (78%)
  Pallas kernels  4.24 us (12%)
  waiting for transfers between devices  2.37 us (6%)
  between operations  0.68 us (2%)
  starting transfers between devices  0.66 us (2%)
    all_to_all x1, blocking collectives, shards(): lax.all_to_all(chunks, 'seq', split_axis=0, concat_axis=0, tiled=True)  15.2 us
    all_to_all x1, blocking collectives, shards(): got = lax.all_to_all(send, 'seq', split_axis=0, concat_axis=0, tiled=True)  13.3 us
    ppermute x1, waiting for transfers between devices, shards(): other = lax.ppermute(part, 'exp', cores)  1.29 us
    pallas_call x1, Pallas kernels, shards(): call(fetch_kernel, (sds((8, half), F32), sds((4, half), BF16), pltpu.VMEM...  1.18 us
    pallas_call x1, Pallas kernels, shards(): call(tokens_kernel, (sds((patches, half), BF16), sds((2, 2 * half), F32))...  1.11 us
    ppermute x2, waiting for transfers between devices, shards(): taken = lax.ppermute(give, 'exp', cores)  1.08 us
    pallas_call x1, Pallas kernels, shards(): call(sums_kernel, (sds((4, half), F32), sds((8 * seq, patches), BF16)), '...  0.91 us
  transfers between devices with their start and end apart: 3, of which 3 were waited for; matrix products, arithmetic and copies ran while one was open for 0% of the time, Pallas kernels for 2%

profile of v2, /device:TPU:0, one launch (start us, length us, event | category | flops | bytes accessed | tf_op | source)
XLA Modules:
  0.0 36.5 jit_solution(17850483072178833478)
XLA Ops:
  0.6 0.0 copy-start
  0.6 1.2 %fetch.1 = (f32[8,1024]{1,0:T(8,128)S(1)}, bf16[4,1024]{1,0:T(4,128)(2,1)S(1)}, bf16[256,1024]{1,0:T(8,128)(2,1)S(1)}) custom-call(bf16[4,1024]{1,0:T(4,128)(2,1)} %params_ref.1, bf16[2,2048]{1,0:T(2,128)(2,1)} %outs_ref.1, bf16[2,2048]{1,0:T(2,128)(2,1)} %grads_ref.1, bf16[256,1024]{1,0:T(8,128)(2,1)} %upstream_ref.1), custom_call_target="tpu_custom_call" | custom-call | tf_op jit(solution)/shard_map/fetch/pallas_call | solution.py:206
  1.8 0.5 %collective-permute-start = (bf16[4,1024]{1,0:T(4,128)(2,1)S(1)}, bf16[4,1024]{1,0:T(4,128)(2,1)S(1)}, u32[]{:S(2)}, u32[]{:S(2)}) collective-permute-start(bf16[4,1024]{1,0:T(4,128)(2,1)S(1)} %get-tuple-element.17), channel_id=1, source_target_pairs={{0,1},{1,0},{2,3},{3,2},{4,5},{5,4},{6,7},{7,6},{8,9},{9,8},{10,11... | collective-permute-start | bytes 24584 | tf_op jit(solution)/shard_map/ppermute | solution.py:219
  2.4 0.8 %collective-permute-done.taken_ref = bf16[4,1024]{1,0:T(4,128)(2,1)S(1)} collective-permute-done((bf16[4,1024]{1,0:T(4,128)(2,1)S(1)}, bf16[4,1024]{1,0:T(4,128)(2,1)S(1)}, u32[]{:S(2)}, u32[]{:S(2)}) %collective-permute-start) | collective-permute-done | bytes 8224 | tf_op jit(solution)/shard_map/ppermute | solution.py:219
  3.2 15.2 %all_to_all.10.slots_ref = bf16[8,8,1536]{2,1,0:T(8,128)(2,1)S(1)} all-to-all(bf16[8,8,1536]{2,1,0:T(8,128)(2,1)S(1)} %pack.1), channel_id=1, replica_groups=mesh['group'=2,'seq'=8,'exp'=2] {'seq'}, dimensions={0} | all-to-all | bytes 393216 | tf_op jit(solution)/shard_map/all_to_all | solution.py:221
  18.4 0.0 copy-done
  18.4 0.4 %partial.1.mine_ref = f32[96,256]{1,0:T(8,128)S(1)} custom-call(bf16[8,8,1536]{2,1,0:T(8,128)(2,1)S(1)} %all_to_all.10.slots_ref, bf16[256,1024]{1,0:T(8,128)(2,1)S(1)} %copy-done, bf16[256,1024]{1,0:T(8,128)(2,1)S(1)} %get-tuple-element.18.upstream_ref), custom_call_target="tpu_custom_call" | custom-call | tf_op jit(solution)/shard_map/partial/pallas_call | solution.py:222
  18.9 0.1 collective-permute-start.1
  19.0 1.3 %collective-permute-done.1.other_ref = f32[96,256]{1,0:T(8,128)S(1)} collective-permute-done((f32[96,256]{1,0:T(8,128)S(1)}, f32[96,256]{1,0:T(8,128)S(1)}, u32[]{:S(2)}, u32[]{:S(2)}) %collective-permute-start.1) | collective-permute-done | bytes 98336 | tf_op jit(solution)/shard_map/ppermute | solution.py:223
  20.2 0.5 %local.1 = (bf16[8,8,2176]{2,1,0:T(8,128)(2,1)S(1)}, f32[32,256]{1,0:T(8,128)S(1)}, f32[32,256]{1,0:T(8,128)S(1)}, f32[32,256]{1,0:T(8,128)S(1)}) custom-call(f32[96,256]{1,0:T(8,128)S(1)} %partial.1.mine_ref, f32[96,256]{1,0:T(8,128)S(1)} %collective-permute-done.1.other_ref, bf16[256,1024]{1,0:T(8,128)(2,1)S(1)} %copy-done, ...), custom_call_target="tpu_custom_call" | custom-call | tf_op jit(solution)/shard_map/local/pallas_call | solution.py:225
  20.8 13.3 %all_to_all.11.got_ref = bf16[8,8,2176]{2,1,0:T(8,128)(2,1)S(1)} all-to-all(bf16[8,8,2176]{2,1,0:T(8,128)(2,1)S(1)} %get-tuple-element.19), channel_id=1, replica_groups=mesh['group'=2,'seq'=8,'exp'=2] {'seq'}, dimensions={0} | all-to-all | bytes 557056 | tf_op jit(solution)/shard_map/all_to_all | solution.py:232
  34.1 0.1 collective-permute-start.2
  34.2 0.9 %sums.1 = (f32[4,1024]{1,0:T(4,128)}, bf16[64,256]{1,0:T(8,128)(2,1)S(1)}) custom-call(bf16[8,8,2176]{2,1,0:T(8,128)(2,1)S(1)} %all_to_all.11.got_ref, f32[32,256]{1,0:T(8,128)S(1)} %get-tuple-element.20.col_ref, f32[32,256]{1,0:T(8,128)S(1)} %get-tuple-element.21.row_ref, f32[32,256]{1,0:T(8,128)S(1)} %get-tuple-element.22.disp_ref), custom_call_target="tpu_custom_call" | custom-call | tf_op jit(solution)/shard_map/sums/pallas_call | solution.py:236
  35.1 0.2 collective-permute-done.2.taken_ref
  35.4 1.1 %token_grads.1 = (bf16[256,1024]{1,0:T(8,128)(2,1)}, f32[2,2048]{1,0:T(2,128)}) custom-call(bf16[64,256]{1,0:T(8,128)(2,1)S(1)} %get-tuple-element.23.left_ref, bf16[8,8,1536]{2,1,0:T(8,128)(2,1)S(1)} %all_to_all.10.slots_ref, f32[2,1024]{1,0:T(2,128)S(1)} %get-tuple-element.24.keep_ref, f32[2,1024]{1,0:T(2,128)S(1)} %collective-permute-done.2.taken_ref), custom_call_target="tpu_custom_call" | custom-call | tf_op jit(solution)/shard_map/token_grads/pallas_call | solution.py:243
  (2 shorter events, 0.0 us)
Async XLA Ops:
  0.6 17.8 %copy-start = (bf16[256,1024]{1,0:T(8,128)(2,1)S(1)}, bf16[256,1024]{1,0:T(8,128)(2,1)}, u32[]{:S(2)}) copy-start(bf16[256,1024]{1,0:T(8,128)(2,1)} %tokens_ref.3) | copy-start | bytes 1572868
  1.8 1.3 %collective-permute-start = (bf16[4,1024]{1,0:T(4,128)(2,1)S(1)}, bf16[4,1024]{1,0:T(4,128)(2,1)S(1)}, u32[]{:S(2)}, u32[]{:S(2)}) collective-permute-start(bf16[4,1024]{1,0:T(4,128)(2,1)S(1)} %get-tuple-element.17), channel_id=1, source_target_pairs={{0,1},{1,0},{2,3},{3,2},{4,5},{5,4},{6,7},{7,6},{8,9},{9,8},{10,11... | collective-permute-start | bytes 24584 | tf_op jit(solution)/shard_map/ppermute | solution.py:219
  18.9 1.4 %collective-permute-start.1 = (f32[96,256]{1,0:T(8,128)S(1)}, f32[96,256]{1,0:T(8,128)S(1)}, u32[]{:S(2)}, u32[]{:S(2)}) collective-permute-start(f32[96,256]{1,0:T(8,128)S(1)} %partial.1.mine_ref), channel_id=1, source_target_pairs={{0,1},{1,0},{2,3},{3,2},{4,5},{5,4},{6,7},{7,6},{8,9},{9,8},{10,11... | collective-permute-start | bytes 294920 | tf_op jit(solution)/shard_map/ppermute | solution.py:223
  34.1 1.2 %collective-permute-start.2 = (f32[2,1024]{1,0:T(2,128)S(1)}, f32[2,1024]{1,0:T(2,128)S(1)}, u32[]{:S(2)}, u32[]{:S(2)}) collective-permute-start(f32[2,1024]{1,0:T(2,128)S(1)} %get-tuple-element.25), channel_id=1, source_target_pairs={{0,1},{1,0},{2,3},{3,2},{4,5},{5,4},{6,7},{7,6},{8,9},{9,8},{10,11... | collective-permute-start | bytes 24584 | tf_op jit(solution)/shard_map/ppermute | solution.py:235

commit v3 on v2

v3 whole, which is shorter than its diff:
```python
import functools

import jax
import jax.numpy as jnp
from jax import lax
from jax.experimental import pallas as pl
from jax.experimental.pallas import tpu as pltpu
from jax.sharding import PartitionSpec as P

F32 = jnp.float32
BF16 = jnp.bfloat16


def dot_nt(left, right):
    return lax.dot_general(left, right, (((1,), (1,)), ((), ())), preferred_element_type=F32)


def dot_tn(left, right):
    return lax.dot_general(left, right, (((0,), (0,)), ((), ())), preferred_element_type=F32)


def call(kernel, outs, name, seq, scratch=(), **specs):
    return pl.pallas_call(
        kernel,
        out_shape=outs,
        scratch_shapes=list(scratch),
        compiler_params=pltpu.CompilerParams(vmem_limit_bytes=(16 if seq <= 16 else 48) << 20),
        name=name,
        **specs,
    )


def split16(value):
    high = value.astype(BF16).astype(F32)
    return high, (value - high).astype(BF16).astype(F32)


def fetch_kernel(params_ref, outs_ref, grads_ref, mine_ref, params, outs, grads, sems):
    side = lax.axis_index("exp")
    half = params_ref.shape[1]
    quarter = half // 2
    sources, targets = (params_ref, outs_ref, grads_ref), (params, outs, grads)
    copies = [pltpu.make_async_copy(*pair, sems.at[i]) for i, pair in enumerate(zip(sources, targets))]
    for copy in copies:
        copy.start()
    for copy in copies:
        copy.wait()
    slot_outputs, slot_grads = outs[...].astype(F32), grads[...].astype(F32)
    own = jnp.where(side == 0, slot_outputs[:, :half], slot_outputs[:, half:])
    far = jnp.where(side == 0, slot_outputs[:, half:], slot_outputs[:, :half])
    mine_ref[0:4, :half] = params[...].astype(F32)
    for core in range(2):
        mine_ref[4 + 2 * core : 6 + 2 * core, :half] = jnp.where(side == 0, slot_grads[:, :half], slot_grads[:, half:])
    for i, block in enumerate((own[:, :quarter], own[:, quarter:], far[:, :quarter], far[:, quarter:])):
        mine_ref[2 * i : 2 * i + 2, half:] = block


def pack_kernel(mine_ref, grads_ref, chunks_ref):
    side = lax.axis_index("exp")
    width = mine_ref.shape[1]
    half = 2 * width // 3
    grads = grads_ref[...].astype(F32)
    taken = jnp.where(side == 0, grads[:, :half], grads[:, half:])
    mine = mine_ref[...]
    first, second = jnp.where(side == 0, mine[4:6, :half], taken), jnp.where(side == 0, taken, mine[6:8, :half])
    left = jnp.concatenate([mine[0:4, :half], first, second], axis=0).astype(BF16)
    right = mine[:, half:].astype(BF16)
    for dest in range(chunks_ref.shape[0]):
        chunks_ref[dest, :, :half] = left
        chunks_ref[dest, :, half:] = right


def partial_kernel(slots_ref, tokens_ref, upstream_ref, far_ref, part_ref):
    side = lax.axis_index("exp")
    seq, _, width = slots_ref.shape
    half = tokens_ref.shape[1]
    quarter = half // 2
    n_slots = 4 * seq
    by_tokens = dot_nt(slots_ref[:, :, :half].reshape(8 * seq, half), tokens_ref[...])
    outs = slots_ref[:, :, half:].reshape(8 * seq, quarter)
    pieces = (upstream_ref[:, :quarter], upstream_ref[:, quarter:], far_ref[:, :quarter], far_ref[:, quarter:])
    by_quarter = [dot_nt(outs, piece) for piece in pieces]
    for chip in range(seq):
        at = 4 * chip
        base = 8 * chip
        d_comb = sum(block[base + 2 * i : base + 2 * i + 2] for i, block in enumerate(by_quarter))
        part_ref[at : at + 4, :] = by_tokens[base : base + 4]
        part_ref[n_slots + at : n_slots + at + 2, :] = jnp.where(side == 0, d_comb, 0.0)
        part_ref[n_slots + at + 2 : n_slots + at + 4, :] = jnp.where(side == 1, d_comb, 0.0)
        part_ref[2 * n_slots + at : 2 * n_slots + at + 4, :] = by_tokens[base + 4 : base + 8]


def local_kernel(
    mine_ref, other_ref, tokens_ref, upstream_ref, far_ref, send_ref, col_ref, row_ref, disp_ref, *rows
):
    own_ref, cross_ref, two_ref, three_ref = rows
    side = lax.axis_index("exp")
    n_slots = col_ref.shape[0]
    seq, _, width = send_ref.shape
    half = tokens_ref.shape[1]
    extra = width - 2 * half
    groups = n_slots // 8 + 1
    both = mine_ref[...] + other_ref[...]
    logits, d_comb, d_disp = both[:n_slots], both[n_slots : 2 * n_slots], both[2 * n_slots :]
    row_exp = jnp.exp(logits - jnp.max(logits, axis=0, keepdims=True))
    combine = row_exp / jnp.sum(row_exp, axis=0, keepdims=True)
    row_part = combine * (d_comb - jnp.sum(combine * d_comb, axis=0, keepdims=True))
    top_high, top_low = split16(jnp.max(logits, axis=1, keepdims=True))
    col_exp = jnp.exp(logits - (top_high + top_low))
    sum_high, sum_low = split16(jnp.sum(col_exp, axis=1, keepdims=True))
    inner_high, inner_low = split16(jnp.sum(col_exp * d_disp, axis=1, keepdims=True))
    centre = (inner_high + inner_low) / (sum_high + sum_low)
    col_part = col_exp * (d_disp - centre)
    col_ref[...] = col_exp
    row_ref[...] = row_part
    disp_ref[...] = d_disp

    zero = jnp.zeros((4, col_ref.shape[1]), F32)
    ours = lax.broadcasted_iota(jnp.int32, zero.shape, 0) // 2 == side
    for chip in range(seq):
        span = slice(4 * chip, 4 * chip + 4)
        upper, lower = slice(8 * chip, 8 * chip + 4), slice(8 * chip + 4, 8 * chip + 8)
        kept = jnp.where(ours, combine[span], 0.0)
        own_ref[upper, :] = kept
        own_ref[lower, :] = zero
        cross_ref[upper, :] = jnp.concatenate([kept[2:4], kept[0:2]], axis=0)
        cross_ref[lower, :] = zero
        two_ref[upper, :] = zero
        two_ref[lower, :] = col_part[span]
        three_ref[upper, :] = row_part[span]
        three_ref[lower, :] = col_exp[span]
    left = jnp.dot(own_ref[...].astype(BF16), upstream_ref[...], preferred_element_type=F32)
    left = left + jnp.dot(cross_ref[...].astype(BF16), far_ref[...], preferred_element_type=F32)
    left = left + jnp.dot(two_ref[...].astype(BF16), tokens_ref[...], preferred_element_type=F32)
    right = jnp.dot(three_ref[...].astype(BF16), tokens_ref[...], preferred_element_type=F32)
    send_ref[:, :, :half] = left.astype(BF16).reshape(seq, 8, half)
    send_ref[:, :, half : 2 * half] = right.astype(BF16).reshape(seq, 8, half)

    lane = lax.broadcasted_iota(jnp.int32, (n_slots, extra), 1)
    stats = jnp.zeros((n_slots, extra), F32)
    for j, stat in enumerate((top_high, top_low, sum_high, sum_low, inner_high, inner_low)):
        stats = jnp.where(lane == j * groups, stat, stats)
    every = jnp.zeros((8, extra), F32)
    for group in range(groups - 1):
        every = every + pltpu.roll(stats[8 * group : 8 * group + 8], group + 1, 1)
    for chip in range(seq):
        own = stats[4 * chip : 4 * chip + 4]
        send_ref[chip, :, 2 * half :] = (every + jnp.concatenate([own, own], axis=0)).astype(BF16)


def column_stats(stats, groups):
    extra = stats.shape[1]
    pair = stats + pltpu.roll(stats, extra - groups, 1)
    return pair, pltpu.roll(pair, extra - 2 * groups, 1), pltpu.roll(pair, extra - 4 * groups, 1)


def finish_kernel(
    got_ref, slots_ref, col_ref, row_ref, disp_ref, *outs_and_scratch
):
    params_out, tokens_out, sums_out, rows_ref, params_ref, tokens_ref, sums_ref, sems = outs_and_scratch
    me = lax.axis_index("seq")
    half = params_ref.shape[1]
    seq = got_ref.shape[0]
    n_slots = col_ref.shape[0]
    groups = n_slots // 8 + 1
    blocks = [column_stats(got_ref[chip, :, 2 * half :].astype(F32), groups) for chip in range(seq)]
    high = functools.reduce(jnp.maximum, [top for top, _, _ in blocks])
    scales = [jnp.exp(top - high) for top, _, _ in blocks]
    total = sum(scale * value for scale, (_, value, _) in zip(scales, blocks))
    centre = sum(scale * value for scale, (_, _, value) in zip(scales, blocks)) / total

    top, _, _ = column_stats(got_ref[pl.ds(me, 1), :, 2 * half :][0].astype(F32), groups)
    weight = jnp.exp(top - high) / total
    for group in range(groups - 1):
        span = slice(8 * group, 8 * group + 8)
        dispatch = col_ref[span] * weight[:, group + 1 : group + 2]
        d_logit = row_ref[span] + dispatch * (disp_ref[span] - centre[:, group + 1 : group + 2])
        for j in range(2):
            at = 16 * group + 8 * j
            rows_ref[at : at + 4, :] = d_logit[4 * j : 4 * j + 4]
            rows_ref[at + 4 : at + 8, :] = dispatch[4 * j : 4 * j + 4]
    right = slots_ref[:, :, :half].reshape(8 * seq, half)
    left = rows_ref[...].astype(BF16)
    patches = tokens_ref.shape[0] // 2
    copies = []
    for part in range(2):
        span = slice(part * patches, (part + 1) * patches)
        tokens_ref[span, :] = dot_tn(left[:, span], right).astype(BF16)
        copies.append(pltpu.make_async_copy(tokens_ref.at[span], tokens_out.at[span], sems.at[part]))
        copies[-1].start()

    upper = lax.broadcasted_iota(jnp.int32, centre.shape, 0) < 4
    left = right = jnp.zeros((8, half), F32)
    for chip, (scale, (_, own_total, own_inner)) in enumerate(zip(scales, blocks)):
        weight = scale / total
        by_left = jnp.where(upper, 1.0, weight)
        by_right = jnp.where(upper, 1.0, weight * (own_inner / own_total - centre))
        left = left + by_left[:, 0:1] * got_ref[chip, :, :half].astype(F32)
        right = right + by_right[:, 0:1] * got_ref[chip, :, half : 2 * half].astype(F32)
    sums_ref[:, :half] = left[0:2]
    sums_ref[:, half:] = left[2:4]
    params_ref[...] = left[4:8] + right[0:4] + right[4:8]
    for i, (source, target) in enumerate(((params_ref, params_out), (sums_ref, sums_out))):
        copies.append(pltpu.make_async_copy(source, target, sems.at[2 + i]))
        copies[-1].start()
    for copy in copies:
        copy.wait()


def shards(seq, tokens, upstream, slot_params, slot_outputs, slot_input_grads):
    patches, half = tokens.shape
    n_slots = slot_params.shape[0] * seq
    extra = -(-6 * (n_slots // 8 + 1) // 128) * 128
    sds = jax.ShapeDtypeStruct
    cores = [(0, 1), (1, 0)]

    grads_far = lax.ppermute(slot_input_grads, "exp", cores)
    far = lax.ppermute(upstream, "exp", cores)
    mine = call(
        fetch_kernel,
        sds((8, half + half // 2), F32),
        "fetch",
        seq,
        [
            pltpu.VMEM(slot_params.shape, BF16),
            pltpu.VMEM(slot_outputs.shape, BF16),
            pltpu.VMEM(slot_input_grads.shape, BF16),
            pltpu.SemaphoreType.DMA((3,)),
        ],
        in_specs=[pl.BlockSpec(memory_space=pl.ANY)] * 3,
        cost_estimate=pl.CostEstimate(flops=10000000000, bytes_accessed=10000000, transcendentals=0),
    )(*(pltpu.with_memory_space_constraint(x, pltpu.HBM) for x in (slot_params, slot_outputs, slot_input_grads)))
    chunks = call(pack_kernel, sds((seq, 8, half + half // 2), BF16), "pack", seq)(mine, grads_far)
    slots = lax.all_to_all(chunks, "seq", split_axis=0, concat_axis=0, tiled=True)
    part = call(partial_kernel, sds((3 * n_slots, patches), F32), "partial", seq)(slots, tokens, upstream, far)
    other = lax.ppermute(part, "exp", cores)
    by_slot = sds((n_slots, patches), F32)
    send, col, row, disp = call(
        local_kernel,
        (sds((seq, 8, 2 * half + extra), BF16), by_slot, by_slot, by_slot),
        "local",
        seq,
        [pltpu.VMEM((8 * seq, patches), F32)] * 4,
    )(part, other, tokens, upstream, far)
    got = lax.all_to_all(send, "seq", split_axis=0, concat_axis=0, tiled=True)
    param_grads, token_grads, slot_output_grads = call(
        finish_kernel,
        (sds((4, half), F32), sds((patches, half), BF16), sds((2, 2 * half), F32)),
        "finish",
        seq,
        [
            pltpu.VMEM((8 * seq, patches), F32),
            pltpu.VMEM((4, half), F32),
            pltpu.VMEM((patches, half), BF16),
            pltpu.VMEM((2, 2 * half), F32),
            pltpu.SemaphoreType.DMA((4,)),
        ],
        out_specs=[pl.BlockSpec(memory_space=pl.ANY)] * 3,
    )(got, slots, col, row, disp)
    return token_grads, param_grads, slot_output_grads


def solution(mesh):
    in_specs = (
        P(("group", "seq"), "exp"),
        P(("group", "seq"), "exp"),
        P(("group", "seq"), "exp"),
        P(("group", "seq", "exp"), None),
        P(("group", "seq", "exp"), None),
    )
    out_specs = (
        P(("group", "seq"), "exp"),
        P(("group", "seq"), "exp"),
        P(("group", "seq", "exp"), None),
    )
    return jax.shard_map(
        functools.partial(shards, mesh.shape["seq"]),
        mesh=mesh,
        in_specs=in_specs,
        out_specs=out_specs,
        check_vma=False,
    )
```

time: 36.7 us -> 34.9 us (0.951)
  waiting for transfers between devices: 2.37 us -> 1.4 us
  Pallas kernels: 4.24 us -> 3.3 us
    pallas_call x4 -> x2, Pallas kernels: 3.23 us -> 2.16 us  [the longest x1 1.34 us: shards(): call(finish_kernel, (sds((4, half), F32), sds((patches, half), BF16), sds...]
    ppermute x2, waiting for transfers between devices: 1.08 us -> 0.12 us  [the longest x1 0.11 us: shards(): grads_far = lax.ppermute(slot_input_grads, 'exp', cores)]
  transfers between devices with their start and end apart: 3 -> 3, of which waited for: 3 -> 2; matrix products, arithmetic and copies ran while one was open for 0% -> 0% of each run, Pallas kernels for 2% -> 2%
where the time goes in v3:
time: 34.9 us; the launch traced here: 34.6 us
  blocking collectives  28.5 us (82%)
  Pallas kernels  3.3 us (9%)
  waiting for transfers between devices  1.4 us (4%)
  between operations  0.68 us (2%)
  starting transfers between devices  0.67 us (2%)
    all_to_all x1, blocking collectives, shards(): lax.all_to_all(chunks, 'seq', split_axis=0, concat_axis=0, tiled=True)  15.2 us
    all_to_all x1, blocking collectives, shards(): got = lax.all_to_all(send, 'seq', split_axis=0, concat_axis=0, tiled=True)  13.3 us
    pallas_call x1, Pallas kernels, shards(): call(finish_kernel, (sds((4, half), F32), sds((patches, half), BF16), sds...  1.34 us
    ppermute x1, waiting for transfers between devices, shards(): other = lax.ppermute(part, 'exp', cores)  1.29 us
    pallas_call x1, Pallas kernels, shards(): call(fetch_kernel, sds((8, half + half // 2), F32), 'fetch', seq, [pltpu....  0.83 us
  transfers between devices with their start and end apart: 3, of which 2 were waited for; matrix products, arithmetic and copies ran while one was open for 0% of the time, Pallas kernels for 2%

profile of v3, /device:TPU:0, one launch (start us, length us, event | category | flops | bytes accessed | tf_op | source)
XLA Modules:
  0.0 34.6 jit_solution(3903070853437403816)
XLA Ops:
  0.6 0.5 %collective-permute-start = (bf16[2,2048]{1,0:T(2,128)(2,1)}, bf16[2,2048]{1,0:T(2,128)(2,1)S(1)}, u32[]{:S(2)}, u32[]{:S(2)}) collective-permute-start(bf16[2,2048]{1,0:T(2,128)(2,1)} %grads_ref.1), channel_id=1, source_target_pairs={{0,1},{1,0},{2,3},{3,2},{4,5},{5,4},{6,7},{7,6},{8,9},{9,8},{10,11... | collective-permute-start | bytes 24584 | tf_op jit(solution)/shard_map/ppermute | solution.py:217
  1.1 0.1 collective-permute-start.1
  1.2 0.0 copy-start.1
  1.2 0.8 %fetch.1.mine_ref = f32[8,1536]{1,0:T(8,128)S(1)} custom-call(bf16[4,1024]{1,0:T(4,128)(2,1)} %params_ref.1, bf16[2,2048]{1,0:T(2,128)(2,1)} %outs_ref.1, bf16[2,2048]{1,0:T(2,128)(2,1)} %grads_ref.1), custom_call_target="tpu_custom_call" | custom-call | flops 10000000000 | bytes 10000000 | tf_op jit(solution)/shard_map/fetch/pallas_call | solution.py:219
  2.1 0.0 copy-start
  2.1 0.1 collective-permute-done.grads_ref
  2.2 15.2 %all_to_all.10.slots_ref = bf16[8,8,1536]{2,1,0:T(8,128)(2,1)S(1)} all-to-all(bf16[8,8,1536]{2,1,0:T(8,128)(2,1)S(1)} %pack.1), channel_id=1, replica_groups=mesh['group'=2,'seq'=8,'exp'=2] {'seq'}, dimensions={0} | all-to-all | bytes 393216 | tf_op jit(solution)/shard_map/all_to_all | solution.py:234
  17.4 0.0 collective-permute-done.1.far_ref
  17.4 0.0 copy-done.1
  17.4 0.0 copy-done
  17.5 0.6 %partial.1.mine_ref = f32[96,256]{1,0:T(8,128)S(1)} custom-call(bf16[8,8,1536]{2,1,0:T(8,128)(2,1)S(1)} %all_to_all.10.slots_ref, bf16[256,1024]{1,0:T(8,128)(2,1)S(1)} %copy-done, bf16[256,1024]{1,0:T(8,128)(2,1)S(1)} %copy-done.1, bf16[256,1024]{1,0:T(8,128)(2,1)S(1)} %collective-permute-done.1.far_ref), custom_call_target="tpu_custom_call" | custom-call | tf_op jit(solution)/shard_map/partial/pallas_call | solution.py:235
  18.1 0.1 collective-permute-start.2
  18.1 1.3 %collective-permute-done.2.other_ref = f32[96,256]{1,0:T(8,128)S(1)} collective-permute-done((f32[96,256]{1,0:T(8,128)S(1)}, f32[96,256]{1,0:T(8,128)S(1)}, u32[]{:S(2)}, u32[]{:S(2)}) %collective-permute-start.2) | collective-permute-done | bytes 98336 | tf_op jit(solution)/shard_map/ppermute | solution.py:236
  19.4 0.5 %local.1 = (bf16[8,8,2176]{2,1,0:T(8,128)(2,1)S(1)}, f32[32,256]{1,0:T(8,128)S(1)}, f32[32,256]{1,0:T(8,128)S(1)}, f32[32,256]{1,0:T(8,128)S(1)}) custom-call(f32[96,256]{1,0:T(8,128)S(1)} %partial.1.mine_ref, f32[96,256]{1,0:T(8,128)S(1)} %collective-permute-done.2.other_ref, bf16[256,1024]{1,0:T(8,128)(2,1)S(1)} %copy-done, ...), custom_call_target="tpu_custom_call" | custom-call | tf_op jit(solution)/shard_map/local/pallas_call | solution.py:238
  19.9 13.3 %all_to_all.11.got_ref = bf16[8,8,2176]{2,1,0:T(8,128)(2,1)S(1)} all-to-all(bf16[8,8,2176]{2,1,0:T(8,128)(2,1)S(1)} %get-tuple-element.10), channel_id=1, replica_groups=mesh['group'=2,'seq'=8,'exp'=2] {'seq'}, dimensions={0} | all-to-all | bytes 557056 | tf_op jit(solution)/shard_map/all_to_all | solution.py:245
  33.3 1.3 %finish.1 = (f32[4,1024]{1,0:T(4,128)}, bf16[256,1024]{1,0:T(8,128)(2,1)}, f32[2,2048]{1,0:T(2,128)}) custom-call(bf16[8,8,2176]{2,1,0:T(8,128)(2,1)S(1)} %all_to_all.11.got_ref, bf16[8,8,1536]{2,1,0:T(8,128)(2,1)S(1)} %all_to_all.10.slots_ref, f32[32,256]{1,0:T(8,128)S(1)} %get-tuple-element.11.col_ref, f32[32,256]{1,0:T(8,128)S(1)} %get-tuple-element.12.row_ref, ...), custom_call_target="tpu_custom_call" | custom-call | tf_op jit(solution)/shard_map/finish/pallas_call | solution.py:246
  (1 shorter events, 0.0 us)
Async XLA Ops:
  0.6 1.6 %collective-permute-start = (bf16[2,2048]{1,0:T(2,128)(2,1)}, bf16[2,2048]{1,0:T(2,128)(2,1)S(1)}, u32[]{:S(2)}, u32[]{:S(2)}) collective-permute-start(bf16[2,2048]{1,0:T(2,128)(2,1)} %grads_ref.1), channel_id=1, source_target_pairs={{0,1},{1,0},{2,3},{3,2},{4,5},{5,4},{6,7},{7,6},{8,9},{9,8},{10,11... | collective-permute-start | bytes 24584 | tf_op jit(solution)/shard_map/ppermute | solution.py:217
  1.1 16.3 %collective-permute-start.1 = (bf16[256,1024]{1,0:T(8,128)(2,1)}, bf16[256,1024]{1,0:T(8,128)(2,1)S(1)}, u32[]{:S(2)}, u32[]{:S(2)}) collective-permute-start(bf16[256,1024]{1,0:T(8,128)(2,1)} %upstream_ref.3), channel_id=1, source_target_pairs={{0,1},{1,0},{2,3},{3,2},{4,5},{5,4},{6,7},{7,6},{8,9},{9,8},{10,11... | collective-permute-start | bytes 1572872 | tf_op jit(solution)/shard_map/ppermute | solution.py:218
  1.2 16.2 %copy-start.1 = (bf16[256,1024]{1,0:T(8,128)(2,1)S(1)}, bf16[256,1024]{1,0:T(8,128)(2,1)}, u32[]{:S(2)}) copy-start(bf16[256,1024]{1,0:T(8,128)(2,1)} %upstream_ref.3) | copy-start | bytes 1572868
  2.1 15.4 %copy-start = (bf16[256,1024]{1,0:T(8,128)(2,1)S(1)}, bf16[256,1024]{1,0:T(8,128)(2,1)}, u32[]{:S(2)}) copy-start(bf16[256,1024]{1,0:T(8,128)(2,1)} %tokens_ref.3) | copy-start | bytes 1572868
  18.1 1.4 %collective-permute-start.2 = (f32[96,256]{1,0:T(8,128)S(1)}, f32[96,256]{1,0:T(8,128)S(1)}, u32[]{:S(2)}, u32[]{:S(2)}) collective-permute-start(f32[96,256]{1,0:T(8,128)S(1)} %partial.1.mine_ref), channel_id=1, source_target_pairs={{0,1},{1,0},{2,3},{3,2},{4,5},{5,4},{6,7},{7,6},{8,9},{9,8},{10,11... | collective-permute-start | bytes 294920 | tf_op jit(solution)/shard_map/ppermute | solution.py:236

commit v4 on v3

v4 whole, which is shorter than its diff:
```python
import functools

import jax
import jax.numpy as jnp
from jax import lax
from jax.experimental import pallas as pl
from jax.experimental.pallas import tpu as pltpu
from jax.sharding import PartitionSpec as P

F32 = jnp.float32
BF16 = jnp.bfloat16
LONG = pl.CostEstimate(flops=10**10, bytes_accessed=10**7, transcendentals=0)


def dot_nt(left, right):
    return lax.dot_general(left, right, (((1,), (1,)), ((), ())), preferred_element_type=F32)


def dot_tn(left, right):
    return lax.dot_general(left, right, (((0,), (0,)), ((), ())), preferred_element_type=F32)


def call(kernel, outs, name, seq, scratch=(), **specs):
    return pl.pallas_call(
        kernel,
        out_shape=outs,
        scratch_shapes=list(scratch),
        compiler_params=pltpu.CompilerParams(vmem_limit_bytes=(16 if seq <= 16 else 48) << 20),
        name=name,
        **specs,
    )


def split16(value):
    high = value.astype(BF16).astype(F32)
    return high, (value - high).astype(BF16).astype(F32)


def seed_kernel(seed_ref):
    seed_ref[...] = jnp.zeros_like(seed_ref)


def pack_kernel(seed_ref, params_ref, outs_ref, grads_ref, chunks_ref):
    side = lax.axis_index("exp")
    half = params_ref.shape[1]
    quarter = half // 2

    def halves(ref):
        value = ref[...].astype(F32)
        first, second = value[:, :half], value[:, half:]
        return jnp.where(side == 0, first, second), jnp.where(side == 0, second, first)

    own, far = halves(outs_ref)
    pieces = (own[:, :quarter], own[:, quarter:], far[:, :quarter], far[:, quarter:])
    left = jnp.concatenate([params_ref[...].astype(F32), *halves(grads_ref)], axis=0).astype(BF16)
    right = jnp.concatenate(pieces, axis=0).astype(BF16)
    for dest in range(chunks_ref.shape[0]):
        chunks_ref[dest, :, :half] = left
        chunks_ref[dest, :, half:] = right


def products(slots_ref, tokens_ref, tokens_far_ref, upstream_ref, upstream_far_ref, side):
    seq, _, width = slots_ref.shape
    half = tokens_ref.shape[1]
    quarter = half // 2
    left = slots_ref[:, :, :half].reshape(8 * seq, half)
    right = slots_ref[:, :, half:].reshape(8 * seq, quarter)
    near, far = dot_nt(left, tokens_ref[...]), dot_nt(left, tokens_far_ref[...])
    by_quarter = [
        dot_nt(right, ref[:, i * quarter : (i + 1) * quarter])
        for ref in (upstream_ref, upstream_far_ref)
        for i in range(2)
    ]
    row = lax.broadcasted_iota(jnp.int32, (8, near.shape[1]), 0)
    ours = row // 2 % 2 == side
    blocks = []
    for chip in range(0, seq, 2):
        parts = []
        for at in (8 * chip, 8 * chip + 8):
            one, two, three, four = (block[at : at + 8] for block in by_quarter)
            comb = jnp.where(row < 4, jnp.where(row < 2, one, two), jnp.where(row < 6, three, four))
            disp = jnp.where(row < 4, 0.0, jnp.where(row < 6, near[at : at + 8], far[at : at + 8]))
            comb, disp = comb + pltpu.roll(comb, 4, 0), disp + pltpu.roll(disp, 4, 0)
            comb, disp = comb + pltpu.roll(comb, 2, 0), disp + pltpu.roll(disp, 2, 0)
            parts.append((near[at : at + 8], comb, disp))
        (even, even_comb, even_disp), (odd, odd_comb, odd_disp) = parts
        logits = jnp.where(row < 4, even, pltpu.roll(odd, 4, 0))
        comb = jnp.where(ours, jnp.where(row < 4, even_comb, odd_comb), 0.0)
        disp = jnp.where(ours, jnp.where(row < 4, even_disp, odd_disp), 0.0)
        blocks.append((logits, comb, disp))
    return [jnp.concatenate(parts, axis=0) for parts in zip(*blocks)]


def near_kernel(slots_ref, tokens_ref, tokens_far_ref, upstream_ref, upstream_far_ref, *part_refs):
    side = lax.axis_index("exp")
    parts = products(slots_ref, tokens_ref, tokens_far_ref, upstream_ref, upstream_far_ref, side)
    for ref, part in zip(part_refs, parts):
        ref[...] = part


def local_kernel(
    slots_ref, tokens_ref, tokens_far_ref, upstream_ref, upstream_far_ref, logit_ref, comb_ref, disp_ref, *outs
):
    send_ref, col_ref, row_ref, d_disp_ref, own_ref, cross_ref, tokens_rows_ref = outs
    side = lax.axis_index("exp")
    n_slots = col_ref.shape[0]
    seq, _, width = send_ref.shape
    half = tokens_ref.shape[1]
    extra = width - 2 * half
    groups = n_slots // 8 + 1
    parts = products(slots_ref, tokens_far_ref, tokens_ref, upstream_far_ref, upstream_ref, 1 - side)
    logits, d_comb, d_disp = (ref[...] + part for ref, part in zip((logit_ref, comb_ref, disp_ref), parts))
    row_exp = jnp.exp(logits - jnp.max(logits, axis=0, keepdims=True))
    combine = row_exp / jnp.sum(row_exp, axis=0, keepdims=True)
    row_part = combine * (d_comb - jnp.sum(combine * d_comb, axis=0, keepdims=True))
    top_high, top_low = split16(jnp.max(logits, axis=1, keepdims=True))
    col_exp = jnp.exp(logits - (top_high + top_low))
    sum_high, sum_low = split16(jnp.sum(col_exp, axis=1, keepdims=True))
    inner_high, inner_low = split16(jnp.sum(col_exp * d_disp, axis=1, keepdims=True))
    centre = (inner_high + inner_low) / (sum_high + sum_low)
    col_part = col_exp * (d_disp - centre)
    col_ref[...] = col_exp
    row_ref[...] = row_part
    d_disp_ref[...] = d_disp

    zero = jnp.zeros((4, col_ref.shape[1]), F32)
    ours = lax.broadcasted_iota(jnp.int32, zero.shape, 0) // 2 == side
    for chip in range(seq):
        span = slice(4 * chip, 4 * chip + 4)
        upper, lower = slice(8 * chip, 8 * chip + 4), slice(8 * chip + 4, 8 * chip + 8)
        kept = jnp.where(ours, combine[span], 0.0)
        own_ref[upper, :] = kept
        own_ref[lower, :] = zero
        cross_ref[upper, :] = jnp.concatenate([kept[2:4], kept[0:2]], axis=0)
        cross_ref[lower, :] = zero
        tokens_rows_ref[0, upper, :] = zero
        tokens_rows_ref[0, lower, :] = col_part[span]
        tokens_rows_ref[1, upper, :] = row_part[span]
        tokens_rows_ref[1, lower, :] = col_exp[span]
    left = jnp.dot(own_ref[...].astype(BF16), upstream_ref[...], preferred_element_type=F32)
    left = left + jnp.dot(cross_ref[...].astype(BF16), upstream_far_ref[...], preferred_element_type=F32)
    rows = tokens_rows_ref[...].reshape(16 * seq, -1).astype(BF16)
    by_tokens = jnp.dot(rows, tokens_ref[...], preferred_element_type=F32)
    left, right = left + by_tokens[: 8 * seq], by_tokens[8 * seq :]
    send_ref[:, :, :half] = left.astype(BF16).reshape(seq, 8, half)
    send_ref[:, :, half : 2 * half] = right.astype(BF16).reshape(seq, 8, half)

    lane = lax.broadcasted_iota(jnp.int32, (n_slots, extra), 1)
    stats = jnp.zeros((n_slots, extra), F32)
    for j, stat in enumerate((top_high, top_low, sum_high, sum_low, inner_high, inner_low)):
        stats = jnp.where(lane == j * groups, stat, stats)
    every = jnp.zeros((8, extra), F32)
    for group in range(groups - 1):
        every = every + pltpu.roll(stats[8 * group : 8 * group + 8], group + 1, 1)
    for chip in range(seq):
        own = stats[4 * chip : 4 * chip + 4]
        send_ref[chip, :, 2 * half :] = (every + jnp.concatenate([own, own], axis=0)).astype(BF16)


def column_stats(stats, groups):
    extra = stats.shape[1]
    pair = stats + pltpu.roll(stats, extra - groups, 1)
    return pair, pltpu.roll(pair, extra - 2 * groups, 1), pltpu.roll(pair, extra - 4 * groups, 1)


def finish_kernel(
    got_ref, slots_ref, other_ref, col_ref, row_ref, disp_ref, *outs_and_scratch
):
    params_out, tokens_out, sums_out, rows_ref, params_ref, tokens_ref, sums_ref, sems = outs_and_scratch
    me, side = lax.axis_index("seq"), lax.axis_index("exp")
    half = params_ref.shape[1]
    seq = got_ref.shape[0]
    n_slots = col_ref.shape[0]
    groups = n_slots // 8 + 1
    blocks = [column_stats(got_ref[chip, :, 2 * half :].astype(F32), groups) for chip in range(seq)]
    high = functools.reduce(jnp.maximum, [top for top, _, _ in blocks])
    scales = [jnp.exp(top - high) for top, _, _ in blocks]
    total = sum(scale * value for scale, (_, value, _) in zip(scales, blocks))
    centre = sum(scale * value for scale, (_, _, value) in zip(scales, blocks)) / total

    top, _, _ = column_stats(got_ref[pl.ds(me, 1), :, 2 * half :][0].astype(F32), groups)
    weight = jnp.exp(top - high) / total
    zero = jnp.zeros((6, col_ref.shape[1]), F32)
    for group in range(groups - 1):
        span = slice(8 * group, 8 * group + 8)
        dispatch = col_ref[span] * weight[:, group + 1 : group + 2]
        d_logit = row_ref[span] + dispatch * (disp_ref[span] - centre[:, group + 1 : group + 2])
        first = jnp.where(side == 0, dispatch, pltpu.roll(dispatch, 6, 0))
        second = jnp.where(side == 0, pltpu.roll(dispatch, 6, 0), dispatch)
        for j in range(2):
            span = slice(16 * group + 8 * j, 16 * group + 8 * j + 8)
            ours, theirs = first[4 * j : 4 * j + 2], second[4 * j : 4 * j + 2]
            rows_ref[0, span, :] = jnp.concatenate([d_logit[4 * j : 4 * j + 4], ours, zero[0:2]], axis=0)
            rows_ref[1, span, :] = jnp.concatenate([zero, theirs], axis=0)
    left = rows_ref[...].reshape(16 * seq, -1).astype(BF16)
    right = jnp.concatenate([ref[:, :, :half].reshape(8 * seq, half) for ref in (slots_ref, other_ref)], axis=0)
    patches = tokens_ref.shape[0] // 2
    copies = []
    for part in range(2):
        span = slice(part * patches, (part + 1) * patches)
        tokens_ref[span, :] = dot_tn(left[:, span], right).astype(BF16)
        copies.append(pltpu.make_async_copy(tokens_ref.at[span], tokens_out.at[span], sems.at[part]))
        copies[-1].start()

    upper = lax.broadcasted_iota(jnp.int32, centre.shape, 0) < 4
    left = right = jnp.zeros((8, half), F32)
    for chip, (scale, (_, own_total, own_inner)) in enumerate(zip(scales, blocks)):
        weight = scale / total
        by_left = jnp.where(upper, 1.0, weight)
        by_right = jnp.where(upper, 1.0, weight * (own_inner / own_total - centre))
        left = left + by_left[:, 0:1] * got_ref[chip, :, :half].astype(F32)
        right = right + by_right[:, 0:1] * got_ref[chip, :, half : 2 * half].astype(F32)
    sums_ref[:, :half] = left[0:2]
    sums_ref[:, half:] = left[2:4]
    params_ref[...] = left[4:8] + right[0:4] + right[4:8]
    for i, (source, target) in enumerate(((params_ref, params_out), (sums_ref, sums_out))):
        copies.append(pltpu.make_async_copy(source, target, sems.at[2 + i]))
        copies[-1].start()
    for copy in copies:
        copy.wait()


def shards(seq, tokens, upstream, slot_params, slot_outputs, slot_input_grads):
    patches, half = tokens.shape
    n_slots = slot_params.shape[0] * seq
    extra = -(-6 * (n_slots // 8 + 1) // 128) * 128
    sds = jax.ShapeDtypeStruct
    cores = [(0, 1), (1, 0)]

    tokens_far, far = (lax.ppermute(x, "exp", cores) for x in (tokens, upstream))
    seed = call(seed_kernel, sds((8, 128), F32), "seed", seq, cost_estimate=LONG)()
    chunks = call(pack_kernel, sds((seq, 8, half + half // 2), BF16), "pack", seq)(
        seed, slot_params, slot_outputs, slot_input_grads
    )
    slots = lax.all_to_all(chunks, "seq", split_axis=0, concat_axis=0, tiled=True)
    other = lax.ppermute(slots, "exp", cores)
    by_slot = sds((n_slots, patches), F32)
    near = call(near_kernel, (by_slot,) * 3, "near", seq, cost_estimate=LONG)(slots, tokens, tokens_far, upstream, far)
    send, col, row, disp = call(
        local_kernel,
        (sds((seq, 8, 2 * half + extra), BF16), by_slot, by_slot, by_slot),
        "local",
        seq,
        [pltpu.VMEM((8 * seq, patches), F32)] * 2 + [pltpu.VMEM((2, 8 * seq, patches), F32)],
    )(other, tokens, tokens_far, upstream, far, *near)
    got = lax.all_to_all(send, "seq", split_axis=0, concat_axis=0, tiled=True)
    param_grads, token_grads, slot_output_grads = call(
        finish_kernel,
        (sds((4, half), F32), sds((patches, half), BF16), sds((2, 2 * half), F32)),
        "finish",
        seq,
        [
            pltpu.VMEM((2, 8 * seq, patches), F32),
            pltpu.VMEM((4, half), F32),
            pltpu.VMEM((patches, half), BF16),
            pltpu.VMEM((2, 2 * half), F32),
            pltpu.SemaphoreType.DMA((4,)),
        ],
        out_specs=[pl.BlockSpec(memory_space=pl.ANY)] * 3,
    )(got, slots, other, col, row, disp)
    return token_grads, param_grads, slot_output_grads


def solution(mesh):
    in_specs = (
        P(("group", "seq"), "exp"),
        P(("group", "seq"), "exp"),
        P(("group", "seq"), "exp"),
        P(("group", "seq", "exp"), None),
        P(("group", "seq", "exp"), None),
    )
    out_specs = (
        P(("group", "seq"), "exp"),
        P(("group", "seq"), "exp"),
        P(("group", "seq", "exp"), None),
    )
    return jax.shard_map(
        functools.partial(shards, mesh.shape["seq"]),
        mesh=mesh,
        in_specs=in_specs,
        out_specs=out_specs,
        check_vma=False,
    )
```

time: 34.9 us -> 34.1 us (0.977)
  waiting for transfers between devices: 1.4 us -> 0.65 us
    ppermute x3, waiting for transfers between devices: 1.4 us -> 0.65 us  [the longest x1 0.64 us: shards(): other = lax.ppermute(slots, 'exp', cores)]
    pallas_call x2, Pallas kernels: 1.43 us -> 0.77 us  [the longest x1 0.77 us: shards(): call(near_kernel, (by_slot,) * 3, 'near', seq, cost_estimate=LONG)]
    pallas_call x1, Pallas kernels: 0.51 us -> 1.05 us  [shards(): call(local_kernel, (sds((seq, 8, 2 * half + extra), BF16), by_slot, by_sl...]
  transfers between devices with their start and end apart: 3 -> 3, of which waited for: 2 -> 1; matrix products, arithmetic and copies ran while one was open for 0% -> 0% of each run, Pallas kernels for 2% -> 2%
where the time goes in v4:
time: 34.1 us; the launch traced here: 33.8 us
  blocking collectives  28.6 us (84%)
  Pallas kernels  3.17 us (9%)
  between operations  0.69 us (2%)
  waiting for transfers between devices  0.65 us (2%)
  starting transfers between devices  0.6 us (2%)
    all_to_all x1, blocking collectives, shards(): lax.all_to_all(chunks, 'seq', split_axis=0, concat_axis=0, tiled=True)  15.3 us
    all_to_all x1, blocking collectives, shards(): got = lax.all_to_all(send, 'seq', split_axis=0, concat_axis=0, tiled=True)  13.3 us
    pallas_call x1, Pallas kernels, shards(): call(finish_kernel, (sds((4, half), F32), sds((patches, half), BF16), sds...  1.33 us
    pallas_call x1, Pallas kernels, shards(): call(local_kernel, (sds((seq, 8, 2 * half + extra), BF16), by_slot, by_sl...  1.05 us
    pallas_call x1, Pallas kernels, shards(): call(near_kernel, (by_slot,) * 3, 'near', seq, cost_estimate=LONG)  0.77 us
  transfers between devices with their start and end apart: 3, of which 1 were waited for; matrix products, arithmetic and copies ran while one was open for 0% of the time, Pallas kernels for 2%

profile of v4, /device:TPU:0, one launch (start us, length us, event | category | flops | bytes accessed | tf_op | source)
XLA Modules:
  0.0 33.8 jit_solution(9002359692708731377)
XLA Ops:
  0.6 0.0 copy-start.4
  0.6 0.0 copy-start.3
  0.7 0.0 copy-start.2
  0.7 0.5 %collective-permute-start.1 = (bf16[256,1024]{1,0:T(8,128)(2,1)}, bf16[256,1024]{1,0:T(8,128)(2,1)S(1)}, u32[]{:S(2)}, u32[]{:S(2)}) collective-permute-start(bf16[256,1024]{1,0:T(8,128)(2,1)} %tokens_ref.3), channel_id=1, source_target_pairs={{0,1},{1,0},{2,3},{3,2},{4,5},{5,4},{6,7},{7,6},{8,9},{9,8},{10,11... | collective-permute-start | bytes 1572872 | tf_op jit(solution)/shard_map/ppermute | solution.py:230
  1.2 0.1 collective-permute-start.2
  1.3 0.0 copy-start.1
  1.3 0.1 copy-done.4
  1.3 0.0 copy-done.3
  1.3 0.0 copy-done.2
  1.4 0.0 copy-start
  1.4 15.3 %all_to_all.10.slots_ref = bf16[8,8,1536]{2,1,0:T(8,128)(2,1)S(1)} all-to-all(bf16[8,8,1536]{2,1,0:T(8,128)(2,1)S(1)} %pack.1), channel_id=1, replica_groups=mesh['group'=2,'seq'=8,'exp'=2] {'seq'}, dimensions={0} | all-to-all | bytes 393216 | tf_op jit(solution)/shard_map/all_to_all | solution.py:235
  16.7 0.0 collective-permute-start
  16.7 0.0 collective-permute-done.1.tokens_far_ref
  16.7 0.0 collective-permute-done.2.upstream_far_ref
  16.7 0.0 copy-done.1
  16.7 0.0 copy-done
  16.7 0.8 %near.1 = (f32[32,256]{1,0:T(8,128)S(1)}, f32[32,256]{1,0:T(8,128)S(1)}, f32[32,256]{1,0:T(8,128)S(1)}) custom-call(bf16[8,8,1536]{2,1,0:T(8,128)(2,1)S(1)} %all_to_all.10.slots_ref, bf16[256,1024]{1,0:T(8,128)(2,1)S(1)} %copy-done, bf16[256,1024]{1,0:T(8,128)(2,1)S(1)} %collective-permute-done.1.tokens_far_ref, bf16[256,1024]{1,0:T(8,128)(2,1)S(1)} %copy-done.1, ...), custom_call_target="tpu_custom_call" | custom-call | flops 10000000000 | bytes 10000000 | tf_op jit(solution)/shard_map/near/pallas_call | solution.py:238
  17.5 0.6 %collective-permute-done.slots_ref.other_ref = bf16[8,8,1536]{2,1,0:T(8,128)(2,1)S(1)} collective-permute-done((bf16[8,8,1536]{2,1,0:T(8,128)(2,1)S(1)}, bf16[8,8,1536]{2,1,0:T(8,128)(2,1)S(1)}, u32[]{:S(2)}, u32[]{:S(2)}) %collective-permute-start) | collective-permute-done | bytes 196640 | tf_op jit(solution)/shard_map/ppermute | solution.py:236
  18.1 1.1 %local.1 = (bf16[8,8,2176]{2,1,0:T(8,128)(2,1)S(1)}, f32[32,256]{1,0:T(8,128)S(1)}, f32[32,256]{1,0:T(8,128)S(1)}, f32[32,256]{1,0:T(8,128)S(1)}) custom-call(bf16[8,8,1536]{2,1,0:T(8,128)(2,1)S(1)} %collective-permute-done.slots_ref.other_ref, bf16[256,1024]{1,0:T(8,128)(2,1)S(1)} %copy-done, bf16[256,1024]{1,0:T(8,128)(2,1)S(1)} %collective-permute-done.1.tokens_far_ref, ...), custom_call_target="tpu_custom_call" | custom-call | tf_op jit(solution)/shard_map/local/pallas_call | solution.py:239
  19.2 13.3 %all_to_all.11.got_ref = bf16[8,8,2176]{2,1,0:T(8,128)(2,1)S(1)} all-to-all(bf16[8,8,2176]{2,1,0:T(8,128)(2,1)S(1)} %get-tuple-element.16), channel_id=1, replica_groups=mesh['group'=2,'seq'=8,'exp'=2] {'seq'}, dimensions={0} | all-to-all | bytes 557056 | tf_op jit(solution)/shard_map/all_to_all | solution.py:246
  32.5 1.3 %finish.1 = (f32[4,1024]{1,0:T(4,128)}, bf16[256,1024]{1,0:T(8,128)(2,1)}, f32[2,2048]{1,0:T(2,128)}) custom-call(bf16[8,8,2176]{2,1,0:T(8,128)(2,1)S(1)} %all_to_all.11.got_ref, bf16[8,8,1536]{2,1,0:T(8,128)(2,1)S(1)} %all_to_all.10.slots_ref, bf16[8,8,1536]{2,1,0:T(8,128)(2,1)S(1)} %collective-permute-done.slots_ref.other_ref, ...), custom_call_target="tpu_custom_call" | custom-call | tf_op jit(solution)/shard_map/finish/pallas_call | solution.py:247
  (2 shorter events, 0.0 us)
Async XLA Ops:
  0.6 0.7 %copy-start.4 = (bf16[2,2048]{1,0:T(2,128)(2,1)S(1)}, bf16[2,2048]{1,0:T(2,128)(2,1)}, u32[]{:S(2)}) copy-start(bf16[2,2048]{1,0:T(2,128)(2,1)} %grads_ref.1) | copy-start | bytes 24580
  0.6 0.7 %copy-start.3 = (bf16[2,2048]{1,0:T(2,128)(2,1)S(1)}, bf16[2,2048]{1,0:T(2,128)(2,1)}, u32[]{:S(2)}) copy-start(bf16[2,2048]{1,0:T(2,128)(2,1)} %outs_ref.1) | copy-start | bytes 24580
  0.7 0.7 %copy-start.2 = (bf16[4,1024]{1,0:T(4,128)(2,1)S(1)}, bf16[4,1024]{1,0:T(4,128)(2,1)}, u32[]{:S(2)}) copy-start(bf16[4,1024]{1,0:T(4,128)(2,1)} %params_ref.1) | copy-start | bytes 24580
  0.7 16.0 %collective-permute-start.1 = (bf16[256,1024]{1,0:T(8,128)(2,1)}, bf16[256,1024]{1,0:T(8,128)(2,1)S(1)}, u32[]{:S(2)}, u32[]{:S(2)}) collective-permute-start(bf16[256,1024]{1,0:T(8,128)(2,1)} %tokens_ref.3), channel_id=1, source_target_pairs={{0,1},{1,0},{2,3},{3,2},{4,5},{5,4},{6,7},{7,6},{8,9},{9,8},{10,11... | collective-permute-start | bytes 1572872 | tf_op jit(solution)/shard_map/ppermute | solution.py:230
  1.2 15.5 %collective-permute-start.2 = (bf16[256,1024]{1,0:T(8,128)(2,1)}, bf16[256,1024]{1,0:T(8,128)(2,1)S(1)}, u32[]{:S(2)}, u32[]{:S(2)}) collective-permute-start(bf16[256,1024]{1,0:T(8,128)(2,1)} %upstream_ref.3), channel_id=1, source_target_pairs={{0,1},{1,0},{2,3},{3,2},{4,5},{5,4},{6,7},{7,6},{8,9},{9,8},{10,11... | collective-permute-start | bytes 1572872 | tf_op jit(solution)/shard_map/ppermute | solution.py:230
  1.3 15.4 %copy-start.1 = (bf16[256,1024]{1,0:T(8,128)(2,1)S(1)}, bf16[256,1024]{1,0:T(8,128)(2,1)}, u32[]{:S(2)}) copy-start(bf16[256,1024]{1,0:T(8,128)(2,1)} %upstream_ref.3) | copy-start | bytes 1572868
  1.4 15.4 %copy-start = (bf16[256,1024]{1,0:T(8,128)(2,1)S(1)}, bf16[256,1024]{1,0:T(8,128)(2,1)}, u32[]{:S(2)}) copy-start(bf16[256,1024]{1,0:T(8,128)(2,1)} %tokens_ref.3) | copy-start | bytes 1572868
  16.7 1.4 %collective-permute-start = (bf16[8,8,1536]{2,1,0:T(8,128)(2,1)S(1)}, bf16[8,8,1536]{2,1,0:T(8,128)(2,1)S(1)}, u32[]{:S(2)}, u32[]{:S(2)}) collective-permute-start(bf16[8,8,1536]{2,1,0:T(8,128)(2,1)S(1)} %all_to_all.10.slots_ref), channel_id=1, source_target_pairs={{0,1},{1,0},{2,3},{3,2},{4,5},{5,4},{6,7},{7,6},{8,9},{9,8},{10,11... | collective-permute-start | bytes 589832 | tf_op jit(solution)/shard_map/ppermute | solution.py:236

commit v5 on v4

--- a/solution.py
+++ b/solution.py
@@ -12,8 +12,8 @@
 LONG = pl.CostEstimate(flops=10**10, bytes_accessed=10**7, transcendentals=0)
 
 
-def dot_nt(left, right):
-    return lax.dot_general(left, right, (((1,), (1,)), ((), ())), preferred_element_type=F32)
+def dot(left, right):
+    return jnp.dot(left, right, preferred_element_type=F32)
 
 
 def dot_tn(left, right):
@@ -61,13 +61,13 @@
 
 def products(slots_ref, tokens_ref, tokens_far_ref, upstream_ref, upstream_far_ref, side):
     seq, _, width = slots_ref.shape
-    half = tokens_ref.shape[1]
+    half = tokens_ref.shape[0]
     quarter = half // 2
     left = slots_ref[:, :, :half].reshape(8 * seq, half)
     right = slots_ref[:, :, half:].reshape(8 * seq, quarter)
-    near, far = dot_nt(left, tokens_ref[...]), dot_nt(left, tokens_far_ref[...])
+    near, far = dot(left, tokens_ref[...]), dot(left, tokens_far_ref[...])
     by_quarter = [
-        dot_nt(right, ref[:, i * quarter : (i + 1) * quarter])
+        dot(right, ref[i * quarter : (i + 1) * quarter, :])
         for ref in (upstream_ref, upstream_far_ref)
         for i in range(2)
     ]
@@ -91,24 +91,37 @@
     return [jnp.concatenate(parts, axis=0) for parts in zip(*blocks)]
 
 
-def near_kernel(slots_ref, tokens_ref, tokens_far_ref, upstream_ref, upstream_far_ref, *part_refs):
+def near_kernel(slots_ref, *refs):
     side = lax.axis_index("exp")
-    parts = products(slots_ref, tokens_ref, tokens_far_ref, upstream_ref, upstream_far_ref, side)
-    for ref, part in zip(part_refs, parts):
+    inputs, turned, part_refs = refs[:4], refs[4:8], refs[8:]
+    for source, target in zip(inputs, turned):
+        target[...] = source[...].T
+    for ref, part in zip(part_refs, products(slots_ref, *turned, side)):
         ref[...] = part
 
 
+def receiver(me, fours, step, four):
+    return lax.bitwise_xor(me, step + 4 * four) if fours == 2 else 4 * four + lax.bitwise_xor(lax.rem(me, 4), step)
+
+
+def crosses(fours, step, four):
+    return (step > 0) != (fours == 2 and four > 0)
+
+
 def local_kernel(
-    slots_ref, tokens_ref, tokens_far_ref, upstream_ref, upstream_far_ref, logit_ref, comb_ref, disp_ref, *outs
+    slots_ref, tokens_ref, tokens_far_ref, upstream_ref, upstream_far_ref, *refs
 ):
-    send_ref, col_ref, row_ref, d_disp_ref, own_ref, cross_ref, tokens_rows_ref = outs
-    side = lax.axis_index("exp")
-    n_slots = col_ref.shape[0]
-    seq, _, width = send_ref.shape
+    turned, (logit_ref, comb_ref, disp_ref), outs = refs[:4], refs[4:7], refs[7:]
+    sends, (col_ref, row_ref, d_disp_ref) = outs[:4], outs[4:7]
+    first_ref, second_ref, stats_ref, near_ref, far_ref = outs[7:]
+    side, me = lax.axis_index("exp"), lax.axis_index("seq")
+    n_slots, patches = col_ref.shape
+    fours, _, width = sends[0].shape
+    seq = 4 * fours
     half = tokens_ref.shape[1]
     extra = width - 2 * half
     groups = n_slots // 8 + 1
-    parts = products(slots_ref, tokens_far_ref, tokens_ref, upstream_far_ref, upstream_ref, 1 - side)
+    parts = products(slots_ref, turned[1], turned[0], turned[3], turned[2], 1 - side)
     logits, d_comb, d_disp = (ref[...] + part for ref, part in zip((logit_ref, comb_ref, disp_ref), parts))
     row_exp = jnp.exp(logits - jnp.max(logits, axis=0, keepdims=True))
     combine = row_exp / jnp.sum(row_exp, axis=0, keepdims=True)
@@ -123,28 +136,6 @@
     row_ref[...] = row_part
     d_disp_ref[...] = d_disp
 
-    zero = jnp.zeros((4, col_ref.shape[1]), F32)
-    ours = lax.broadcasted_iota(jnp.int32, zero.shape, 0) // 2 == side
-    for chip in range(seq):
-        span = slice(4 * chip, 4 * chip + 4)
-        upper, lower = slice(8 * chip, 8 * chip + 4), slice(8 * chip + 4, 8 * chip + 8)
-        kept = jnp.where(ours, combine[span], 0.0)
-        own_ref[upper, :] = kept
-        own_ref[lower, :] = zero
-        cross_ref[upper, :] = jnp.concatenate([kept[2:4], kept[0:2]], axis=0)
-        cross_ref[lower, :] = zero
-        tokens_rows_ref[0, upper, :] = zero
-        tokens_rows_ref[0, lower, :] = col_part[span]
-        tokens_rows_ref[1, upper, :] = row_part[span]
-        tokens_rows_ref[1, lower, :] = col_exp[span]
-    left = jnp.dot(own_ref[...].astype(BF16), upstream_ref[...], preferred_element_type=F32)
-    left = left + jnp.dot(cross_ref[...].astype(BF16), upstream_far_ref[...], preferred_element_type=F32)
-    rows = tokens_rows_ref[...].reshape(16 * seq, -1).astype(BF16)
-    by_tokens = jnp.dot(rows, tokens_ref[...], preferred_element_type=F32)
-    left, right = left + by_tokens[: 8 * seq], by_tokens[8 * seq :]
-    send_ref[:, :, :half] = left.astype(BF16).reshape(seq, 8, half)
-    send_ref[:, :, half : 2 * half] = right.astype(BF16).reshape(seq, 8, half)
-
     lane = lax.broadcasted_iota(jnp.int32, (n_slots, extra), 1)
     stats = jnp.zeros((n_slots, extra), F32)
     for j, stat in enumerate((top_high, top_low, sum_high, sum_low, inner_high, inner_low)):
@@ -152,9 +143,47 @@
     every = jnp.zeros((8, extra), F32)
     for group in range(groups - 1):
         every = every + pltpu.roll(stats[8 * group : 8 * group + 8], group + 1, 1)
-    for chip in range(seq):
-        own = stats[4 * chip : 4 * chip + 4]
-        send_ref[chip, :, 2 * half :] = (every + jnp.concatenate([own, own], axis=0)).astype(BF16)
+
+    row = lax.broadcasted_iota(jnp.int32, (8, patches), 0)
+    for chip in range(0, seq, 2):
+        span = slice(4 * chip, 4 * chip + 8)
+        for ref, upper, lower in ((first_ref, combine, col_part), (second_ref, row_part, col_exp)):
+            upper, lower = upper[span], lower[span]
+            ref[chip] = jnp.where(row < 4, upper, pltpu.roll(lower, 4, 0))
+            ref[chip + 1] = jnp.where(row < 4, pltpu.roll(upper, 4, 0), lower)
+        own = stats[span]
+        other = pltpu.roll(own, 4, 0)
+        upper = lax.broadcasted_iota(jnp.int32, own.shape, 0) < 4
+        stats_ref[chip] = every + jnp.where(upper, own, other)
+        stats_ref[chip + 1] = every + jnp.where(upper, other, own)
+
+    ours, theirs = (row // 2 == core for core in (side, 1 - side))
+    for step in range(4):
+        for four in range(fours):
+            at = step * fours + four
+            chip = receiver(me, fours, step, four)
+            first, second = first_ref[chip], second_ref[chip]
+            turned_first = jnp.where(row % 4 < 2, pltpu.roll(first, 6, 0), pltpu.roll(first, 2, 0))
+            lower = jnp.where(row < 4, 0.0, first)
+            here, there = (near_ref, far_ref) if not crosses(fours, step, four) else (far_ref, near_ref)
+            direct, swapped = (first, turned_first) if not crosses(fours, step, four) else (turned_first, first)
+            here[0, at], here[1, at] = lower, second
+            there[0, at] = there[1, at] = jnp.zeros_like(lower)
+            near_ref[2, at] = jnp.where(ours, direct, 0.0)
+            far_ref[2, at] = jnp.where(theirs, swapped, 0.0)
+
+    total = None
+    for ref, token_half, upstream_half in ((near_ref, tokens_ref, upstream_ref), (far_ref, tokens_far_ref, upstream_far_ref)):
+        rows = ref[...].reshape(3 * 8 * seq, patches).astype(BF16)
+        by_tokens = dot(rows[: 16 * seq], token_half[...])
+        left, right = by_tokens[: 8 * seq] + dot(rows[16 * seq :], upstream_half[...]), by_tokens[8 * seq :]
+        total = (left, right) if total is None else (total[0] + left, total[1] + right)
+    left, right = (value.reshape(4, fours, 8, half).astype(BF16) for value in total)
+    for step, send_ref in enumerate(sends):
+        send_ref[:, :, :half] = left[step]
+        send_ref[:, :, half : 2 * half] = right[step]
+        for four in range(fours):
+            send_ref[four, :, 2 * half :] = stats_ref[receiver(me, fours, step, four)].astype(BF16)
 
 
 def column_stats(stats, groups):
@@ -163,22 +192,56 @@
     return pair, pltpu.roll(pair, extra - 2 * groups, 1), pltpu.roll(pair, extra - 4 * groups, 1)
 
 
-def finish_kernel(
-    got_ref, slots_ref, other_ref, col_ref, row_ref, disp_ref, *outs_and_scratch
-):
-    params_out, tokens_out, sums_out, rows_ref, params_ref, tokens_ref, sums_ref, sems = outs_and_scratch
-    me, side = lax.axis_index("seq"), lax.axis_index("exp")
-    half = params_ref.shape[1]
-    seq = got_ref.shape[0]
-    n_slots = col_ref.shape[0]
-    groups = n_slots // 8 + 1
-    blocks = [column_stats(got_ref[chip, :, 2 * half :].astype(F32), groups) for chip in range(seq)]
+def merge_stats(chunks, half, groups):
+    blocks = [column_stats(chunk[:, 2 * half :].astype(F32), groups) for chunk in chunks]
     high = functools.reduce(jnp.maximum, [top for top, _, _ in blocks])
     scales = [jnp.exp(top - high) for top, _, _ in blocks]
     total = sum(scale * value for scale, (_, value, _) in zip(scales, blocks))
-    centre = sum(scale * value for scale, (_, _, value) in zip(scales, blocks)) / total
-
-    top, _, _ = column_stats(got_ref[pl.ds(me, 1), :, 2 * half :][0].astype(F32), groups)
+    inner = sum(scale * value for scale, (_, _, value) in zip(scales, blocks))
+    return high, total, inner, scales, [inner / total for _, total, inner in blocks]
+
+
+def merge_kernel(*refs, groups, half):
+    chunk_refs, out_ref = refs[:4], refs[4]
+    fours, _, width = chunk_refs[0].shape
+    merged = out_ref.shape[0]
+    lane = lax.broadcasted_iota(jnp.int32, (8, width - 2 * half), 1)
+    upper = lax.broadcasted_iota(jnp.int32, lane.shape, 0) < 4
+    for four in range(merged):
+        chunks = [ref.at[four + fours - merged] for ref in chunk_refs]
+        high, total, inner, scales, means = merge_stats(chunks, half, groups)
+        stats = [part for stat in (high, total, inner) for part in split16(stat)]
+        centre = (stats[4] + stats[5]) / (stats[2] + stats[3])
+        left = right = jnp.zeros((8, half), F32)
+        for chunk, scale, mean in zip(chunks, scales, means):
+            weight = jnp.where(upper, 1.0, scale)[:, 0:1]
+            moved = jnp.where(upper, 0.0, scale * (mean - centre))[:, 0:1]
+            by_right = chunk[:, half : 2 * half].astype(F32)
+            left = left + weight * chunk[:, :half].astype(F32) + moved * by_right
+            right = right + weight * by_right
+        out_ref[four, :, :half] = left.astype(BF16)
+        out_ref[four, :, half : 2 * half] = right.astype(BF16)
+        block = sum(pltpu.roll(jnp.where(lane < groups, stat, 0.0), j * groups, 1) for j, stat in enumerate(stats))
+        out_ref[four, :, 2 * half :] = block.astype(BF16)
+
+
+def finish_kernel(*refs):
+    inputs, outs_and_scratch = refs[:-8], refs[-8:]
+    slots_ref, other_ref, col_ref, row_ref, disp_ref, mine_ref, *rest = inputs
+    params_out, tokens_out, sums_out, rows_ref, params_ref, tokens_ref, sums_ref, sems = outs_and_scratch
+    side = lax.axis_index("exp")
+    half = params_ref.shape[1]
+    seq = slots_ref.shape[0]
+    n_slots = col_ref.shape[0]
+    groups = n_slots // 8 + 1
+    if seq == 8:
+        chunks = [ref.at[0] for ref in (mine_ref, *rest)]
+    else:
+        chunks = [rest[0].at[four] for four in range(rest[0].shape[0])]
+    high, total, inner, scales, means = merge_stats(chunks, half, groups)
+    centre = inner / total
+
+    top, _, _ = column_stats(mine_ref[0, :, 2 * half :].astype(F32), groups)
     weight = jnp.exp(top - high) / total
     zero = jnp.zeros((6, col_ref.shape[1]), F32)
     for group in range(groups - 1):
@@ -204,12 +267,12 @@
 
     upper = lax.broadcasted_iota(jnp.int32, centre.shape, 0) < 4
     left = right = jnp.zeros((8, half), F32)
-    for chip, (scale, (_, own_total, own_inner)) in enumerate(zip(scales, blocks)):
+    for chunk, scale, mean in zip(chunks, scales, means):
         weight = scale / total
         by_left = jnp.where(upper, 1.0, weight)
-        by_right = jnp.where(upper, 1.0, weight * (own_inner / own_total - centre))
-        left = left + by_left[:, 0:1] * got_ref[chip, :, :half].astype(F32)
-        right = right + by_right[:, 0:1] * got_ref[chip, :, half : 2 * half].astype(F32)
+        by_right = jnp.where(upper, 1.0, weight * (mean - centre))
+        left = left + by_left[:, 0:1] * chunk[:, :half].astype(F32)
+        right = right + by_right[:, 0:1] * chunk[:, half : 2 * half].astype(F32)
     sums_ref[:, :half] = left[0:2]
     sums_ref[:, half:] = left[2:4]
     params_ref[...] = left[4:8] + right[0:4] + right[4:8]
@@ -220,6 +283,11 @@
         copy.wait()
 
 
+def to_other_core(value, seq, step):
+    pairs = [(2 * chip + core, 2 * (chip ^ step) + 1 - core) for chip in range(seq) for core in range(2)]
+    return lax.ppermute(value, ("seq", "exp"), pairs)
+
+
 def shards(seq, tokens, upstream, slot_params, slot_outputs, slot_input_grads):
     patches, half = tokens.shape
     n_slots = slot_params.shape[0] * seq
@@ -235,15 +303,33 @@
     slots = lax.all_to_all(chunks, "seq", split_axis=0, concat_axis=0, tiled=True)
     other = lax.ppermute(slots, "exp", cores)
     by_slot = sds((n_slots, patches), F32)
-    near = call(near_kernel, (by_slot,) * 3, "near", seq, cost_estimate=LONG)(slots, tokens, tokens_far, upstream, far)
-    send, col, row, disp = call(
+    turned = sds((half, patches), BF16)
+    near = call(near_kernel, (turned,) * 4 + (by_slot,) * 3, "near", seq, cost_estimate=LONG)(
+        slots, tokens, tokens_far, upstream, far
+    )
+    fours = seq // 4
+    chunk = (8, 2 * half + extra)
+    *sends, col, row, disp = call(
         local_kernel,
-        (sds((seq, 8, 2 * half + extra), BF16), by_slot, by_slot, by_slot),
+        (sds((fours, *chunk), BF16),) * 4 + (by_slot,) * 3,
         "local",
         seq,
-        [pltpu.VMEM((8 * seq, patches), F32)] * 2 + [pltpu.VMEM((2, 8 * seq, patches), F32)],
+        [pltpu.VMEM((seq, 8, patches), F32)] * 2
+        + [pltpu.VMEM((seq, 8, extra), F32)]
+        + [pltpu.VMEM((3, seq, 8, patches), F32)] * 2,
     )(other, tokens, tokens_far, upstream, far, *near)
-    got = lax.all_to_all(send, "seq", split_axis=0, concat_axis=0, tiled=True)
+    got = [sends[0]] + [to_other_core(sends[step], seq, step) for step in range(1, 4)]
+    merged = call(
+        functools.partial(merge_kernel, groups=n_slots // 8 + 1, half=half),
+        sds((1 if fours == 2 else fours, *chunk), BF16),
+        "merge",
+        seq,
+    )(*got)
+    if fours == 2:
+        got.append(to_other_core(merged, seq, 4))
+    else:
+        same = [[4 * four + step for four in range(fours)] for step in range(4)]
+        got[1:] = [lax.all_to_all(merged, "seq", split_axis=0, concat_axis=0, tiled=True, axis_index_groups=same)]
     param_grads, token_grads, slot_output_grads = call(
         finish_kernel,
         (sds((4, half), F32), sds((patches, half), BF16), sds((2, 2 * half), F32)),
@@ -257,7 +343,7 @@
             pltpu.SemaphoreType.DMA((4,)),
         ],
         out_specs=[pl.BlockSpec(memory_space=pl.ANY)] * 3,
-    )(got, slots, other, col, row, disp)
+    )(slots, other, col, row, disp, *got)
     return token_grads, param_grads, slot_output_grads
 
 

time: 34.1 us -> 32.6 us (0.956)
  the two profiles are of different devices: /device:TPU:0 before, /device:TPU:1 now
where the time goes in v5:
time: 32.6 us; the launch traced here: 32.4 us
  blocking collectives  13.1 us (40%)
  waiting for transfers between devices  8.09 us (25%)
  starting transfers between devices  6.97 us (21%)
  Pallas kernels  3.36 us (10%)
  between operations  0.7 us (2%)
    all_to_all x1, blocking collectives, shards(): lax.all_to_all(chunks, 'seq', split_axis=0, concat_axis=0, tiled=True)  13.1 us
    ppermute x4, waiting for transfers between devices, to_other_core(): return lax.ppermute(value, ('seq', 'exp'), pairs)  7.83 us
    ppermute x4, starting transfers between devices, to_other_core(): return lax.ppermute(value, ('seq', 'exp'), pairs)  4.18 us
    ppermute x1, starting transfers between devices, shards(): other = lax.ppermute(slots, 'exp', cores)  2.21 us
    pallas_call x1, Pallas kernels, shards(): call(finish_kernel, (sds((4, half), F32), sds((patches, half), BF16), sds...  1.32 us
    pallas_call x1, Pallas kernels, shards(): call(local_kernel, (sds((fours, *chunk), BF16),) * 4 + (by_slot,) * 3, 'l...  0.98 us
    pallas_call x1, Pallas kernels, shards(): call(near_kernel, (turned,) * 4 + (by_slot,) * 3, 'near', seq, cost_estim...  0.79 us
  transfers between devices with their start and end apart: 7, of which 5 were waited for; matrix products, arithmetic and copies ran while one was open for 0% of the time, Pallas kernels for 3%

profile of v5, /device:TPU:1, one launch (start us, length us, event | category | flops | bytes accessed | tf_op | source)
XLA Modules:
  0.0 32.4 jit_solution(11314663835737593949)
XLA Ops:
  0.6 0.0 copy-start.4
  0.6 0.0 copy-start.3
  0.7 0.0 copy-start.2
  0.7 0.1 collective-permute-start.1
  0.8 0.5 %collective-permute-start.2 = (bf16[256,1024]{1,0:T(8,128)(2,1)}, bf16[256,1024]{1,0:T(8,128)(2,1)S(1)}, u32[]{:S(2)}, u32[]{:S(2)}) collective-permute-start(bf16[256,1024]{1,0:T(8,128)(2,1)} %upstream_ref.1), channel_id=1, source_target_pairs={{0,1},{1,0},{2,3},{3,2},{4,5},{5,4},{6,7},{7,6},{8,9},{9,8},{10,11... | collective-permute-start | bytes 1572872 | tf_op jit(solution)/shard_map/ppermute | solution.py:298
  1.2 0.0 copy-start.1
  1.2 0.1 copy-done.4
  1.3 0.0 copy-done.3
  1.3 0.0 copy-done.2
  1.4 0.0 copy-start
  1.4 13.1 %all_to_all.5.slots_ref.refs_0_ = bf16[8,8,1536]{2,1,0:T(8,128)(2,1)S(1)} all-to-all(bf16[8,8,1536]{2,1,0:T(8,128)(2,1)S(1)} %pack.1), channel_id=1, replica_groups=mesh['group'=2,'seq'=8,'exp'=2] {'seq'}, dimensions={0} | all-to-all | bytes 393216 | tf_op jit(solution)/shard_map/all_to_all | solution.py:303
  14.5 2.2 %collective-permute-start = (bf16[8,8,1536]{2,1,0:T(8,128)(2,1)S(1)}, bf16[8,8,1536]{2,1,0:T(8,128)(2,1)S(1)}, u32[]{:S(2)}, u32[]{:S(2)}) collective-permute-start(bf16[8,8,1536]{2,1,0:T(8,128)(2,1)S(1)} %all_to_all.5.slots_ref.refs_0_), channel_id=1, source_target_pairs={{0,1},{1,0},{2,3},{3,2},{4,5},{5,4},{6,7},{7,6},{8,9},{9,8},{10,11... | collective-permute-start | bytes 589832 | tf_op jit(solution)/shard_map/ppermute | solution.py:304
  16.7 0.0 collective-permute-done.1.refs_1_.tokens_far_ref
  16.8 0.0 collective-permute-done.2.refs_3_.upstream_far_ref
  16.8 0.0 copy-done.1
  16.8 0.0 copy-done
  16.8 0.8 %near.1 = (bf16[1024,256]{1,0:T(8,128)(2,1)S(1)}, bf16[1024,256]{1,0:T(8,128)(2,1)S(1)}, bf16[1024,256]{1,0:T(8,128)(2,1)S(1)}, bf16[1024,256]{1,0:T(8,128)(2,1)...) custom-call(bf16[8,8,1536]{2,1,0:T(8,128)(2,1)S(1)} %all_to_all.5.slots_ref.refs_0_, ...), custom_call_target="tpu_custom_call" | custom-call | flops 10000000000 | bytes 10000000 | tf_op jit(solution)/shard_map/near/pallas_call | solution.py:307
  17.6 0.3 collective-permute-done.slots_ref.refs_1_
  17.8 1.0 %local.1 = (bf16[2,8,2176]{2,1,0:T(8,128)(2,1)S(1)}, bf16[2,8,2176]{2,1,0:T(8,128)(2,1)S(1)}, bf16[2,8,2176]{2,1,0:T(8,128)(2,1)S(1)}, bf16[2,8,2176]{2,1,0:T(8,...) custom-call(bf16[8,8,1536]{2,1,0:T(8,128)(2,1)S(1)} %collective-permute-done.slots_ref.refs_1_, ...), custom_call_target="tpu_custom_call" | custom-call | tf_op jit(solution)/shard_map/local/pallas_call | solution.py:312
  18.8 1.0 %collective-permute-start.3 = (bf16[2,8,2176]{2,1,0:T(8,128)(2,1)S(1)}, bf16[2,8,2176]{2,1,0:T(8,128)(2,1)S(1)}, u32[]{:S(2)}, u32[]{:S(2)}) collective-permute-start(bf16[2,8,2176]{2,1,0:T(8,128)(2,1)S(1)} %get-tuple-element.31), channel_id=1, source_target_pairs={{0,3},{1,2},{2,1},{3,0},{4,7},{5,6},{6,5},{7,4},{8,11},{9,10},{10,... | collective-permute-start | bytes 208904 | tf_op jit(solution)/shard_map/ppermute | solution.py:288
  19.8 0.2 collective-permute-start.4
  20.0 2.1 %collective-permute-start.5 = (bf16[2,8,2176]{2,1,0:T(8,128)(2,1)S(1)}, bf16[2,8,2176]{2,1,0:T(8,128)(2,1)S(1)}, u32[]{:S(2)}, u32[]{:S(2)}) collective-permute-start(bf16[2,8,2176]{2,1,0:T(8,128)(2,1)S(1)} %get-tuple-element.33), channel_id=1, source_target_pairs={{0,7},{1,6},{2,5},{3,4},{4,3},{5,2},{6,1},{7,0},{8,15},{9,14},{10,... | collective-permute-start | bytes 208904 | tf_op jit(solution)/shard_map/ppermute | solution.py:288
  22.1 1.3 %collective-permute-done.3.refs_1_.refs_6_ = bf16[2,8,2176]{2,1,0:T(8,128)(2,1)S(1)} collective-permute-done((bf16[2,8,2176]{2,1,0:T(8,128)(2,1)S(1)}, bf16[2,8,2176]{2,1,0:T(8,128)(2,1)S(1)}, u32[]{:S(2)}, u32[]{:S(2)}) %collective-permute-start.3) | collective-permute-done | bytes 69664 | tf_op jit(solution)/shard_map/ppermute | solution.py:288
  23.3 1.2 %collective-permute-done.4.refs_2_.refs_7_ = bf16[2,8,2176]{2,1,0:T(8,128)(2,1)S(1)} collective-permute-done((bf16[2,8,2176]{2,1,0:T(8,128)(2,1)S(1)}, bf16[2,8,2176]{2,1,0:T(8,128)(2,1)S(1)}, u32[]{:S(2)}, u32[]{:S(2)}) %collective-permute-start.4) | collective-permute-done | bytes 69664 | tf_op jit(solution)/shard_map/ppermute | solution.py:288
  24.5 1.2 %collective-permute-done.5.refs_3_.refs_8_ = bf16[2,8,2176]{2,1,0:T(8,128)(2,1)S(1)} collective-permute-done((bf16[2,8,2176]{2,1,0:T(8,128)(2,1)S(1)}, bf16[2,8,2176]{2,1,0:T(8,128)(2,1)S(1)}, u32[]{:S(2)}, u32[]{:S(2)}) %collective-permute-start.5) | collective-permute-done | bytes 69664 | tf_op jit(solution)/shard_map/ppermute | solution.py:288
  25.7 0.2 merge.1
  26.0 0.9 %collective-permute-start.6 = (bf16[1,8,2176]{2,1,0:T(8,128)(2,1)S(1)}, bf16[1,8,2176]{2,1,0:T(8,128)(2,1)S(1)}, u32[]{:S(2)}, u32[]{:S(2)}) collective-permute-start(bf16[1,8,2176]{2,1,0:T(8,128)(2,1)S(1)} %merge.1), channel_id=1, source_target_pairs={{0,9},{1,8},{2,11},{3,10},{4,13},{5,12},{6,15},{7,14},{8,1},{9,0},... | collective-permute-start | bytes 104456 | tf_op jit(solution)/shard_map/ppermute | solution.py:288
  26.9 4.1 %collective-permute-done.6.refs_9_ = bf16[1,8,2176]{2,1,0:T(8,128)(2,1)S(1)} collective-permute-done((bf16[1,8,2176]{2,1,0:T(8,128)(2,1)S(1)}, bf16[1,8,2176]{2,1,0:T(8,128)(2,1)S(1)}, u32[]{:S(2)}, u32[]{:S(2)}) %collective-permute-start.6) | collective-permute-done | bytes 34848 | tf_op jit(solution)/shard_map/ppermute | solution.py:288
  31.1 1.3 %finish.1 = (f32[4,1024]{1,0:T(4,128)}, bf16[256,1024]{1,0:T(8,128)(2,1)}, f32[2,2048]{1,0:T(2,128)}) custom-call(bf16[8,8,1536]{2,1,0:T(8,128)(2,1)S(1)} %all_to_all.5.slots_ref.refs_0_, bf16[8,8,1536]{2,1,0:T(8,128)(2,1)S(1)} %collective-permute-done.slots_ref.refs_1_, f32[32,256]{1,0:T(8,128)S(1)} %get-tuple-element.27.refs_2_, ...), custom_call_target="tpu_custom_call" | custom-call | tf_op jit(solution)/shard_map/finish/pallas_call | solution.py:333
  (2 shorter events, 0.0 us)
Async XLA Ops:
  0.6 0.7 %copy-start.4 = (bf16[2,2048]{1,0:T(2,128)(2,1)S(1)}, bf16[2,2048]{1,0:T(2,128)(2,1)}, u32[]{:S(2)}) copy-start(bf16[2,2048]{1,0:T(2,128)(2,1)} %grads_ref.1) | copy-start | bytes 24580
  0.6 0.7 %copy-start.3 = (bf16[2,2048]{1,0:T(2,128)(2,1)S(1)}, bf16[2,2048]{1,0:T(2,128)(2,1)}, u32[]{:S(2)}) copy-start(bf16[2,2048]{1,0:T(2,128)(2,1)} %outs_ref.1) | copy-start | bytes 24580
  0.7 0.7 %copy-start.2 = (bf16[4,1024]{1,0:T(4,128)(2,1)S(1)}, bf16[4,1024]{1,0:T(4,128)(2,1)}, u32[]{:S(2)}) copy-start(bf16[4,1024]{1,0:T(4,128)(2,1)} %params_ref.1) | copy-start | bytes 24580
  0.7 16.1 %collective-permute-start.1 = (bf16[256,1024]{1,0:T(8,128)(2,1)}, bf16[256,1024]{1,0:T(8,128)(2,1)S(1)}, u32[]{:S(2)}, u32[]{:S(2)}) collective-permute-start(bf16[256,1024]{1,0:T(8,128)(2,1)} %tokens_ref.1), channel_id=1, source_target_pairs={{0,1},{1,0},{2,3},{3,2},{4,5},{5,4},{6,7},{7,6},{8,9},{9,8},{10,11... | collective-permute-start | bytes 1572872 | tf_op jit(solution)/shard_map/ppermute | solution.py:298
  0.8 16.0 %collective-permute-start.2 = (bf16[256,1024]{1,0:T(8,128)(2,1)}, bf16[256,1024]{1,0:T(8,128)(2,1)S(1)}, u32[]{:S(2)}, u32[]{:S(2)}) collective-permute-start(bf16[256,1024]{1,0:T(8,128)(2,1)} %upstream_ref.1), channel_id=1, source_target_pairs={{0,1},{1,0},{2,3},{3,2},{4,5},{5,4},{6,7},{7,6},{8,9},{9,8},{10,11... | collective-permute-start | bytes 1572872 | tf_op jit(solution)/shard_map/ppermute | solution.py:298
  1.2 15.5 %copy-start.1 = (bf16[256,1024]{1,0:T(8,128)(2,1)S(1)}, bf16[256,1024]{1,0:T(8,128)(2,1)}, u32[]{:S(2)}) copy-start(bf16[256,1024]{1,0:T(8,128)(2,1)} %upstream_ref.1) | copy-start | bytes 1572868
  1.4 15.4 %copy-start = (bf16[256,1024]{1,0:T(8,128)(2,1)S(1)}, bf16[256,1024]{1,0:T(8,128)(2,1)}, u32[]{:S(2)}) copy-start(bf16[256,1024]{1,0:T(8,128)(2,1)} %tokens_ref.1) | copy-start | bytes 1572868
  14.5 3.3 %collective-permute-start = (bf16[8,8,1536]{2,1,0:T(8,128)(2,1)S(1)}, bf16[8,8,1536]{2,1,0:T(8,128)(2,1)S(1)}, u32[]{:S(2)}, u32[]{:S(2)}) collective-permute-start(bf16[8,8,1536]{2,1,0:T(8,128)(2,1)S(1)} %all_to_all.5.slots_ref.refs_0_), channel_id=1, source_target_pairs={{0,1},{1,0},{2,3},{3,2},{4,5},{5,4},{6,7},{7,6},{8,9},{9,8},{10,11... | collective-permute-start | bytes 589832 | tf_op jit(solution)/shard_map/ppermute | solution.py:304
  18.8 4.5 %collective-permute-start.3 = (bf16[2,8,2176]{2,1,0:T(8,128)(2,1)S(1)}, bf16[2,8,2176]{2,1,0:T(8,128)(2,1)S(1)}, u32[]{:S(2)}, u32[]{:S(2)}) collective-permute-start(bf16[2,8,2176]{2,1,0:T(8,128)(2,1)S(1)} %get-tuple-element.31), channel_id=1, source_target_pairs={{0,3},{1,2},{2,1},{3,0},{4,7},{5,6},{6,5},{7,4},{8,11},{9,10},{10,... | collective-permute-start | bytes 208904 | tf_op jit(solution)/shard_map/ppermute | solution.py:288
  19.8 4.7 %collective-permute-start.4 = (bf16[2,8,2176]{2,1,0:T(8,128)(2,1)S(1)}, bf16[2,8,2176]{2,1,0:T(8,128)(2,1)S(1)}, u32[]{:S(2)}, u32[]{:S(2)}) collective-permute-start(bf16[2,8,2176]{2,1,0:T(8,128)(2,1)S(1)} %get-tuple-element.32), channel_id=1, source_target_pairs={{0,5},{1,4},{2,7},{3,6},{4,1},{5,0},{6,3},{7,2},{8,13},{9,12},{10,... | collective-permute-start | bytes 208904 | tf_op jit(solution)/shard_map/ppermute | solution.py:288
  20.0 5.7 %collective-permute-start.5 = (bf16[2,8,2176]{2,1,0:T(8,128)(2,1)S(1)}, bf16[2,8,2176]{2,1,0:T(8,128)(2,1)S(1)}, u32[]{:S(2)}, u32[]{:S(2)}) collective-permute-start(bf16[2,8,2176]{2,1,0:T(8,128)(2,1)S(1)} %get-tuple-element.33), channel_id=1, source_target_pairs={{0,7},{1,6},{2,5},{3,4},{4,3},{5,2},{6,1},{7,0},{8,15},{9,14},{10,... | collective-permute-start | bytes 208904 | tf_op jit(solution)/shard_map/ppermute | solution.py:288
  26.0 5.1 %collective-permute-start.6 = (bf16[1,8,2176]{2,1,0:T(8,128)(2,1)S(1)}, bf16[1,8,2176]{2,1,0:T(8,128)(2,1)S(1)}, u32[]{:S(2)}, u32[]{:S(2)}) collective-permute-start(bf16[1,8,2176]{2,1,0:T(8,128)(2,1)S(1)} %merge.1), channel_id=1, source_target_pairs={{0,9},{1,8},{2,11},{3,10},{4,13},{5,12},{6,15},{7,14},{8,1},{9,0},... | collective-permute-start | bytes 104456 | tf_op jit(solution)/shard_map/ppermute | solution.py:288

commit v6 on v5

--- a/solution.py
+++ b/solution.py
@@ -36,6 +36,14 @@
     return high, (value - high).astype(BF16).astype(F32)
 
 
+def receiver(me, fours, step, four):
+    return lax.bitwise_xor(me, step + 4 * four) if fours == 2 else 4 * four + lax.bitwise_xor(lax.rem(me, 4), step)
+
+
+def crosses(fours, step, four):
+    return (step > 0) != (fours == 2 and four > 0)
+
+
 def seed_kernel(seed_ref):
     seed_ref[...] = jnp.zeros_like(seed_ref)
 
@@ -59,7 +67,29 @@
         chunks_ref[dest, :, half:] = right
 
 
-def products(slots_ref, tokens_ref, tokens_far_ref, upstream_ref, upstream_far_ref, side):
+def pair_kernel(mine_ref, taken_ref, pair_ref):
+    pair_ref[0:1] = mine_ref[...]
+    pair_ref[1:2] = taken_ref[...]
+
+
+def order_kernel(*refs):
+    me = lax.axis_index("seq")
+    *piece_refs, slots_ref = refs
+    for step, piece_ref in enumerate(piece_refs):
+        for four in range(2):
+            slots_ref[receiver(me, 2, step, four)] = piece_ref[four]
+
+
+def owner(chip, seq):
+    side = lax.axis_index("exp")
+    if seq != 8:
+        return side
+    path = lax.bitwise_xor(chip, lax.axis_index("seq"))
+    return lax.rem(side + (lax.rem(path, 4) > 0).astype(jnp.int32) + path // 4, 2)
+
+
+def products(slots_ref, tokens_ref, tokens_far_ref, upstream_ref, upstream_far_ref, cores):
+    side = lax.axis_index("exp")
     seq, _, width = slots_ref.shape
     half = tokens_ref.shape[0]
     quarter = half // 2
@@ -72,40 +102,35 @@
         for i in range(2)
     ]
     row = lax.broadcasted_iota(jnp.int32, (8, near.shape[1]), 0)
-    ours = row // 2 % 2 == side
     blocks = []
     for chip in range(0, seq, 2):
         parts = []
-        for at in (8 * chip, 8 * chip + 8):
-            one, two, three, four = (block[at : at + 8] for block in by_quarter)
+        for core, at in ((cores[chip], 8 * chip), (cores[chip + 1], 8 * chip + 8)):
+            direct = core == side
+            one, two, three, four, same, cross = (block[at : at + 8] for block in (*by_quarter, near, far))
+            one, three = jnp.where(direct, one, three), jnp.where(direct, three, one)
+            two, four = jnp.where(direct, two, four), jnp.where(direct, four, two)
+            same, cross = jnp.where(direct, same, cross), jnp.where(direct, cross, same)
             comb = jnp.where(row < 4, jnp.where(row < 2, one, two), jnp.where(row < 6, three, four))
-            disp = jnp.where(row < 4, 0.0, jnp.where(row < 6, near[at : at + 8], far[at : at + 8]))
+            disp = jnp.where(row < 4, 0.0, jnp.where(row < 6, same, cross))
             comb, disp = comb + pltpu.roll(comb, 4, 0), disp + pltpu.roll(disp, 4, 0)
             comb, disp = comb + pltpu.roll(comb, 2, 0), disp + pltpu.roll(disp, 2, 0)
-            parts.append((near[at : at + 8], comb, disp))
+            ours = row // 2 % 2 == core
+            parts.append((same, jnp.where(ours, comb, 0.0), jnp.where(ours, disp, 0.0)))
         (even, even_comb, even_disp), (odd, odd_comb, odd_disp) = parts
         logits = jnp.where(row < 4, even, pltpu.roll(odd, 4, 0))
-        comb = jnp.where(ours, jnp.where(row < 4, even_comb, odd_comb), 0.0)
-        disp = jnp.where(ours, jnp.where(row < 4, even_disp, odd_disp), 0.0)
-        blocks.append((logits, comb, disp))
+        blocks.append((logits, jnp.where(row < 4, even_comb, odd_comb), jnp.where(row < 4, even_disp, odd_disp)))
     return [jnp.concatenate(parts, axis=0) for parts in zip(*blocks)]
 
 
 def near_kernel(slots_ref, *refs):
-    side = lax.axis_index("exp")
     inputs, turned, part_refs = refs[:4], refs[4:8], refs[8:]
+    seq = slots_ref.shape[0]
     for source, target in zip(inputs, turned):
         target[...] = source[...].T
-    for ref, part in zip(part_refs, products(slots_ref, *turned, side)):
+    cores = [owner(chip, seq) for chip in range(seq)]
+    for ref, part in zip(part_refs, products(slots_ref, *turned, cores)):
         ref[...] = part
-
-
-def receiver(me, fours, step, four):
-    return lax.bitwise_xor(me, step + 4 * four) if fours == 2 else 4 * four + lax.bitwise_xor(lax.rem(me, 4), step)
-
-
-def crosses(fours, step, four):
-    return (step > 0) != (fours == 2 and four > 0)
 
 
 def local_kernel(
@@ -121,7 +146,7 @@
     half = tokens_ref.shape[1]
     extra = width - 2 * half
     groups = n_slots // 8 + 1
-    parts = products(slots_ref, turned[1], turned[0], turned[3], turned[2], 1 - side)
+    parts = products(slots_ref, *turned, [1 - owner(chip, seq) for chip in range(seq)])
     logits, d_comb, d_disp = (ref[...] + part for ref, part in zip((logit_ref, comb_ref, disp_ref), parts))
     row_exp = jnp.exp(logits - jnp.max(logits, axis=0, keepdims=True))
     combine = row_exp / jnp.sum(row_exp, axis=0, keepdims=True)
@@ -252,9 +277,10 @@
         second = jnp.where(side == 0, pltpu.roll(dispatch, 6, 0), dispatch)
         for j in range(2):
             span = slice(16 * group + 8 * j, 16 * group + 8 * j + 8)
+            ahead = lax.rem(owner(2 * group + j, seq) + side, 2)
             ours, theirs = first[4 * j : 4 * j + 2], second[4 * j : 4 * j + 2]
-            rows_ref[0, span, :] = jnp.concatenate([d_logit[4 * j : 4 * j + 4], ours, zero[0:2]], axis=0)
-            rows_ref[1, span, :] = jnp.concatenate([zero, theirs], axis=0)
+            rows_ref[ahead, span, :] = jnp.concatenate([d_logit[4 * j : 4 * j + 4], ours, zero[0:2]], axis=0)
+            rows_ref[1 - ahead, span, :] = jnp.concatenate([zero, theirs], axis=0)
     left = rows_ref[...].reshape(16 * seq, -1).astype(BF16)
     right = jnp.concatenate([ref[:, :, :half].reshape(8 * seq, half) for ref in (slots_ref, other_ref)], axis=0)
     patches = tokens_ref.shape[0] // 2
@@ -297,17 +323,24 @@
 
     tokens_far, far = (lax.ppermute(x, "exp", cores) for x in (tokens, upstream))
     seed = call(seed_kernel, sds((8, 128), F32), "seed", seq, cost_estimate=LONG)()
-    chunks = call(pack_kernel, sds((seq, 8, half + half // 2), BF16), "pack", seq)(
+    fours = seq // 4
+    rows = (8, half + half // 2)
+    chunks = call(pack_kernel, sds((1 if fours == 2 else seq, *rows), BF16), "pack", seq)(
         seed, slot_params, slot_outputs, slot_input_grads
     )
-    slots = lax.all_to_all(chunks, "seq", split_axis=0, concat_axis=0, tiled=True)
+    if fours == 2:
+        taken = to_other_core(chunks, seq, 4)
+        pieces = [call(pair_kernel, sds((2, *rows), BF16), "pair", seq)(chunks, taken)]
+        pieces += [to_other_core(pieces[0], seq, step) for step in range(1, 4)]
+        slots = call(order_kernel, sds((seq, *rows), BF16), "order", seq)(*pieces)
+    else:
+        slots = lax.all_to_all(chunks, "seq", split_axis=0, concat_axis=0, tiled=True)
     other = lax.ppermute(slots, "exp", cores)
     by_slot = sds((n_slots, patches), F32)
     turned = sds((half, patches), BF16)
     near = call(near_kernel, (turned,) * 4 + (by_slot,) * 3, "near", seq, cost_estimate=LONG)(
         slots, tokens, tokens_far, upstream, far
     )
-    fours = seq // 4
     chunk = (8, 2 * half + extra)
     *sends, col, row, disp = call(
         local_kernel,

time: 32.6 us -> 30.5 us (0.936)
  blocking collectives: 13.1 us -> 0 us
  starting transfers between devices: 6.97 us -> 14.2 us
  waiting for transfers between devices: 8.09 us -> 11.9 us
    all_to_all x1 -> x0, blocking collectives: 13.1 us -> none  [shards(): lax.all_to_all(chunks, 'seq', split_axis=0, concat_axis=0, tiled=True)]
    ppermute x4 -> x8, starting transfers between devices: 4.18 us -> 13.2 us  [to_other_core(): return lax.ppermute(value, ('seq', 'exp'), pairs)]
    ppermute x4 -> x8, waiting for transfers between devices: 7.83 us -> 11.6 us  [to_other_core(): return lax.ppermute(value, ('seq', 'exp'), pairs)]
    ppermute x1, starting transfers between devices: 2.21 us -> 0.46 us  [shards(): other = lax.ppermute(slots, 'exp', cores)]
  transfers between devices with their start and end apart: 7 -> 11, of which waited for: 5 -> 9; matrix products, arithmetic and copies ran while one was open for 0% -> 0% of each run, Pallas kernels for 3% -> 3%
where the time goes in v6:
time: 30.5 us; the launch traced here: 30.3 us
  starting transfers between devices  14.2 us (47%)
  waiting for transfers between devices  11.9 us (39%)
  Pallas kernels  3.4 us (11%)
  between operations  0.71 us (2%)
    ppermute x8, starting transfers between devices, to_other_core(): return lax.ppermute(value, ('seq', 'exp'), pairs)  13.2 us
    ppermute x8, waiting for transfers between devices, to_other_core(): return lax.ppermute(value, ('seq', 'exp'), pairs)  11.6 us
    pallas_call x1, Pallas kernels, shards(): call(finish_kernel, (sds((4, half), F32), sds((patches, half), BF16), sds...  1.33 us
    pallas_call x1, Pallas kernels, shards(): call(local_kernel, (sds((fours, *chunk), BF16),) * 4 + (by_slot,) * 3, 'l...  0.98 us
    pallas_call x1, Pallas kernels, shards(): call(near_kernel, (turned,) * 4 + (by_slot,) * 3, 'near', seq, cost_estim...  0.8 us
  transfers between devices with their start and end apart: 11, of which 9 were waited for; matrix products, arithmetic and copies ran while one was open for 0% of the time, Pallas kernels for 3%

profile of v6, /device:TPU:1, one launch (start us, length us, event | category | flops | bytes accessed | tf_op | source)
XLA Modules:
  0.0 30.3 jit_solution(17613878747006767733)
XLA Ops:
  0.6 0.0 copy-start.4
  0.6 0.0 copy-start.3
  0.7 0.0 copy-start.2
  0.7 0.1 collective-permute-start.5
  0.8 0.5 %collective-permute-start.6 = (bf16[256,1024]{1,0:T(8,128)(2,1)}, bf16[256,1024]{1,0:T(8,128)(2,1)S(1)}, u32[]{:S(2)}, u32[]{:S(2)}) collective-permute-start(bf16[256,1024]{1,0:T(8,128)(2,1)} %upstream_ref.1), channel_id=1, source_target_pairs={{0,1},{1,0},{2,3},{3,2},{4,5},{5,4},{6,7},{7,6},{8,9},{9,8},{10,11... | collective-permute-start | bytes 1572872 | tf_op jit(solution)/shard_map/ppermute | solution.py:324
  1.2 0.0 copy-start.1
  1.2 0.1 copy-done.4
  1.3 0.0 copy-done.3
  1.3 0.0 copy-done.2
  1.4 0.0 copy-start
  1.4 3.8 %collective-permute-start = (bf16[1,8,1536]{2,1,0:T(8,128)(2,1)S(1)}, bf16[1,8,1536]{2,1,0:T(8,128)(2,1)S(1)}, u32[]{:S(2)}, u32[]{:S(2)}) collective-permute-start(bf16[1,8,1536]{2,1,0:T(8,128)(2,1)S(1)} %pack.1.mine_ref), channel_id=1, source_target_pairs={{0,9},{1,8},{2,11},{3,10},{4,13},{5,12},{6,15},{7,14},{8,1},{9,0},... | collective-permute-start | bytes 73736 | tf_op jit(solution)/shard_map/ppermute | solution.py:314
  5.2 1.5 %collective-permute-done.taken_ref = bf16[1,8,1536]{2,1,0:T(8,128)(2,1)S(1)} collective-permute-done((bf16[1,8,1536]{2,1,0:T(8,128)(2,1)S(1)}, bf16[1,8,1536]{2,1,0:T(8,128)(2,1)S(1)}, u32[]{:S(2)}, u32[]{:S(2)}) %collective-permute-start) | collective-permute-done | bytes 24608 | tf_op jit(solution)/shard_map/ppermute | solution.py:314
  6.7 2.6 %collective-permute-start.3 = (bf16[2,8,1536]{2,1,0:T(8,128)(2,1)S(1)}, bf16[2,8,1536]{2,1,0:T(8,128)(2,1)S(1)}, u32[]{:S(2)}, u32[]{:S(2)}) collective-permute-start(bf16[2,8,1536]{2,1,0:T(8,128)(2,1)S(1)} %pair.1.refs_0_), channel_id=1, source_target_pairs={{0,7},{1,6},{2,5},{3,4},{4,3},{5,2},{6,1},{7,0},{8,15},{9,14},{10,... | collective-permute-start | bytes 147464 | tf_op jit(solution)/shard_map/ppermute | solution.py:314
  9.2 0.2 collective-permute-start.2
  9.4 0.2 collective-permute-start.1
  9.6 1.5 %collective-permute-done.3.refs_3_ = bf16[2,8,1536]{2,1,0:T(8,128)(2,1)S(1)} collective-permute-done((bf16[2,8,1536]{2,1,0:T(8,128)(2,1)S(1)}, bf16[2,8,1536]{2,1,0:T(8,128)(2,1)S(1)}, u32[]{:S(2)}, u32[]{:S(2)}) %collective-permute-start.3) | collective-permute-done | bytes 49184 | tf_op jit(solution)/shard_map/ppermute | solution.py:314
  11.1 2.0 %collective-permute-done.2.refs_2_ = bf16[2,8,1536]{2,1,0:T(8,128)(2,1)S(1)} collective-permute-done((bf16[2,8,1536]{2,1,0:T(8,128)(2,1)S(1)}, bf16[2,8,1536]{2,1,0:T(8,128)(2,1)S(1)}, u32[]{:S(2)}, u32[]{:S(2)}) %collective-permute-start.2) | collective-permute-done | bytes 49184 | tf_op jit(solution)/shard_map/ppermute | solution.py:314
  13.1 0.1 collective-permute-done.1.refs_1_
  13.2 0.5 %collective-permute-start.4 = (bf16[8,8,1536]{2,1,0:T(8,128)(2,1)S(1)}, bf16[8,8,1536]{2,1,0:T(8,128)(2,1)S(1)}, u32[]{:S(2)}, u32[]{:S(2)}) collective-permute-start(bf16[8,8,1536]{2,1,0:T(8,128)(2,1)S(1)} %order.1.slots_ref.refs_0_), channel_id=1, source_target_pairs={{0,1},{1,0},{2,3},{3,2},{4,5},{5,4},{6,7},{7,6},{8,9},{9,8},{10,11... | collective-permute-start | bytes 589832 | tf_op jit(solution)/shard_map/ppermute | solution.py:338
  13.7 0.0 collective-permute-done.5.refs_1_.tokens_far_ref
  13.7 0.0 collective-permute-done.6.refs_3_.upstream_far_ref
  13.7 0.0 copy-done.1
  13.7 0.0 copy-done
  13.7 0.8 %near.1 = (bf16[1024,256]{1,0:T(8,128)(2,1)S(1)}, bf16[1024,256]{1,0:T(8,128)(2,1)S(1)}, bf16[1024,256]{1,0:T(8,128)(2,1)S(1)}, bf16[1024,256]{1,0:T(8,128)(2,1)...) custom-call(bf16[8,8,1536]{2,1,0:T(8,128)(2,1)S(1)} %order.1.slots_ref.refs_0_, ...), custom_call_target="tpu_custom_call" | custom-call | flops 10000000000 | bytes 10000000 | tf_op jit(solution)/shard_map/near/pallas_call | solution.py:341
  14.5 0.2 collective-permute-done.4.slots_ref.refs_1_
  14.8 1.0 %local.1 = (bf16[2,8,2176]{2,1,0:T(8,128)(2,1)S(1)}, bf16[2,8,2176]{2,1,0:T(8,128)(2,1)S(1)}, bf16[2,8,2176]{2,1,0:T(8,128)(2,1)S(1)}, bf16[2,8,2176]{2,1,0:T(8,...) custom-call(bf16[8,8,1536]{2,1,0:T(8,128)(2,1)S(1)} %collective-permute-done.4.slots_ref.refs_1_,, ...), custom_call_target="tpu_custom_call" | custom-call | tf_op jit(solution)/shard_map/local/pallas_call | solution.py:345
  15.8 1.0 %collective-permute-start.7 = (bf16[2,8,2176]{2,1,0:T(8,128)(2,1)S(1)}, bf16[2,8,2176]{2,1,0:T(8,128)(2,1)S(1)}, u32[]{:S(2)}, u32[]{:S(2)}) collective-permute-start(bf16[2,8,2176]{2,1,0:T(8,128)(2,1)S(1)} %get-tuple-element.31), channel_id=1, source_target_pairs={{0,3},{1,2},{2,1},{3,0},{4,7},{5,6},{6,5},{7,4},{8,11},{9,10},{10,... | collective-permute-start | bytes 208904 | tf_op jit(solution)/shard_map/ppermute | solution.py:314
  16.8 1.3 %collective-permute-start.8 = (bf16[2,8,2176]{2,1,0:T(8,128)(2,1)S(1)}, bf16[2,8,2176]{2,1,0:T(8,128)(2,1)S(1)}, u32[]{:S(2)}, u32[]{:S(2)}) collective-permute-start(bf16[2,8,2176]{2,1,0:T(8,128)(2,1)S(1)} %get-tuple-element.32), channel_id=1, source_target_pairs={{0,5},{1,4},{2,7},{3,6},{4,1},{5,0},{6,3},{7,2},{8,13},{9,12},{10,... | collective-permute-start | bytes 208904 | tf_op jit(solution)/shard_map/ppermute | solution.py:314
  18.1 1.0 %collective-permute-start.9 = (bf16[2,8,2176]{2,1,0:T(8,128)(2,1)S(1)}, bf16[2,8,2176]{2,1,0:T(8,128)(2,1)S(1)}, u32[]{:S(2)}, u32[]{:S(2)}) collective-permute-start(bf16[2,8,2176]{2,1,0:T(8,128)(2,1)S(1)} %get-tuple-element.33), channel_id=1, source_target_pairs={{0,7},{1,6},{2,5},{3,4},{4,3},{5,2},{6,1},{7,0},{8,15},{9,14},{10,... | collective-permute-start | bytes 208904 | tf_op jit(solution)/shard_map/ppermute | solution.py:314
  19.0 1.3 %collective-permute-done.7.refs_1_.refs_6_ = bf16[2,8,2176]{2,1,0:T(8,128)(2,1)S(1)} collective-permute-done((bf16[2,8,2176]{2,1,0:T(8,128)(2,1)S(1)}, bf16[2,8,2176]{2,1,0:T(8,128)(2,1)S(1)}, u32[]{:S(2)}, u32[]{:S(2)}) %collective-permute-start.7) | collective-permute-done | bytes 69664 | tf_op jit(solution)/shard_map/ppermute | solution.py:314
  20.3 0.4 %collective-permute-done.8.refs_2_.refs_7_ = bf16[2,8,2176]{2,1,0:T(8,128)(2,1)S(1)} collective-permute-done((bf16[2,8,2176]{2,1,0:T(8,128)(2,1)S(1)}, bf16[2,8,2176]{2,1,0:T(8,128)(2,1)S(1)}, u32[]{:S(2)}, u32[]{:S(2)}) %collective-permute-start.8) | collective-permute-done | bytes 69664 | tf_op jit(solution)/shard_map/ppermute | solution.py:314
  20.7 2.4 %collective-permute-done.9.refs_3_.refs_8_ = bf16[2,8,2176]{2,1,0:T(8,128)(2,1)S(1)} collective-permute-done((bf16[2,8,2176]{2,1,0:T(8,128)(2,1)S(1)}, bf16[2,8,2176]{2,1,0:T(8,128)(2,1)S(1)}, u32[]{:S(2)}, u32[]{:S(2)}) %collective-permute-start.9) | collective-permute-done | bytes 69664 | tf_op jit(solution)/shard_map/ppermute | solution.py:314
  23.1 0.2 merge.1
  23.4 3.3 %collective-permute-start.10 = (bf16[1,8,2176]{2,1,0:T(8,128)(2,1)S(1)}, bf16[1,8,2176]{2,1,0:T(8,128)(2,1)S(1)}, u32[]{:S(2)}, u32[]{:S(2)}) collective-permute-start(bf16[1,8,2176]{2,1,0:T(8,128)(2,1)S(1)} %merge.1), channel_id=1, source_target_pairs={{0,9},{1,8},{2,11},{3,10},{4,13},{5,12},{6,15},{7,14},{8,1},{9,0},... | collective-permute-start | bytes 104456 | tf_op jit(solution)/shard_map/ppermute | solution.py:314
  26.6 2.4 %collective-permute-done.10.refs_9_ = bf16[1,8,2176]{2,1,0:T(8,128)(2,1)S(1)} collective-permute-done((bf16[1,8,2176]{2,1,0:T(8,128)(2,1)S(1)}, bf16[1,8,2176]{2,1,0:T(8,128)(2,1)S(1)}, u32[]{:S(2)}, u32[]{:S(2)}) %collective-permute-start.10) | collective-permute-done | bytes 34848 | tf_op jit(solution)/shard_map/ppermute | solution.py:314
  29.0 1.3 %finish.1 = (f32[4,1024]{1,0:T(4,128)}, bf16[256,1024]{1,0:T(8,128)(2,1)}, f32[2,2048]{1,0:T(2,128)}) custom-call(bf16[8,8,1536]{2,1,0:T(8,128)(2,1)S(1)} %order.1.slots_ref.refs_0_, bf16[8,8,1536]{2,1,0:T(8,128)(2,1)S(1)} %collective-permute-done.4.slots_ref.refs_1_, f32[32,256]{1,0:T(8,128)S(1)} %get-tuple-element.27.refs_2_, ...), custom_call_target="tpu_custom_call" | custom-call | tf_op jit(solution)/shard_map/finish/pallas_call | solution.py:366
  (4 shorter events, 0.0 us)
Async XLA Ops:
  0.6 0.7 %copy-start.4 = (bf16[2,2048]{1,0:T(2,128)(2,1)S(1)}, bf16[2,2048]{1,0:T(2,128)(2,1)}, u32[]{:S(2)}) copy-start(bf16[2,2048]{1,0:T(2,128)(2,1)} %grads_ref.1) | copy-start | bytes 24580
  0.6 0.7 %copy-start.3 = (bf16[2,2048]{1,0:T(2,128)(2,1)S(1)}, bf16[2,2048]{1,0:T(2,128)(2,1)}, u32[]{:S(2)}) copy-start(bf16[2,2048]{1,0:T(2,128)(2,1)} %outs_ref.1) | copy-start | bytes 24580
  0.7 0.7 %copy-start.2 = (bf16[4,1024]{1,0:T(4,128)(2,1)S(1)}, bf16[4,1024]{1,0:T(4,128)(2,1)}, u32[]{:S(2)}) copy-start(bf16[4,1024]{1,0:T(4,128)(2,1)} %params_ref.1) | copy-start | bytes 24580
  0.7 13.1 %collective-permute-start.5 = (bf16[256,1024]{1,0:T(8,128)(2,1)}, bf16[256,1024]{1,0:T(8,128)(2,1)S(1)}, u32[]{:S(2)}, u32[]{:S(2)}) collective-permute-start(bf16[256,1024]{1,0:T(8,128)(2,1)} %tokens_ref.1), channel_id=1, source_target_pairs={{0,1},{1,0},{2,3},{3,2},{4,5},{5,4},{6,7},{7,6},{8,9},{9,8},{10,11... | collective-permute-start | bytes 1572872 | tf_op jit(solution)/shard_map/ppermute | solution.py:324
  0.8 12.9 %collective-permute-start.6 = (bf16[256,1024]{1,0:T(8,128)(2,1)}, bf16[256,1024]{1,0:T(8,128)(2,1)S(1)}, u32[]{:S(2)}, u32[]{:S(2)}) collective-permute-start(bf16[256,1024]{1,0:T(8,128)(2,1)} %upstream_ref.1), channel_id=1, source_target_pairs={{0,1},{1,0},{2,3},{3,2},{4,5},{5,4},{6,7},{7,6},{8,9},{9,8},{10,11... | collective-permute-start | bytes 1572872 | tf_op jit(solution)/shard_map/ppermute | solution.py:324
  1.2 12.5 %copy-start.1 = (bf16[256,1024]{1,0:T(8,128)(2,1)S(1)}, bf16[256,1024]{1,0:T(8,128)(2,1)}, u32[]{:S(2)}) copy-start(bf16[256,1024]{1,0:T(8,128)(2,1)} %upstream_ref.1) | copy-start | bytes 1572868
  1.4 12.4 %copy-start = (bf16[256,1024]{1,0:T(8,128)(2,1)S(1)}, bf16[256,1024]{1,0:T(8,128)(2,1)}, u32[]{:S(2)}) copy-start(bf16[256,1024]{1,0:T(8,128)(2,1)} %tokens_ref.1) | copy-start | bytes 1572868
  1.4 5.3 %collective-permute-start = (bf16[1,8,1536]{2,1,0:T(8,128)(2,1)S(1)}, bf16[1,8,1536]{2,1,0:T(8,128)(2,1)S(1)}, u32[]{:S(2)}, u32[]{:S(2)}) collective-permute-start(bf16[1,8,1536]{2,1,0:T(8,128)(2,1)S(1)} %pack.1.mine_ref), channel_id=1, source_target_pairs={{0,9},{1,8},{2,11},{3,10},{4,13},{5,12},{6,15},{7,14},{8,1},{9,0},... | collective-permute-start | bytes 73736 | tf_op jit(solution)/shard_map/ppermute | solution.py:314
  6.7 4.4 %collective-permute-start.3 = (bf16[2,8,1536]{2,1,0:T(8,128)(2,1)S(1)}, bf16[2,8,1536]{2,1,0:T(8,128)(2,1)S(1)}, u32[]{:S(2)}, u32[]{:S(2)}) collective-permute-start(bf16[2,8,1536]{2,1,0:T(8,128)(2,1)S(1)} %pair.1.refs_0_), channel_id=1, source_target_pairs={{0,7},{1,6},{2,5},{3,4},{4,3},{5,2},{6,1},{7,0},{8,15},{9,14},{10,... | collective-permute-start | bytes 147464 | tf_op jit(solution)/shard_map/ppermute | solution.py:314
  9.2 3.8 %collective-permute-start.2 = (bf16[2,8,1536]{2,1,0:T(8,128)(2,1)S(1)}, bf16[2,8,1536]{2,1,0:T(8,128)(2,1)S(1)}, u32[]{:S(2)}, u32[]{:S(2)}) collective-permute-start(bf16[2,8,1536]{2,1,0:T(8,128)(2,1)S(1)} %pair.1.refs_0_), channel_id=1, source_target_pairs={{0,5},{1,4},{2,7},{3,6},{4,1},{5,0},{6,3},{7,2},{8,13},{9,12},{10,... | collective-permute-start | bytes 147464 | tf_op jit(solution)/shard_map/ppermute | solution.py:314
  9.4 3.8 %collective-permute-start.1 = (bf16[2,8,1536]{2,1,0:T(8,128)(2,1)S(1)}, bf16[2,8,1536]{2,1,0:T(8,128)(2,1)S(1)}, u32[]{:S(2)}, u32[]{:S(2)}) collective-permute-start(bf16[2,8,1536]{2,1,0:T(8,128)(2,1)S(1)} %pair.1.refs_0_), channel_id=1, source_target_pairs={{0,3},{1,2},{2,1},{3,0},{4,7},{5,6},{6,5},{7,4},{8,11},{9,10},{10,... | collective-permute-start | bytes 147464 | tf_op jit(solution)/shard_map/ppermute | solution.py:314
  13.2 1.5 %collective-permute-start.4 = (bf16[8,8,1536]{2,1,0:T(8,128)(2,1)S(1)}, bf16[8,8,1536]{2,1,0:T(8,128)(2,1)S(1)}, u32[]{:S(2)}, u32[]{:S(2)}) collective-permute-start(bf16[8,8,1536]{2,1,0:T(8,128)(2,1)S(1)} %order.1.slots_ref.refs_0_), channel_id=1, source_target_pairs={{0,1},{1,0},{2,3},{3,2},{4,5},{5,4},{6,7},{7,6},{8,9},{9,8},{10,11... | collective-permute-start | bytes 589832 | tf_op jit(solution)/shard_map/ppermute | solution.py:338
  15.8 4.5 %collective-permute-start.7 = (bf16[2,8,2176]{2,1,0:T(8,128)(2,1)S(1)}, bf16[2,8,2176]{2,1,0:T(8,128)(2,1)S(1)}, u32[]{:S(2)}, u32[]{:S(2)}) collective-permute-start(bf16[2,8,2176]{2,1,0:T(8,128)(2,1)S(1)} %get-tuple-element.31), channel_id=1, source_target_pairs={{0,3},{1,2},{2,1},{3,0},{4,7},{5,6},{6,5},{7,4},{8,11},{9,10},{10,... | collective-permute-start | bytes 208904 | tf_op jit(solution)/shard_map/ppermute | solution.py:314
  16.8 3.9 %collective-permute-start.8 = (bf16[2,8,2176]{2,1,0:T(8,128)(2,1)S(1)}, bf16[2,8,2176]{2,1,0:T(8,128)(2,1)S(1)}, u32[]{:S(2)}, u32[]{:S(2)}) collective-permute-start(bf16[2,8,2176]{2,1,0:T(8,128)(2,1)S(1)} %get-tuple-element.32), channel_id=1, source_target_pairs={{0,5},{1,4},{2,7},{3,6},{4,1},{5,0},{6,3},{7,2},{8,13},{9,12},{10,... | collective-permute-start | bytes 208904 | tf_op jit(solution)/shard_map/ppermute | solution.py:314
  18.1 5.0 %collective-permute-start.9 = (bf16[2,8,2176]{2,1,0:T(8,128)(2,1)S(1)}, bf16[2,8,2176]{2,1,0:T(8,128)(2,1)S(1)}, u32[]{:S(2)}, u32[]{:S(2)}) collective-permute-start(bf16[2,8,2176]{2,1,0:T(8,128)(2,1)S(1)} %get-tuple-element.33), channel_id=1, source_target_pairs={{0,7},{1,6},{2,5},{3,4},{4,3},{5,2},{6,1},{7,0},{8,15},{9,14},{10,... | collective-permute-start | bytes 208904 | tf_op jit(solution)/shard_map/ppermute | solution.py:314
  23.4 5.6 %collective-permute-start.10 = (bf16[1,8,2176]{2,1,0:T(8,128)(2,1)S(1)}, bf16[1,8,2176]{2,1,0:T(8,128)(2,1)S(1)}, u32[]{:S(2)}, u32[]{:S(2)}) collective-permute-start(bf16[1,8,2176]{2,1,0:T(8,128)(2,1)S(1)} %merge.1), channel_id=1, source_target_pairs={{0,9},{1,8},{2,11},{3,10},{4,13},{5,12},{6,15},{7,14},{8,1},{9,0},... | collective-permute-start | bytes 104456 | tf_op jit(solution)/shard_map/ppermute | solution.py:314

commit v7 on v6

--- a/solution.py
+++ b/solution.py
@@ -351,7 +351,7 @@
         + [pltpu.VMEM((seq, 8, extra), F32)]
         + [pltpu.VMEM((3, seq, 8, patches), F32)] * 2,
     )(other, tokens, tokens_far, upstream, far, *near)
-    got = [sends[0]] + [to_other_core(sends[step], seq, step) for step in range(1, 4)]
+    got = [sends[0]] + [to_other_core(sends[step], seq, step) for step in (3, 2, 1)]
     merged = call(
         functools.partial(merge_kernel, groups=n_slots // 8 + 1, half=half),
         sds((1 if fours == 2 else fours, *chunk), BF16),

time: 30.5 us -> 29.1 us (0.954)
  the two profiles are of different devices: /device:TPU:1 before, /device:TPU:0 now
where the time goes in v7:
time: 29.1 us; the launch traced here: 28.9 us
  starting transfers between devices  13 us (45%)
  waiting for transfers between devices  11.7 us (40%)
  Pallas kernels  3.4 us (12%)
  between operations  0.71 us (2%)
    ppermute x8, starting transfers between devices, to_other_core(): return lax.ppermute(value, ('seq', 'exp'), pairs)  12.2 us
    ppermute x8, waiting for transfers between devices, to_other_core(): return lax.ppermute(value, ('seq', 'exp'), pairs)  11.1 us
    pallas_call x1, Pallas kernels, shards(): call(finish_kernel, (sds((4, half), F32), sds((patches, half), BF16), sds...  1.33 us
    pallas_call x1, Pallas kernels, shards(): call(local_kernel, (sds((fours, *chunk), BF16),) * 4 + (by_slot,) * 3, 'l...  0.99 us
    pallas_call x1, Pallas kernels, shards(): call(near_kernel, (turned,) * 4 + (by_slot,) * 3, 'near', seq, cost_estim...  0.8 us
    ppermute x2, starting transfers between devices, shards(): lax.ppermute(x, 'exp', cores)  0.6 us
  transfers between devices with their start and end apart: 11, of which 9 were waited for; matrix products, arithmetic and copies ran while one was open for 0% of the time, Pallas kernels for 3%

profile of v7, /device:TPU:0, one launch (start us, length us, event | category | flops | bytes accessed | tf_op | source)
XLA Modules:
  0.0 28.9 jit_solution(5577459003241491043)
XLA Ops:
  0.6 0.0 copy-start.4
  0.6 0.0 copy-start.3
  0.7 0.0 copy-start.2
  0.7 0.5 %collective-permute-start.5 = (bf16[256,1024]{1,0:T(8,128)(2,1)}, bf16[256,1024]{1,0:T(8,128)(2,1)S(1)}, u32[]{:S(2)}, u32[]{:S(2)}) collective-permute-start(bf16[256,1024]{1,0:T(8,128)(2,1)} %tokens_ref.1), channel_id=1, source_target_pairs={{0,1},{1,0},{2,3},{3,2},{4,5},{5,4},{6,7},{7,6},{8,9},{9,8},{10,11... | collective-permute-start | bytes 1572872 | tf_op jit(solution)/shard_map/ppermute | solution.py:324
  1.2 0.1 collective-permute-start.6
  1.3 0.0 copy-start.1
  1.3 0.1 copy-done.4
  1.3 0.0 copy-done.3
  1.3 0.0 copy-done.2
  1.4 0.0 copy-start
  1.4 3.7 %collective-permute-start = (bf16[1,8,1536]{2,1,0:T(8,128)(2,1)S(1)}, bf16[1,8,1536]{2,1,0:T(8,128)(2,1)S(1)}, u32[]{:S(2)}, u32[]{:S(2)}) collective-permute-start(bf16[1,8,1536]{2,1,0:T(8,128)(2,1)S(1)} %pack.1.mine_ref), channel_id=1, source_target_pairs={{0,9},{1,8},{2,11},{3,10},{4,13},{5,12},{6,15},{7,14},{8,1},{9,0},... | collective-permute-start | bytes 73736 | tf_op jit(solution)/shard_map/ppermute | solution.py:314
  5.1 1.5 %collective-permute-done.taken_ref = bf16[1,8,1536]{2,1,0:T(8,128)(2,1)S(1)} collective-permute-done((bf16[1,8,1536]{2,1,0:T(8,128)(2,1)S(1)}, bf16[1,8,1536]{2,1,0:T(8,128)(2,1)S(1)}, u32[]{:S(2)}, u32[]{:S(2)}) %collective-permute-start) | collective-permute-done | bytes 24608 | tf_op jit(solution)/shard_map/ppermute | solution.py:314
  6.6 2.7 %collective-permute-start.3 = (bf16[2,8,1536]{2,1,0:T(8,128)(2,1)S(1)}, bf16[2,8,1536]{2,1,0:T(8,128)(2,1)S(1)}, u32[]{:S(2)}, u32[]{:S(2)}) collective-permute-start(bf16[2,8,1536]{2,1,0:T(8,128)(2,1)S(1)} %pair.1.refs_0_), channel_id=1, source_target_pairs={{0,7},{1,6},{2,5},{3,4},{4,3},{5,2},{6,1},{7,0},{8,15},{9,14},{10,... | collective-permute-start | bytes 147464 | tf_op jit(solution)/shard_map/ppermute | solution.py:314
  9.3 0.5 %collective-permute-start.2 = (bf16[2,8,1536]{2,1,0:T(8,128)(2,1)S(1)}, bf16[2,8,1536]{2,1,0:T(8,128)(2,1)S(1)}, u32[]{:S(2)}, u32[]{:S(2)}) collective-permute-start(bf16[2,8,1536]{2,1,0:T(8,128)(2,1)S(1)} %pair.1.refs_0_), channel_id=1, source_target_pairs={{0,5},{1,4},{2,7},{3,6},{4,1},{5,0},{6,3},{7,2},{8,13},{9,12},{10,... | collective-permute-start | bytes 147464 | tf_op jit(solution)/shard_map/ppermute | solution.py:314
  9.8 0.2 collective-permute-start.1
  10.0 1.5 %collective-permute-done.3.refs_3_ = bf16[2,8,1536]{2,1,0:T(8,128)(2,1)S(1)} collective-permute-done((bf16[2,8,1536]{2,1,0:T(8,128)(2,1)S(1)}, bf16[2,8,1536]{2,1,0:T(8,128)(2,1)S(1)}, u32[]{:S(2)}, u32[]{:S(2)}) %collective-permute-start.3) | collective-permute-done | bytes 49184 | tf_op jit(solution)/shard_map/ppermute | solution.py:314
  11.4 1.4 %collective-permute-done.2.refs_2_ = bf16[2,8,1536]{2,1,0:T(8,128)(2,1)S(1)} collective-permute-done((bf16[2,8,1536]{2,1,0:T(8,128)(2,1)S(1)}, bf16[2,8,1536]{2,1,0:T(8,128)(2,1)S(1)}, u32[]{:S(2)}, u32[]{:S(2)}) %collective-permute-start.2) | collective-permute-done | bytes 49184 | tf_op jit(solution)/shard_map/ppermute | solution.py:314
  12.8 0.7 %collective-permute-done.1.refs_1_ = bf16[2,8,1536]{2,1,0:T(8,128)(2,1)S(1)} collective-permute-done((bf16[2,8,1536]{2,1,0:T(8,128)(2,1)S(1)}, bf16[2,8,1536]{2,1,0:T(8,128)(2,1)S(1)}, u32[]{:S(2)}, u32[]{:S(2)}) %collective-permute-start.1) | collective-permute-done | bytes 49184 | tf_op jit(solution)/shard_map/ppermute | solution.py:314
  13.6 0.2 collective-permute-start.4
  13.8 0.0 collective-permute-done.5.refs_1_.tokens_far_ref
  13.8 0.0 collective-permute-done.6.refs_3_.upstream_far_ref
  13.8 0.0 copy-done.1
  13.8 0.0 copy-done
  13.8 0.8 %near.1 = (bf16[1024,256]{1,0:T(8,128)(2,1)S(1)}, bf16[1024,256]{1,0:T(8,128)(2,1)S(1)}, bf16[1024,256]{1,0:T(8,128)(2,1)S(1)}, bf16[1024,256]{1,0:T(8,128)(2,1)...) custom-call(bf16[8,8,1536]{2,1,0:T(8,128)(2,1)S(1)} %order.1.slots_ref.refs_0_, ...), custom_call_target="tpu_custom_call" | custom-call | flops 10000000000 | bytes 10000000 | tf_op jit(solution)/shard_map/near/pallas_call | solution.py:341
  14.6 0.5 %collective-permute-done.4.slots_ref.refs_1_ = bf16[8,8,1536]{2,1,0:T(8,128)(2,1)S(1)} collective-permute-done((bf16[8,8,1536]{2,1,0:T(8,128)(2,1)S(1)}, bf16[8,8,1536]{2,1,0:T(8,128)(2,1)S(1)}, u32[]{:S(2)}, u32[]{:S(2)}) %collective-permute-start.4) | collective-permute-done | bytes 196640 | tf_op jit(solution)/shard_map/ppermute | solution.py:338
  15.1 1.0 %local.1 = (bf16[2,8,2176]{2,1,0:T(8,128)(2,1)S(1)}, bf16[2,8,2176]{2,1,0:T(8,128)(2,1)S(1)}, bf16[2,8,2176]{2,1,0:T(8,128)(2,1)S(1)}, bf16[2,8,2176]{2,1,0:T(8,...) custom-call(bf16[8,8,1536]{2,1,0:T(8,128)(2,1)S(1)} %collective-permute-done.4.slots_ref.refs_1_,, ...), custom_call_target="tpu_custom_call" | custom-call | tf_op jit(solution)/shard_map/local/pallas_call | solution.py:345
  16.1 1.7 %collective-permute-start.7 = (bf16[2,8,2176]{2,1,0:T(8,128)(2,1)S(1)}, bf16[2,8,2176]{2,1,0:T(8,128)(2,1)S(1)}, u32[]{:S(2)}, u32[]{:S(2)}) collective-permute-start(bf16[2,8,2176]{2,1,0:T(8,128)(2,1)S(1)} %get-tuple-element.31), channel_id=1, source_target_pairs={{0,7},{1,6},{2,5},{3,4},{4,3},{5,2},{6,1},{7,0},{8,15},{9,14},{10,... | collective-permute-start | bytes 208904 | tf_op jit(solution)/shard_map/ppermute | solution.py:314
  17.8 0.4 %collective-permute-start.8 = (bf16[2,8,2176]{2,1,0:T(8,128)(2,1)S(1)}, bf16[2,8,2176]{2,1,0:T(8,128)(2,1)S(1)}, u32[]{:S(2)}, u32[]{:S(2)}) collective-permute-start(bf16[2,8,2176]{2,1,0:T(8,128)(2,1)S(1)} %get-tuple-element.32), channel_id=1, source_target_pairs={{0,5},{1,4},{2,7},{3,6},{4,1},{5,0},{6,3},{7,2},{8,13},{9,12},{10,... | collective-permute-start | bytes 208904 | tf_op jit(solution)/shard_map/ppermute | solution.py:314
  18.3 0.8 %collective-permute-start.9 = (bf16[2,8,2176]{2,1,0:T(8,128)(2,1)S(1)}, bf16[2,8,2176]{2,1,0:T(8,128)(2,1)S(1)}, u32[]{:S(2)}, u32[]{:S(2)}) collective-permute-start(bf16[2,8,2176]{2,1,0:T(8,128)(2,1)S(1)} %get-tuple-element.33), channel_id=1, source_target_pairs={{0,3},{1,2},{2,1},{3,0},{4,7},{5,6},{6,5},{7,4},{8,11},{9,10},{10,... | collective-permute-start | bytes 208904 | tf_op jit(solution)/shard_map/ppermute | solution.py:314
  19.1 2.1 %collective-permute-done.7.refs_1_.refs_6_ = bf16[2,8,2176]{2,1,0:T(8,128)(2,1)S(1)} collective-permute-done((bf16[2,8,2176]{2,1,0:T(8,128)(2,1)S(1)}, bf16[2,8,2176]{2,1,0:T(8,128)(2,1)S(1)}, u32[]{:S(2)}, u32[]{:S(2)}) %collective-permute-start.7) | collective-permute-done | bytes 69664 | tf_op jit(solution)/shard_map/ppermute | solution.py:314
  21.2 1.0 %collective-permute-done.8.refs_2_.refs_7_ = bf16[2,8,2176]{2,1,0:T(8,128)(2,1)S(1)} collective-permute-done((bf16[2,8,2176]{2,1,0:T(8,128)(2,1)S(1)}, bf16[2,8,2176]{2,1,0:T(8,128)(2,1)S(1)}, u32[]{:S(2)}, u32[]{:S(2)}) %collective-permute-start.8) | collective-permute-done | bytes 69664 | tf_op jit(solution)/shard_map/ppermute | solution.py:314
  22.2 0.7 %collective-permute-done.9.refs_3_.refs_8_ = bf16[2,8,2176]{2,1,0:T(8,128)(2,1)S(1)} collective-permute-done((bf16[2,8,2176]{2,1,0:T(8,128)(2,1)S(1)}, bf16[2,8,2176]{2,1,0:T(8,128)(2,1)S(1)}, u32[]{:S(2)}, u32[]{:S(2)}) %collective-permute-start.9) | collective-permute-done | bytes 69664 | tf_op jit(solution)/shard_map/ppermute | solution.py:314
  22.9 0.2 merge.1
  23.2 2.2 %collective-permute-start.10 = (bf16[1,8,2176]{2,1,0:T(8,128)(2,1)S(1)}, bf16[1,8,2176]{2,1,0:T(8,128)(2,1)S(1)}, u32[]{:S(2)}, u32[]{:S(2)}) collective-permute-start(bf16[1,8,2176]{2,1,0:T(8,128)(2,1)S(1)} %merge.1), channel_id=1, source_target_pairs={{0,9},{1,8},{2,11},{3,10},{4,13},{5,12},{6,15},{7,14},{8,1},{9,0},... | collective-permute-start | bytes 104456 | tf_op jit(solution)/shard_map/ppermute | solution.py:314
  25.3 2.2 %collective-permute-done.10.refs_9_ = bf16[1,8,2176]{2,1,0:T(8,128)(2,1)S(1)} collective-permute-done((bf16[1,8,2176]{2,1,0:T(8,128)(2,1)S(1)}, bf16[1,8,2176]{2,1,0:T(8,128)(2,1)S(1)}, u32[]{:S(2)}, u32[]{:S(2)}) %collective-permute-start.10) | collective-permute-done | bytes 34848 | tf_op jit(solution)/shard_map/ppermute | solution.py:314
  27.6 1.3 %finish.1 = (f32[4,1024]{1,0:T(4,128)}, bf16[256,1024]{1,0:T(8,128)(2,1)}, f32[2,2048]{1,0:T(2,128)}) custom-call(bf16[8,8,1536]{2,1,0:T(8,128)(2,1)S(1)} %order.1.slots_ref.refs_0_, bf16[8,8,1536]{2,1,0:T(8,128)(2,1)S(1)} %collective-permute-done.4.slots_ref.refs_1_, f32[32,256]{1,0:T(8,128)S(1)} %get-tuple-element.27.refs_2_, ...), custom_call_target="tpu_custom_call" | custom-call | tf_op jit(solution)/shard_map/finish/pallas_call | solution.py:366
  (4 shorter events, 0.0 us)
Async XLA Ops:
  0.6 0.7 %copy-start.4 = (bf16[2,2048]{1,0:T(2,128)(2,1)S(1)}, bf16[2,2048]{1,0:T(2,128)(2,1)}, u32[]{:S(2)}) copy-start(bf16[2,2048]{1,0:T(2,128)(2,1)} %grads_ref.1) | copy-start | bytes 24580
  0.6 0.7 %copy-start.3 = (bf16[2,2048]{1,0:T(2,128)(2,1)S(1)}, bf16[2,2048]{1,0:T(2,128)(2,1)}, u32[]{:S(2)}) copy-start(bf16[2,2048]{1,0:T(2,128)(2,1)} %outs_ref.1) | copy-start | bytes 24580
  0.7 0.7 %copy-start.2 = (bf16[4,1024]{1,0:T(4,128)(2,1)S(1)}, bf16[4,1024]{1,0:T(4,128)(2,1)}, u32[]{:S(2)}) copy-start(bf16[4,1024]{1,0:T(4,128)(2,1)} %params_ref.1) | copy-start | bytes 24580
  0.7 13.1 %collective-permute-start.5 = (bf16[256,1024]{1,0:T(8,128)(2,1)}, bf16[256,1024]{1,0:T(8,128)(2,1)S(1)}, u32[]{:S(2)}, u32[]{:S(2)}) collective-permute-start(bf16[256,1024]{1,0:T(8,128)(2,1)} %tokens_ref.1), channel_id=1, source_target_pairs={{0,1},{1,0},{2,3},{3,2},{4,5},{5,4},{6,7},{7,6},{8,9},{9,8},{10,11... | collective-permute-start | bytes 1572872 | tf_op jit(solution)/shard_map/ppermute | solution.py:324
  1.2 12.6 %collective-permute-start.6 = (bf16[256,1024]{1,0:T(8,128)(2,1)}, bf16[256,1024]{1,0:T(8,128)(2,1)S(1)}, u32[]{:S(2)}, u32[]{:S(2)}) collective-permute-start(bf16[256,1024]{1,0:T(8,128)(2,1)} %upstream_ref.1), channel_id=1, source_target_pairs={{0,1},{1,0},{2,3},{3,2},{4,5},{5,4},{6,7},{7,6},{8,9},{9,8},{10,11... | collective-permute-start | bytes 1572872 | tf_op jit(solution)/shard_map/ppermute | solution.py:324
  1.3 12.5 %copy-start.1 = (bf16[256,1024]{1,0:T(8,128)(2,1)S(1)}, bf16[256,1024]{1,0:T(8,128)(2,1)}, u32[]{:S(2)}) copy-start(bf16[256,1024]{1,0:T(8,128)(2,1)} %upstream_ref.1) | copy-start | bytes 1572868
  1.4 12.4 %copy-start = (bf16[256,1024]{1,0:T(8,128)(2,1)S(1)}, bf16[256,1024]{1,0:T(8,128)(2,1)}, u32[]{:S(2)}) copy-start(bf16[256,1024]{1,0:T(8,128)(2,1)} %tokens_ref.1) | copy-start | bytes 1572868
  1.4 5.2 %collective-permute-start = (bf16[1,8,1536]{2,1,0:T(8,128)(2,1)S(1)}, bf16[1,8,1536]{2,1,0:T(8,128)(2,1)S(1)}, u32[]{:S(2)}, u32[]{:S(2)}) collective-permute-start(bf16[1,8,1536]{2,1,0:T(8,128)(2,1)S(1)} %pack.1.mine_ref), channel_id=1, source_target_pairs={{0,9},{1,8},{2,11},{3,10},{4,13},{5,12},{6,15},{7,14},{8,1},{9,0},... | collective-permute-start | bytes 73736 | tf_op jit(solution)/shard_map/ppermute | solution.py:314
  6.6 4.8 %collective-permute-start.3 = (bf16[2,8,1536]{2,1,0:T(8,128)(2,1)S(1)}, bf16[2,8,1536]{2,1,0:T(8,128)(2,1)S(1)}, u32[]{:S(2)}, u32[]{:S(2)}) collective-permute-start(bf16[2,8,1536]{2,1,0:T(8,128)(2,1)S(1)} %pair.1.refs_0_), channel_id=1, source_target_pairs={{0,7},{1,6},{2,5},{3,4},{4,3},{5,2},{6,1},{7,0},{8,15},{9,14},{10,... | collective-permute-start | bytes 147464 | tf_op jit(solution)/shard_map/ppermute | solution.py:314
  9.3 3.5 %collective-permute-start.2 = (bf16[2,8,1536]{2,1,0:T(8,128)(2,1)S(1)}, bf16[2,8,1536]{2,1,0:T(8,128)(2,1)S(1)}, u32[]{:S(2)}, u32[]{:S(2)}) collective-permute-start(bf16[2,8,1536]{2,1,0:T(8,128)(2,1)S(1)} %pair.1.refs_0_), channel_id=1, source_target_pairs={{0,5},{1,4},{2,7},{3,6},{4,1},{5,0},{6,3},{7,2},{8,13},{9,12},{10,... | collective-permute-start | bytes 147464 | tf_op jit(solution)/shard_map/ppermute | solution.py:314
  9.8 3.8 %collective-permute-start.1 = (bf16[2,8,1536]{2,1,0:T(8,128)(2,1)S(1)}, bf16[2,8,1536]{2,1,0:T(8,128)(2,1)S(1)}, u32[]{:S(2)}, u32[]{:S(2)}) collective-permute-start(bf16[2,8,1536]{2,1,0:T(8,128)(2,1)S(1)} %pair.1.refs_0_), channel_id=1, source_target_pairs={{0,3},{1,2},{2,1},{3,0},{4,7},{5,6},{6,5},{7,4},{8,11},{9,10},{10,... | collective-permute-start | bytes 147464 | tf_op jit(solution)/shard_map/ppermute | solution.py:314
  13.6 1.5 %collective-permute-start.4 = (bf16[8,8,1536]{2,1,0:T(8,128)(2,1)S(1)}, bf16[8,8,1536]{2,1,0:T(8,128)(2,1)S(1)}, u32[]{:S(2)}, u32[]{:S(2)}) collective-permute-start(bf16[8,8,1536]{2,1,0:T(8,128)(2,1)S(1)} %order.1.slots_ref.refs_0_), channel_id=1, source_target_pairs={{0,1},{1,0},{2,3},{3,2},{4,5},{5,4},{6,7},{7,6},{8,9},{9,8},{10,11... | collective-permute-start | bytes 589832 | tf_op jit(solution)/shard_map/ppermute | solution.py:338
  16.1 5.1 %collective-permute-start.7 = (bf16[2,8,2176]{2,1,0:T(8,128)(2,1)S(1)}, bf16[2,8,2176]{2,1,0:T(8,128)(2,1)S(1)}, u32[]{:S(2)}, u32[]{:S(2)}) collective-permute-start(bf16[2,8,2176]{2,1,0:T(8,128)(2,1)S(1)} %get-tuple-element.31), channel_id=1, source_target_pairs={{0,7},{1,6},{2,5},{3,4},{4,3},{5,2},{6,1},{7,0},{8,15},{9,14},{10,... | collective-permute-start | bytes 208904 | tf_op jit(solution)/shard_map/ppermute | solution.py:314
  17.8 4.4 %collective-permute-start.8 = (bf16[2,8,2176]{2,1,0:T(8,128)(2,1)S(1)}, bf16[2,8,2176]{2,1,0:T(8,128)(2,1)S(1)}, u32[]{:S(2)}, u32[]{:S(2)}) collective-permute-start(bf16[2,8,2176]{2,1,0:T(8,128)(2,1)S(1)} %get-tuple-element.32), channel_id=1, source_target_pairs={{0,5},{1,4},{2,7},{3,6},{4,1},{5,0},{6,3},{7,2},{8,13},{9,12},{10,... | collective-permute-start | bytes 208904 | tf_op jit(solution)/shard_map/ppermute | solution.py:314
  18.3 4.6 %collective-permute-start.9 = (bf16[2,8,2176]{2,1,0:T(8,128)(2,1)S(1)}, bf16[2,8,2176]{2,1,0:T(8,128)(2,1)S(1)}, u32[]{:S(2)}, u32[]{:S(2)}) collective-permute-start(bf16[2,8,2176]{2,1,0:T(8,128)(2,1)S(1)} %get-tuple-element.33), channel_id=1, source_target_pairs={{0,3},{1,2},{2,1},{3,0},{4,7},{5,6},{6,5},{7,4},{8,11},{9,10},{10,... | collective-permute-start | bytes 208904 | tf_op jit(solution)/shard_map/ppermute | solution.py:314
  23.2 4.4 %collective-permute-start.10 = (bf16[1,8,2176]{2,1,0:T(8,128)(2,1)S(1)}, bf16[1,8,2176]{2,1,0:T(8,128)(2,1)S(1)}, u32[]{:S(2)}, u32[]{:S(2)}) collective-permute-start(bf16[1,8,2176]{2,1,0:T(8,128)(2,1)S(1)} %merge.1), channel_id=1, source_target_pairs={{0,9},{1,8},{2,11},{3,10},{4,13},{5,12},{6,15},{7,14},{8,1},{9,0},... | collective-permute-start | bytes 104456 | tf_op jit(solution)/shard_map/ppermute | solution.py:314

commit v8 on v7

--- a/solution.py
+++ b/solution.py
@@ -137,14 +137,14 @@
     slots_ref, tokens_ref, tokens_far_ref, upstream_ref, upstream_far_ref, *refs
 ):
     turned, (logit_ref, comb_ref, disp_ref), outs = refs[:4], refs[4:7], refs[7:]
-    sends, (col_ref, row_ref, d_disp_ref) = outs[:4], outs[4:7]
-    first_ref, second_ref, stats_ref, near_ref, far_ref = outs[7:]
+    sends = [ref.at[place] for ref in outs[:-8] for place in range(ref.shape[0])]
+    col_ref, row_ref, d_disp_ref, first_ref, second_ref, stats_ref, near_ref, far_ref = outs[-8:]
     side, me = lax.axis_index("exp"), lax.axis_index("seq")
     n_slots, patches = col_ref.shape
-    fours, _, width = sends[0].shape
-    seq = 4 * fours
+    seq = n_slots // 4
+    fours = seq // 4
     half = tokens_ref.shape[1]
-    extra = width - 2 * half
+    extra = stats_ref.shape[2]
     groups = n_slots // 8 + 1
     parts = products(slots_ref, *turned, [1 - owner(chip, seq) for chip in range(seq)])
     logits, d_comb, d_disp = (ref[...] + part for ref, part in zip((logit_ref, comb_ref, disp_ref), parts))
@@ -203,12 +203,11 @@
         by_tokens = dot(rows[: 16 * seq], token_half[...])
         left, right = by_tokens[: 8 * seq] + dot(rows[16 * seq :], upstream_half[...]), by_tokens[8 * seq :]
         total = (left, right) if total is None else (total[0] + left, total[1] + right)
-    left, right = (value.reshape(4, fours, 8, half).astype(BF16) for value in total)
-    for step, send_ref in enumerate(sends):
-        send_ref[:, :, :half] = left[step]
-        send_ref[:, :, half : 2 * half] = right[step]
-        for four in range(fours):
-            send_ref[four, :, 2 * half :] = stats_ref[receiver(me, fours, step, four)].astype(BF16)
+    left, right = (value.reshape(seq, 8, half).astype(BF16) for value in total)
+    for at, send_ref in enumerate(sends):
+        send_ref[:, :half] = left[at]
+        send_ref[:, half : 2 * half] = right[at]
+        send_ref[:, 2 * half :] = stats_ref[receiver(me, fours, at // fours, at % fours)].astype(BF16)
 
 
 def column_stats(stats, groups):
@@ -228,12 +227,11 @@
 
 def merge_kernel(*refs, groups, half):
     chunk_refs, out_ref = refs[:4], refs[4]
-    fours, _, width = chunk_refs[0].shape
-    merged = out_ref.shape[0]
+    merged, _, width = out_ref.shape
     lane = lax.broadcasted_iota(jnp.int32, (8, width - 2 * half), 1)
     upper = lax.broadcasted_iota(jnp.int32, lane.shape, 0) < 4
     for four in range(merged):
-        chunks = [ref.at[four + fours - merged] for ref in chunk_refs]
+        chunks = [ref.at[four] for ref in chunk_refs]
         high, total, inner, scales, means = merge_stats(chunks, half, groups)
         stats = [part for stat in (high, total, inner) for part in split16(stat)]
         centre = (stats[4] + stats[5]) / (stats[2] + stats[3])
@@ -342,27 +340,29 @@
         slots, tokens, tokens_far, upstream, far
     )
     chunk = (8, 2 * half + extra)
+    parts = 2 if fours == 2 else 1
     *sends, col, row, disp = call(
         local_kernel,
-        (sds((fours, *chunk), BF16),) * 4 + (by_slot,) * 3,
+        (sds((fours // parts, *chunk), BF16),) * (4 * parts) + (by_slot,) * 3,
         "local",
         seq,
         [pltpu.VMEM((seq, 8, patches), F32)] * 2
         + [pltpu.VMEM((seq, 8, extra), F32)]
         + [pltpu.VMEM((3, seq, 8, patches), F32)] * 2,
     )(other, tokens, tokens_far, upstream, far, *near)
-    got = [sends[0]] + [to_other_core(sends[step], seq, step) for step in (3, 2, 1)]
+    theirs = [to_other_core(sends[parts * step + parts - 1], seq, step) for step in (3, 2, 1)]
+    ours = [to_other_core(sends[parts * step], seq, step) for step in (3, 2, 1)] if fours == 2 else []
     merged = call(
         functools.partial(merge_kernel, groups=n_slots // 8 + 1, half=half),
-        sds((1 if fours == 2 else fours, *chunk), BF16),
+        sds((fours // parts, *chunk), BF16),
         "merge",
         seq,
-    )(*got)
+    )(sends[parts - 1], *theirs)
     if fours == 2:
-        got.append(to_other_core(merged, seq, 4))
+        got = [to_other_core(merged, seq, 4), *ours]
     else:
         same = [[4 * four + step for four in range(fours)] for step in range(4)]
-        got[1:] = [lax.all_to_all(merged, "seq", split_axis=0, concat_axis=0, tiled=True, axis_index_groups=same)]
+        got = [lax.all_to_all(merged, "seq", split_axis=0, concat_axis=0, tiled=True, axis_index_groups=same)]
     param_grads, token_grads, slot_output_grads = call(
         finish_kernel,
         (sds((4, half), F32), sds((patches, half), BF16), sds((2, 2 * half), F32)),
@@ -376,7 +376,7 @@
             pltpu.SemaphoreType.DMA((4,)),
         ],
         out_specs=[pl.BlockSpec(memory_space=pl.ANY)] * 3,
-    )(slots, other, col, row, disp, *got)
+    )(slots, other, col, row, disp, sends[0], *got)
     return token_grads, param_grads, slot_output_grads
 
 

time: 29.1 us -> 28.6 us (0.983)
  waiting for transfers between devices: 11.7 us -> 7.28 us
  starting transfers between devices: 13 us -> 16.9 us
    ppermute x8 -> x11, waiting for transfers between devices: 11.1 us -> 6.78 us  [to_other_core(): return lax.ppermute(value, ('seq', 'exp'), pairs)]
    ppermute x8 -> x11, starting transfers between devices: 12.2 us -> 16.1 us  [to_other_core(): return lax.ppermute(value, ('seq', 'exp'), pairs)]
  transfers between devices with their start and end apart: 11 -> 14, of which waited for: 9 -> 6; matrix products, arithmetic and copies ran while one was open for 0% -> 0% of each run, Pallas kernels for 3% -> 4%
where the time goes in v8:
time: 28.6 us; the launch traced here: 28.4 us
  starting transfers between devices  16.9 us (59%)
  waiting for transfers between devices  7.28 us (25%)
  Pallas kernels  3.41 us (12%)
  between operations  0.72 us (3%)
    ppermute x11, starting transfers between devices, to_other_core(): return lax.ppermute(value, ('seq', 'exp'), pairs)  16.1 us
    ppermute x11, waiting for transfers between devices, to_other_core(): return lax.ppermute(value, ('seq', 'exp'), pairs)  6.78 us
    pallas_call x1, Pallas kernels, shards(): call(finish_kernel, (sds((4, half), F32), sds((patches, half), BF16), sds...  1.33 us
    pallas_call x1, Pallas kernels, shards(): call(local_kernel, (sds((fours // parts, *chunk), BF16),) * (4 * parts) +...  0.99 us
    pallas_call x1, Pallas kernels, shards(): call(near_kernel, (turned,) * 4 + (by_slot,) * 3, 'near', seq, cost_estim...  0.8 us
    ppermute x2, starting transfers between devices, shards(): lax.ppermute(x, 'exp', cores)  0.6 us
  transfers between devices with their start and end apart: 14, of which 6 were waited for; matrix products, arithmetic and copies ran while one was open for 0% of the time, Pallas kernels for 4%

profile of v8, /device:TPU:0, one launch (start us, length us, event | category | flops | bytes accessed | tf_op | source)
XLA Modules:
  0.0 28.4 jit_solution(17960201215749967087)
XLA Ops:
  0.6 0.0 copy-start.4
  0.6 0.0 copy-start.3
  0.7 0.0 copy-start.2
  0.7 0.5 %collective-permute-start.5 = (bf16[256,1024]{1,0:T(8,128)(2,1)}, bf16[256,1024]{1,0:T(8,128)(2,1)S(1)}, u32[]{:S(2)}, u32[]{:S(2)}) collective-permute-start(bf16[256,1024]{1,0:T(8,128)(2,1)} %tokens_ref.1), channel_id=1, source_target_pairs={{0,1},{1,0},{2,3},{3,2},{4,5},{5,4},{6,7},{7,6},{8,9},{9,8},{10,11... | collective-permute-start | bytes 1572872 | tf_op jit(solution)/shard_map/ppermute | solution.py:322
  1.2 0.1 collective-permute-start.6
  1.3 0.0 copy-start.1
  1.3 0.1 copy-done.4
  1.3 0.0 copy-done.3
  1.3 0.0 copy-done.2
  1.4 0.0 copy-start
  1.4 3.7 %collective-permute-start = (bf16[1,8,1536]{2,1,0:T(8,128)(2,1)S(1)}, bf16[1,8,1536]{2,1,0:T(8,128)(2,1)S(1)}, u32[]{:S(2)}, u32[]{:S(2)}) collective-permute-start(bf16[1,8,1536]{2,1,0:T(8,128)(2,1)S(1)} %pack.1.mine_ref), channel_id=1, source_target_pairs={{0,9},{1,8},{2,11},{3,10},{4,13},{5,12},{6,15},{7,14},{8,1},{9,0},... | collective-permute-start | bytes 73736 | tf_op jit(solution)/shard_map/ppermute | solution.py:312
  5.1 1.5 %collective-permute-done.taken_ref = bf16[1,8,1536]{2,1,0:T(8,128)(2,1)S(1)} collective-permute-done((bf16[1,8,1536]{2,1,0:T(8,128)(2,1)S(1)}, bf16[1,8,1536]{2,1,0:T(8,128)(2,1)S(1)}, u32[]{:S(2)}, u32[]{:S(2)}) %collective-permute-start) | collective-permute-done | bytes 24608 | tf_op jit(solution)/shard_map/ppermute | solution.py:312
  6.6 2.7 %collective-permute-start.3 = (bf16[2,8,1536]{2,1,0:T(8,128)(2,1)S(1)}, bf16[2,8,1536]{2,1,0:T(8,128)(2,1)S(1)}, u32[]{:S(2)}, u32[]{:S(2)}) collective-permute-start(bf16[2,8,1536]{2,1,0:T(8,128)(2,1)S(1)} %pair.1.refs_0_), channel_id=1, source_target_pairs={{0,7},{1,6},{2,5},{3,4},{4,3},{5,2},{6,1},{7,0},{8,15},{9,14},{10,... | collective-permute-start | bytes 147464 | tf_op jit(solution)/shard_map/ppermute | solution.py:312
  9.3 0.5 %collective-permute-start.2 = (bf16[2,8,1536]{2,1,0:T(8,128)(2,1)S(1)}, bf16[2,8,1536]{2,1,0:T(8,128)(2,1)S(1)}, u32[]{:S(2)}, u32[]{:S(2)}) collective-permute-start(bf16[2,8,1536]{2,1,0:T(8,128)(2,1)S(1)} %pair.1.refs_0_), channel_id=1, source_target_pairs={{0,5},{1,4},{2,7},{3,6},{4,1},{5,0},{6,3},{7,2},{8,13},{9,12},{10,... | collective-permute-start | bytes 147464 | tf_op jit(solution)/shard_map/ppermute | solution.py:312
  9.8 0.2 collective-permute-start.1
  10.0 1.5 %collective-permute-done.3.refs_3_ = bf16[2,8,1536]{2,1,0:T(8,128)(2,1)S(1)} collective-permute-done((bf16[2,8,1536]{2,1,0:T(8,128)(2,1)S(1)}, bf16[2,8,1536]{2,1,0:T(8,128)(2,1)S(1)}, u32[]{:S(2)}, u32[]{:S(2)}) %collective-permute-start.3) | collective-permute-done | bytes 49184 | tf_op jit(solution)/shard_map/ppermute | solution.py:312
  11.4 1.4 %collective-permute-done.2.refs_2_ = bf16[2,8,1536]{2,1,0:T(8,128)(2,1)S(1)} collective-permute-done((bf16[2,8,1536]{2,1,0:T(8,128)(2,1)S(1)}, bf16[2,8,1536]{2,1,0:T(8,128)(2,1)S(1)}, u32[]{:S(2)}, u32[]{:S(2)}) %collective-permute-start.2) | collective-permute-done | bytes 49184 | tf_op jit(solution)/shard_map/ppermute | solution.py:312
  12.8 0.7 %collective-permute-done.1.refs_1_ = bf16[2,8,1536]{2,1,0:T(8,128)(2,1)S(1)} collective-permute-done((bf16[2,8,1536]{2,1,0:T(8,128)(2,1)S(1)}, bf16[2,8,1536]{2,1,0:T(8,128)(2,1)S(1)}, u32[]{:S(2)}, u32[]{:S(2)}) %collective-permute-start.1) | collective-permute-done | bytes 49184 | tf_op jit(solution)/shard_map/ppermute | solution.py:312
  13.6 0.2 collective-permute-start.4
  13.8 0.0 collective-permute-done.5.refs_1_.tokens_far_ref
  13.8 0.0 collective-permute-done.6.refs_3_.upstream_far_ref
  13.8 0.0 copy-done.1
  13.8 0.0 copy-done
  13.8 0.8 %near.1 = (bf16[1024,256]{1,0:T(8,128)(2,1)S(1)}, bf16[1024,256]{1,0:T(8,128)(2,1)S(1)}, bf16[1024,256]{1,0:T(8,128)(2,1)S(1)}, bf16[1024,256]{1,0:T(8,128)(2,1)...) custom-call(bf16[8,8,1536]{2,1,0:T(8,128)(2,1)S(1)} %order.1.slots_ref.refs_0_, ...), custom_call_target="tpu_custom_call" | custom-call | flops 10000000000 | bytes 10000000 | tf_op jit(solution)/shard_map/near/pallas_call | solution.py:339
  14.6 0.5 %collective-permute-done.4.slots_ref.refs_1_ = bf16[8,8,1536]{2,1,0:T(8,128)(2,1)S(1)} collective-permute-done((bf16[8,8,1536]{2,1,0:T(8,128)(2,1)S(1)}, bf16[8,8,1536]{2,1,0:T(8,128)(2,1)S(1)}, u32[]{:S(2)}, u32[]{:S(2)}) %collective-permute-start.4) | collective-permute-done | bytes 196640 | tf_op jit(solution)/shard_map/ppermute | solution.py:336
  15.1 1.0 %local.1 = (bf16[1,8,2176]{2,1,0:T(8,128)(2,1)S(1)}, bf16[1,8,2176]{2,1,0:T(8,128)(2,1)S(1)}, bf16[1,8,2176]{2,1,0:T(8,128)(2,1)S(1)}, bf16[1,8,2176]{2,1,0:T(8,...) custom-call(bf16[8,8,1536]{2,1,0:T(8,128)(2,1)S(1)} %collective-perm, ...), custom_call_target="tpu_custom_call" | custom-call | tf_op jit(solution)/shard_map/local/pallas_call | solution.py:344
  16.1 1.7 %collective-permute-start.7 = (bf16[1,8,2176]{2,1,0:T(8,128)(2,1)S(1)}, bf16[1,8,2176]{2,1,0:T(8,128)(2,1)S(1)}, u32[]{:S(2)}, u32[]{:S(2)}) collective-permute-start(bf16[1,8,2176]{2,1,0:T(8,128)(2,1)S(1)} %get-tuple-element.36), channel_id=1, source_target_pairs={{0,7},{1,6},{2,5},{3,4},{4,3},{5,2},{6,1},{7,0},{8,15},{9,14},{10,... | collective-permute-start | bytes 104456 | tf_op jit(solution)/shard_map/ppermute | solution.py:312
  17.8 0.4 %collective-permute-start.8 = (bf16[1,8,2176]{2,1,0:T(8,128)(2,1)S(1)}, bf16[1,8,2176]{2,1,0:T(8,128)(2,1)S(1)}, u32[]{:S(2)}, u32[]{:S(2)}) collective-permute-start(bf16[1,8,2176]{2,1,0:T(8,128)(2,1)S(1)} %get-tuple-element.37), channel_id=1, source_target_pairs={{0,5},{1,4},{2,7},{3,6},{4,1},{5,0},{6,3},{7,2},{8,13},{9,12},{10,... | collective-permute-start | bytes 104456 | tf_op jit(solution)/shard_map/ppermute | solution.py:312
  18.3 0.8 %collective-permute-start.9 = (bf16[1,8,2176]{2,1,0:T(8,128)(2,1)S(1)}, bf16[1,8,2176]{2,1,0:T(8,128)(2,1)S(1)}, u32[]{:S(2)}, u32[]{:S(2)}) collective-permute-start(bf16[1,8,2176]{2,1,0:T(8,128)(2,1)S(1)} %get-tuple-element.38), channel_id=1, source_target_pairs={{0,3},{1,2},{2,1},{3,0},{4,7},{5,6},{6,5},{7,4},{8,11},{9,10},{10,... | collective-permute-start | bytes 104456 | tf_op jit(solution)/shard_map/ppermute | solution.py:312
  19.1 1.9 %collective-permute-start.11 = (bf16[1,8,2176]{2,1,0:T(8,128)(2,1)S(1)}, bf16[1,8,2176]{2,1,0:T(8,128)(2,1)S(1)}, u32[]{:S(2)}, u32[]{:S(2)}) collective-permute-start(bf16[1,8,2176]{2,1,0:T(8,128)(2,1)S(1)} %get-tuple-element.39), channel_id=1, source_target_pairs={{0,7},{1,6},{2,5},{3,4},{4,3},{5,2},{6,1},{7,0},{8,15},{9,14},{10,... | collective-permute-start | bytes 104456 | tf_op jit(solution)/shard_map/ppermute | solution.py:312
  21.0 0.2 collective-permute-start.12
  21.3 0.0 collective-permute-done.7.refs_1_
  21.3 1.0 %collective-permute-start.13 = (bf16[1,8,2176]{2,1,0:T(8,128)(2,1)S(1)}, bf16[1,8,2176]{2,1,0:T(8,128)(2,1)S(1)}, u32[]{:S(2)}, u32[]{:S(2)}) collective-permute-start(bf16[1,8,2176]{2,1,0:T(8,128)(2,1)S(1)} %get-tuple-element.41), channel_id=1, source_target_pairs={{0,3},{1,2},{2,1},{3,0},{4,7},{5,6},{6,5},{7,4},{8,11},{9,10},{10,... | collective-permute-start | bytes 104456 | tf_op jit(solution)/shard_map/ppermute | solution.py:312
  22.3 0.0 collective-permute-done.8.refs_2_
  22.3 0.0 collective-permute-done.9.refs_3_
  22.3 0.2 merge.1
  22.6 2.9 %collective-permute-start.10 = (bf16[1,8,2176]{2,1,0:T(8,128)(2,1)S(1)}, bf16[1,8,2176]{2,1,0:T(8,128)(2,1)S(1)}, u32[]{:S(2)}, u32[]{:S(2)}) collective-permute-start(bf16[1,8,2176]{2,1,0:T(8,128)(2,1)S(1)} %merge.1), channel_id=1, source_target_pairs={{0,9},{1,8},{2,11},{3,10},{4,13},{5,12},{6,15},{7,14},{8,1},{9,0},... | collective-permute-start | bytes 104456 | tf_op jit(solution)/shard_map/ppermute | solution.py:312
  25.4 0.0 collective-permute-done.11.refs_7_
  25.4 0.0 collective-permute-done.12.refs_8_
  25.4 0.0 collective-permute-done.13.refs_9_
  25.4 1.6 %collective-permute-done.10.refs_6_ = bf16[1,8,2176]{2,1,0:T(8,128)(2,1)S(1)} collective-permute-done((bf16[1,8,2176]{2,1,0:T(8,128)(2,1)S(1)}, bf16[1,8,2176]{2,1,0:T(8,128)(2,1)S(1)}, u32[]{:S(2)}, u32[]{:S(2)}) %collective-permute-start.10) | collective-permute-done | bytes 34848 | tf_op jit(solution)/shard_map/ppermute | solution.py:312
  27.1 1.3 %finish.1 = (f32[4,1024]{1,0:T(4,128)}, bf16[256,1024]{1,0:T(8,128)(2,1)}, f32[2,2048]{1,0:T(2,128)}) custom-call(bf16[8,8,1536]{2,1,0:T(8,128)(2,1)S(1)} %order.1.slots_ref.refs_0_, bf16[8,8,1536]{2,1,0:T(8,128)(2,1)S(1)} %collective-permute-done.4.slots_ref.refs_1_, f32[32,256]{1,0:T(8,128)S(1)} %get-tuple-element.31.refs_2_, ...), custom_call_target="tpu_custom_call" | custom-call | tf_op jit(solution)/shard_map/finish/pallas_call | solution.py:366
  (4 shorter events, 0.0 us)
Async XLA Ops:
  0.6 0.7 %copy-start.4 = (bf16[2,2048]{1,0:T(2,128)(2,1)S(1)}, bf16[2,2048]{1,0:T(2,128)(2,1)}, u32[]{:S(2)}) copy-start(bf16[2,2048]{1,0:T(2,128)(2,1)} %grads_ref.1) | copy-start | bytes 24580
  0.6 0.7 %copy-start.3 = (bf16[2,2048]{1,0:T(2,128)(2,1)S(1)}, bf16[2,2048]{1,0:T(2,128)(2,1)}, u32[]{:S(2)}) copy-start(bf16[2,2048]{1,0:T(2,128)(2,1)} %outs_ref.1) | copy-start | bytes 24580
  0.7 0.7 %copy-start.2 = (bf16[4,1024]{1,0:T(4,128)(2,1)S(1)}, bf16[4,1024]{1,0:T(4,128)(2,1)}, u32[]{:S(2)}) copy-start(bf16[4,1024]{1,0:T(4,128)(2,1)} %params_ref.1) | copy-start | bytes 24580
  0.7 13.1 %collective-permute-start.5 = (bf16[256,1024]{1,0:T(8,128)(2,1)}, bf16[256,1024]{1,0:T(8,128)(2,1)S(1)}, u32[]{:S(2)}, u32[]{:S(2)}) collective-permute-start(bf16[256,1024]{1,0:T(8,128)(2,1)} %tokens_ref.1), channel_id=1, source_target_pairs={{0,1},{1,0},{2,3},{3,2},{4,5},{5,4},{6,7},{7,6},{8,9},{9,8},{10,11... | collective-permute-start | bytes 1572872 | tf_op jit(solution)/shard_map/ppermute | solution.py:322
  1.2 12.6 %collective-permute-start.6 = (bf16[256,1024]{1,0:T(8,128)(2,1)}, bf16[256,1024]{1,0:T(8,128)(2,1)S(1)}, u32[]{:S(2)}, u32[]{:S(2)}) collective-permute-start(bf16[256,1024]{1,0:T(8,128)(2,1)} %upstream_ref.1), channel_id=1, source_target_pairs={{0,1},{1,0},{2,3},{3,2},{4,5},{5,4},{6,7},{7,6},{8,9},{9,8},{10,11... | collective-permute-start | bytes 1572872 | tf_op jit(solution)/shard_map/ppermute | solution.py:322
  1.3 12.5 %copy-start.1 = (bf16[256,1024]{1,0:T(8,128)(2,1)S(1)}, bf16[256,1024]{1,0:T(8,128)(2,1)}, u32[]{:S(2)}) copy-start(bf16[256,1024]{1,0:T(8,128)(2,1)} %upstream_ref.1) | copy-start | bytes 1572868
  1.4 12.4 %copy-start = (bf16[256,1024]{1,0:T(8,128)(2,1)S(1)}, bf16[256,1024]{1,0:T(8,128)(2,1)}, u32[]{:S(2)}) copy-start(bf16[256,1024]{1,0:T(8,128)(2,1)} %tokens_ref.1) | copy-start | bytes 1572868
  1.4 5.2 %collective-permute-start = (bf16[1,8,1536]{2,1,0:T(8,128)(2,1)S(1)}, bf16[1,8,1536]{2,1,0:T(8,128)(2,1)S(1)}, u32[]{:S(2)}, u32[]{:S(2)}) collective-permute-start(bf16[1,8,1536]{2,1,0:T(8,128)(2,1)S(1)} %pack.1.mine_ref), channel_id=1, source_target_pairs={{0,9},{1,8},{2,11},{3,10},{4,13},{5,12},{6,15},{7,14},{8,1},{9,0},... | collective-permute-start | bytes 73736 | tf_op jit(solution)/shard_map/ppermute | solution.py:312
  6.6 4.8 %collective-permute-start.3 = (bf16[2,8,1536]{2,1,0:T(8,128)(2,1)S(1)}, bf16[2,8,1536]{2,1,0:T(8,128)(2,1)S(1)}, u32[]{:S(2)}, u32[]{:S(2)}) collective-permute-start(bf16[2,8,1536]{2,1,0:T(8,128)(2,1)S(1)} %pair.1.refs_0_), channel_id=1, source_target_pairs={{0,7},{1,6},{2,5},{3,4},{4,3},{5,2},{6,1},{7,0},{8,15},{9,14},{10,... | collective-permute-start | bytes 147464 | tf_op jit(solution)/shard_map/ppermute | solution.py:312
  9.3 3.5 %collective-permute-start.2 = (bf16[2,8,1536]{2,1,0:T(8,128)(2,1)S(1)}, bf16[2,8,1536]{2,1,0:T(8,128)(2,1)S(1)}, u32[]{:S(2)}, u32[]{:S(2)}) collective-permute-start(bf16[2,8,1536]{2,1,0:T(8,128)(2,1)S(1)} %pair.1.refs_0_), channel_id=1, source_target_pairs={{0,5},{1,4},{2,7},{3,6},{4,1},{5,0},{6,3},{7,2},{8,13},{9,12},{10,... | collective-permute-start | bytes 147464 | tf_op jit(solution)/shard_map/ppermute | solution.py:312
  9.8 3.8 %collective-permute-start.1 = (bf16[2,8,1536]{2,1,0:T(8,128)(2,1)S(1)}, bf16[2,8,1536]{2,1,0:T(8,128)(2,1)S(1)}, u32[]{:S(2)}, u32[]{:S(2)}) collective-permute-start(bf16[2,8,1536]{2,1,0:T(8,128)(2,1)S(1)} %pair.1.refs_0_), channel_id=1, source_target_pairs={{0,3},{1,2},{2,1},{3,0},{4,7},{5,6},{6,5},{7,4},{8,11},{9,10},{10,... | collective-permute-start | bytes 147464 | tf_op jit(solution)/shard_map/ppermute | solution.py:312
  13.6 1.5 %collective-permute-start.4 = (bf16[8,8,1536]{2,1,0:T(8,128)(2,1)S(1)}, bf16[8,8,1536]{2,1,0:T(8,128)(2,1)S(1)}, u32[]{:S(2)}, u32[]{:S(2)}) collective-permute-start(bf16[8,8,1536]{2,1,0:T(8,128)(2,1)S(1)} %order.1.slots_ref.refs_0_), channel_id=1, source_target_pairs={{0,1},{1,0},{2,3},{3,2},{4,5},{5,4},{6,7},{7,6},{8,9},{9,8},{10,11... | collective-permute-start | bytes 589832 | tf_op jit(solution)/shard_map/ppermute | solution.py:336
  16.1 5.2 %collective-permute-start.7 = (bf16[1,8,2176]{2,1,0:T(8,128)(2,1)S(1)}, bf16[1,8,2176]{2,1,0:T(8,128)(2,1)S(1)}, u32[]{:S(2)}, u32[]{:S(2)}) collective-permute-start(bf16[1,8,2176]{2,1,0:T(8,128)(2,1)S(1)} %get-tuple-element.36), channel_id=1, source_target_pairs={{0,7},{1,6},{2,5},{3,4},{4,3},{5,2},{6,1},{7,0},{8,15},{9,14},{10,... | collective-permute-start | bytes 104456 | tf_op jit(solution)/shard_map/ppermute | solution.py:312
  17.8 4.5 %collective-permute-start.8 = (bf16[1,8,2176]{2,1,0:T(8,128)(2,1)S(1)}, bf16[1,8,2176]{2,1,0:T(8,128)(2,1)S(1)}, u32[]{:S(2)}, u32[]{:S(2)}) collective-permute-start(bf16[1,8,2176]{2,1,0:T(8,128)(2,1)S(1)} %get-tuple-element.37), channel_id=1, source_target_pairs={{0,5},{1,4},{2,7},{3,6},{4,1},{5,0},{6,3},{7,2},{8,13},{9,12},{10,... | collective-permute-start | bytes 104456 | tf_op jit(solution)/shard_map/ppermute | solution.py:312
  18.3 4.0 %collective-permute-start.9 = (bf16[1,8,2176]{2,1,0:T(8,128)(2,1)S(1)}, bf16[1,8,2176]{2,1,0:T(8,128)(2,1)S(1)}, u32[]{:S(2)}, u32[]{:S(2)}) collective-permute-start(bf16[1,8,2176]{2,1,0:T(8,128)(2,1)S(1)} %get-tuple-element.38), channel_id=1, source_target_pairs={{0,3},{1,2},{2,1},{3,0},{4,7},{5,6},{6,5},{7,4},{8,11},{9,10},{10,... | collective-permute-start | bytes 104456 | tf_op jit(solution)/shard_map/ppermute | solution.py:312
  19.1 6.3 %collective-permute-start.11 = (bf16[1,8,2176]{2,1,0:T(8,128)(2,1)S(1)}, bf16[1,8,2176]{2,1,0:T(8,128)(2,1)S(1)}, u32[]{:S(2)}, u32[]{:S(2)}) collective-permute-start(bf16[1,8,2176]{2,1,0:T(8,128)(2,1)S(1)} %get-tuple-element.39), channel_id=1, source_target_pairs={{0,7},{1,6},{2,5},{3,4},{4,3},{5,2},{6,1},{7,0},{8,15},{9,14},{10,... | collective-permute-start | bytes 104456 | tf_op jit(solution)/shard_map/ppermute | solution.py:312
  21.0 4.4 %collective-permute-start.12 = (bf16[1,8,2176]{2,1,0:T(8,128)(2,1)S(1)}, bf16[1,8,2176]{2,1,0:T(8,128)(2,1)S(1)}, u32[]{:S(2)}, u32[]{:S(2)}) collective-permute-start(bf16[1,8,2176]{2,1,0:T(8,128)(2,1)S(1)} %get-tuple-element.40), channel_id=1, source_target_pairs={{0,5},{1,4},{2,7},{3,6},{4,1},{5,0},{6,3},{7,2},{8,13},{9,12},{10,... | collective-permute-start | bytes 104456 | tf_op jit(solution)/shard_map/ppermute | solution.py:312
  21.3 4.2 %collective-permute-start.13 = (bf16[1,8,2176]{2,1,0:T(8,128)(2,1)S(1)}, bf16[1,8,2176]{2,1,0:T(8,128)(2,1)S(1)}, u32[]{:S(2)}, u32[]{:S(2)}) collective-permute-start(bf16[1,8,2176]{2,1,0:T(8,128)(2,1)S(1)} %get-tuple-element.41), channel_id=1, source_target_pairs={{0,3},{1,2},{2,1},{3,0},{4,7},{5,6},{6,5},{7,4},{8,11},{9,10},{10,... | collective-permute-start | bytes 104456 | tf_op jit(solution)/shard_map/ppermute | solution.py:312
  22.6 4.5 %collective-permute-start.10 = (bf16[1,8,2176]{2,1,0:T(8,128)(2,1)S(1)}, bf16[1,8,2176]{2,1,0:T(8,128)(2,1)S(1)}, u32[]{:S(2)}, u32[]{:S(2)}) collective-permute-start(bf16[1,8,2176]{2,1,0:T(8,128)(2,1)S(1)} %merge.1), channel_id=1, source_target_pairs={{0,9},{1,8},{2,11},{3,10},{4,13},{5,12},{6,15},{7,14},{8,1},{9,0},... | collective-permute-start | bytes 104456 | tf_op jit(solution)/shard_map/ppermute | solution.py:312

commit v9 on v8

--- a/solution.py
+++ b/solution.py
@@ -231,7 +231,7 @@
     lane = lax.broadcasted_iota(jnp.int32, (8, width - 2 * half), 1)
     upper = lax.broadcasted_iota(jnp.int32, lane.shape, 0) < 4
     for four in range(merged):
-        chunks = [ref.at[four] for ref in chunk_refs]
+        chunks = [ref.at[ref.shape[0] - merged + four] for ref in chunk_refs]
         high, total, inner, scales, means = merge_stats(chunks, half, groups)
         stats = [part for stat in (high, total, inner) for part in split16(stat)]
         centre = (stats[4] + stats[5]) / (stats[2] + stats[3])
@@ -340,26 +340,28 @@
         slots, tokens, tokens_far, upstream, far
     )
     chunk = (8, 2 * half + extra)
-    parts = 2 if fours == 2 else 1
+    cuts = [2 if fours == 2 and step != 3 else 1 for step in range(4)]
     *sends, col, row, disp = call(
         local_kernel,
-        (sds((fours // parts, *chunk), BF16),) * (4 * parts) + (by_slot,) * 3,
+        tuple(sds((fours // cut, *chunk), BF16) for cut in cuts for _ in range(cut)) + (by_slot,) * 3,
         "local",
         seq,
         [pltpu.VMEM((seq, 8, patches), F32)] * 2
         + [pltpu.VMEM((seq, 8, extra), F32)]
         + [pltpu.VMEM((3, seq, 8, patches), F32)] * 2,
     )(other, tokens, tokens_far, upstream, far, *near)
-    theirs = [to_other_core(sends[parts * step + parts - 1], seq, step) for step in (3, 2, 1)]
-    ours = [to_other_core(sends[parts * step], seq, step) for step in (3, 2, 1)] if fours == 2 else []
+    first = [sends[sum(cuts[:step])] for step in range(4)]
+    last = [sends[sum(cuts[: step + 1]) - 1] for step in range(4)]
+    theirs = {step: to_other_core(last[step], seq, step) for step in (3, 2, 1)}
+    ours = {step: to_other_core(first[step], seq, step) for step in (3, 2, 1) if cuts[step] == 2}
     merged = call(
         functools.partial(merge_kernel, groups=n_slots // 8 + 1, half=half),
-        sds((fours // parts, *chunk), BF16),
+        sds((1 if fours == 2 else fours, *chunk), BF16),
         "merge",
         seq,
-    )(sends[parts - 1], *theirs)
+    )(last[0], *theirs.values())
     if fours == 2:
-        got = [to_other_core(merged, seq, 4), *ours]
+        got = [to_other_core(merged, seq, 4), *({**theirs, **ours}[step] for step in (3, 2, 1))]
     else:
         same = [[4 * four + step for four in range(fours)] for step in range(4)]
         got = [lax.all_to_all(merged, "seq", split_axis=0, concat_axis=0, tiled=True, axis_index_groups=same)]
@@ -376,7 +378,7 @@
             pltpu.SemaphoreType.DMA((4,)),
         ],
         out_specs=[pl.BlockSpec(memory_space=pl.ANY)] * 3,
-    )(slots, other, col, row, disp, sends[0], *got)
+    )(slots, other, col, row, disp, first[0], *got)
     return token_grads, param_grads, slot_output_grads
 
 

time: 28.6 us -> 28.3 us (0.990)
  starting transfers between devices: 16.9 us -> 15.5 us
  waiting for transfers between devices: 7.28 us -> 8.32 us
    ppermute x11 -> x10, starting transfers between devices: 16.1 us -> 14.8 us  [to_other_core(): return lax.ppermute(value, ('seq', 'exp'), pairs)]
    ppermute x11 -> x10, waiting for transfers between devices: 6.78 us -> 7.82 us  [to_other_core(): return lax.ppermute(value, ('seq', 'exp'), pairs)]
  transfers between devices with their start and end apart: 14 -> 13, of which waited for: 6 -> 8; matrix products, arithmetic and copies ran while one was open for 0% -> 0% of each run, Pallas kernels for 4% -> 4%
where the time goes in v9:
time: 28.3 us; the launch traced here: 28.1 us
  starting transfers between devices  15.5 us (55%)
  waiting for transfers between devices  8.32 us (29%)
  Pallas kernels  3.41 us (12%)
  between operations  0.72 us (3%)
    ppermute x10, starting transfers between devices, to_other_core(): return lax.ppermute(value, ('seq', 'exp'), pairs)  14.8 us
    ppermute x10, waiting for transfers between devices, to_other_core(): return lax.ppermute(value, ('seq', 'exp'), pairs)  7.82 us
    pallas_call x1, Pallas kernels, shards(): call(finish_kernel, (sds((4, half), F32), sds((patches, half), BF16), sds...  1.34 us
    pallas_call x1, Pallas kernels, shards(): call(local_kernel, tuple((sds((fours // cut, *chunk), BF16) for cut in cu...  0.98 us
    pallas_call x1, Pallas kernels, shards(): call(near_kernel, (turned,) * 4 + (by_slot,) * 3, 'near', seq, cost_estim...  0.8 us
    ppermute x2, starting transfers between devices, shards(): lax.ppermute(x, 'exp', cores)  0.6 us
  transfers between devices with their start and end apart: 13, of which 8 were waited for; matrix products, arithmetic and copies ran while one was open for 0% of the time, Pallas kernels for 4%

profile of v9, /device:TPU:0, one launch (start us, length us, event | category | flops | bytes accessed | tf_op | source)
XLA Modules:
  0.0 28.1 jit_solution(3324264246212655895)
XLA Ops:
  0.6 0.0 copy-start.4
  0.6 0.0 copy-start.3
  0.7 0.0 copy-start.2
  0.7 0.5 %collective-permute-start.5 = (bf16[256,1024]{1,0:T(8,128)(2,1)}, bf16[256,1024]{1,0:T(8,128)(2,1)S(1)}, u32[]{:S(2)}, u32[]{:S(2)}) collective-permute-start(bf16[256,1024]{1,0:T(8,128)(2,1)} %tokens_ref.1), channel_id=1, source_target_pairs={{0,1},{1,0},{2,3},{3,2},{4,5},{5,4},{6,7},{7,6},{8,9},{9,8},{10,11... | collective-permute-start | bytes 1572872 | tf_op jit(solution)/shard_map/ppermute | solution.py:322
  1.2 0.1 collective-permute-start.6
  1.3 0.0 copy-start.1
  1.3 0.1 copy-done.4
  1.3 0.0 copy-done.3
  1.3 0.0 copy-done.2
  1.4 0.0 copy-start
  1.4 3.7 %collective-permute-start = (bf16[1,8,1536]{2,1,0:T(8,128)(2,1)S(1)}, bf16[1,8,1536]{2,1,0:T(8,128)(2,1)S(1)}, u32[]{:S(2)}, u32[]{:S(2)}) collective-permute-start(bf16[1,8,1536]{2,1,0:T(8,128)(2,1)S(1)} %pack.1.mine_ref), channel_id=1, source_target_pairs={{0,9},{1,8},{2,11},{3,10},{4,13},{5,12},{6,15},{7,14},{8,1},{9,0},... | collective-permute-start | bytes 73736 | tf_op jit(solution)/shard_map/ppermute | solution.py:312
  5.1 1.5 %collective-permute-done.taken_ref = bf16[1,8,1536]{2,1,0:T(8,128)(2,1)S(1)} collective-permute-done((bf16[1,8,1536]{2,1,0:T(8,128)(2,1)S(1)}, bf16[1,8,1536]{2,1,0:T(8,128)(2,1)S(1)}, u32[]{:S(2)}, u32[]{:S(2)}) %collective-permute-start) | collective-permute-done | bytes 24608 | tf_op jit(solution)/shard_map/ppermute | solution.py:312
  6.6 2.7 %collective-permute-start.3 = (bf16[2,8,1536]{2,1,0:T(8,128)(2,1)S(1)}, bf16[2,8,1536]{2,1,0:T(8,128)(2,1)S(1)}, u32[]{:S(2)}, u32[]{:S(2)}) collective-permute-start(bf16[2,8,1536]{2,1,0:T(8,128)(2,1)S(1)} %pair.1.refs_0_), channel_id=1, source_target_pairs={{0,7},{1,6},{2,5},{3,4},{4,3},{5,2},{6,1},{7,0},{8,15},{9,14},{10,... | collective-permute-start | bytes 147464 | tf_op jit(solution)/shard_map/ppermute | solution.py:312
  9.3 0.5 %collective-permute-start.2 = (bf16[2,8,1536]{2,1,0:T(8,128)(2,1)S(1)}, bf16[2,8,1536]{2,1,0:T(8,128)(2,1)S(1)}, u32[]{:S(2)}, u32[]{:S(2)}) collective-permute-start(bf16[2,8,1536]{2,1,0:T(8,128)(2,1)S(1)} %pair.1.refs_0_), channel_id=1, source_target_pairs={{0,5},{1,4},{2,7},{3,6},{4,1},{5,0},{6,3},{7,2},{8,13},{9,12},{10,... | collective-permute-start | bytes 147464 | tf_op jit(solution)/shard_map/ppermute | solution.py:312
  9.8 0.2 collective-permute-start.1
  10.0 1.5 %collective-permute-done.3.refs_3_ = bf16[2,8,1536]{2,1,0:T(8,128)(2,1)S(1)} collective-permute-done((bf16[2,8,1536]{2,1,0:T(8,128)(2,1)S(1)}, bf16[2,8,1536]{2,1,0:T(8,128)(2,1)S(1)}, u32[]{:S(2)}, u32[]{:S(2)}) %collective-permute-start.3) | collective-permute-done | bytes 49184 | tf_op jit(solution)/shard_map/ppermute | solution.py:312
  11.4 1.4 %collective-permute-done.2.refs_2_ = bf16[2,8,1536]{2,1,0:T(8,128)(2,1)S(1)} collective-permute-done((bf16[2,8,1536]{2,1,0:T(8,128)(2,1)S(1)}, bf16[2,8,1536]{2,1,0:T(8,128)(2,1)S(1)}, u32[]{:S(2)}, u32[]{:S(2)}) %collective-permute-start.2) | collective-permute-done | bytes 49184 | tf_op jit(solution)/shard_map/ppermute | solution.py:312
  12.8 0.7 %collective-permute-done.1.refs_1_ = bf16[2,8,1536]{2,1,0:T(8,128)(2,1)S(1)} collective-permute-done((bf16[2,8,1536]{2,1,0:T(8,128)(2,1)S(1)}, bf16[2,8,1536]{2,1,0:T(8,128)(2,1)S(1)}, u32[]{:S(2)}, u32[]{:S(2)}) %collective-permute-start.1) | collective-permute-done | bytes 49184 | tf_op jit(solution)/shard_map/ppermute | solution.py:312
  13.6 0.2 collective-permute-start.4
  13.8 0.0 collective-permute-done.5.refs_1_.tokens_far_ref
  13.8 0.0 collective-permute-done.6.refs_3_.upstream_far_ref
  13.8 0.0 copy-done.1
  13.8 0.0 copy-done
  13.8 0.8 %near.1 = (bf16[1024,256]{1,0:T(8,128)(2,1)S(1)}, bf16[1024,256]{1,0:T(8,128)(2,1)S(1)}, bf16[1024,256]{1,0:T(8,128)(2,1)S(1)}, bf16[1024,256]{1,0:T(8,128)(2,1)...) custom-call(bf16[8,8,1536]{2,1,0:T(8,128)(2,1)S(1)} %order.1.slots_ref.refs_0_, ...), custom_call_target="tpu_custom_call" | custom-call | flops 10000000000 | bytes 10000000 | tf_op jit(solution)/shard_map/near/pallas_call | solution.py:339
  14.6 0.5 %collective-permute-done.4.slots_ref.refs_1_ = bf16[8,8,1536]{2,1,0:T(8,128)(2,1)S(1)} collective-permute-done((bf16[8,8,1536]{2,1,0:T(8,128)(2,1)S(1)}, bf16[8,8,1536]{2,1,0:T(8,128)(2,1)S(1)}, u32[]{:S(2)}, u32[]{:S(2)}) %collective-permute-start.4) | collective-permute-done | bytes 196640 | tf_op jit(solution)/shard_map/ppermute | solution.py:336
  15.1 1.0 %local.1 = (bf16[1,8,2176]{2,1,0:T(8,128)(2,1)S(1)}, bf16[1,8,2176]{2,1,0:T(8,128)(2,1)S(1)}, bf16[1,8,2176]{2,1,0:T(8,128)(2,1)S(1)}, bf16[1,8,2176]{2,1,0:T(8,...) custom-call(bf16[8,8,1536]{2,1,0:T(8,128)(2,1)S(1)} %collective-perm, ...), custom_call_target="tpu_custom_call" | custom-call | tf_op jit(solution)/shard_map/local/pallas_call | solution.py:344
  16.1 1.7 %collective-permute-start.7 = (bf16[2,8,2176]{2,1,0:T(8,128)(2,1)S(1)}, bf16[2,8,2176]{2,1,0:T(8,128)(2,1)S(1)}, u32[]{:S(2)}, u32[]{:S(2)}) collective-permute-start(bf16[2,8,2176]{2,1,0:T(8,128)(2,1)S(1)} %get-tuple-element.35), channel_id=1, source_target_pairs={{0,7},{1,6},{2,5},{3,4},{4,3},{5,2},{6,1},{7,0},{8,15},{9,14},{10,... | collective-permute-start | bytes 208904 | tf_op jit(solution)/shard_map/ppermute | solution.py:312
  17.8 0.5 %collective-permute-start.8 = (bf16[1,8,2176]{2,1,0:T(8,128)(2,1)S(1)}, bf16[1,8,2176]{2,1,0:T(8,128)(2,1)S(1)}, u32[]{:S(2)}, u32[]{:S(2)}) collective-permute-start(bf16[1,8,2176]{2,1,0:T(8,128)(2,1)S(1)} %get-tuple-element.36), channel_id=1, source_target_pairs={{0,5},{1,4},{2,7},{3,6},{4,1},{5,0},{6,3},{7,2},{8,13},{9,12},{10,... | collective-permute-start | bytes 104456 | tf_op jit(solution)/shard_map/ppermute | solution.py:312
  18.3 0.8 %collective-permute-start.9 = (bf16[1,8,2176]{2,1,0:T(8,128)(2,1)S(1)}, bf16[1,8,2176]{2,1,0:T(8,128)(2,1)S(1)}, u32[]{:S(2)}, u32[]{:S(2)}) collective-permute-start(bf16[1,8,2176]{2,1,0:T(8,128)(2,1)S(1)} %get-tuple-element.37), channel_id=1, source_target_pairs={{0,3},{1,2},{2,1},{3,0},{4,7},{5,6},{6,5},{7,4},{8,11},{9,10},{10,... | collective-permute-start | bytes 104456 | tf_op jit(solution)/shard_map/ppermute | solution.py:312
  19.1 1.5 %collective-permute-start.11 = (bf16[1,8,2176]{2,1,0:T(8,128)(2,1)S(1)}, bf16[1,8,2176]{2,1,0:T(8,128)(2,1)S(1)}, u32[]{:S(2)}, u32[]{:S(2)}) collective-permute-start(bf16[1,8,2176]{2,1,0:T(8,128)(2,1)S(1)} %get-tuple-element.38), channel_id=1, source_target_pairs={{0,5},{1,4},{2,7},{3,6},{4,1},{5,0},{6,3},{7,2},{8,13},{9,12},{10,... | collective-permute-start | bytes 104456 | tf_op jit(solution)/shard_map/ppermute | solution.py:312
  20.7 0.7 %collective-permute-start.12 = (bf16[1,8,2176]{2,1,0:T(8,128)(2,1)S(1)}, bf16[1,8,2176]{2,1,0:T(8,128)(2,1)S(1)}, u32[]{:S(2)}, u32[]{:S(2)}) collective-permute-start(bf16[1,8,2176]{2,1,0:T(8,128)(2,1)S(1)} %get-tuple-element.39), channel_id=1, source_target_pairs={{0,3},{1,2},{2,1},{3,0},{4,7},{5,6},{6,5},{7,4},{8,11},{9,10},{10,... | collective-permute-start | bytes 104456 | tf_op jit(solution)/shard_map/ppermute | solution.py:312
  21.3 0.1 collective-permute-done.8.refs_2_
  21.5 0.7 %collective-permute-done.9.refs_3_ = bf16[1,8,2176]{2,1,0:T(8,128)(2,1)S(1)} collective-permute-done((bf16[1,8,2176]{2,1,0:T(8,128)(2,1)S(1)}, bf16[1,8,2176]{2,1,0:T(8,128)(2,1)S(1)}, u32[]{:S(2)}, u32[]{:S(2)}) %collective-permute-start.9) | collective-permute-done | bytes 34848 | tf_op jit(solution)/shard_map/ppermute | solution.py:312
  22.2 0.0 collective-permute-done.7.refs_1_.refs_7_
  22.2 0.2 merge.1
  22.4 2.4 %collective-permute-start.10 = (bf16[1,8,2176]{2,1,0:T(8,128)(2,1)S(1)}, bf16[1,8,2176]{2,1,0:T(8,128)(2,1)S(1)}, u32[]{:S(2)}, u32[]{:S(2)}) collective-permute-start(bf16[1,8,2176]{2,1,0:T(8,128)(2,1)S(1)} %merge.1), channel_id=1, source_target_pairs={{0,9},{1,8},{2,11},{3,10},{4,13},{5,12},{6,15},{7,14},{8,1},{9,0},... | collective-permute-start | bytes 104456 | tf_op jit(solution)/shard_map/ppermute | solution.py:312
  24.9 0.0 collective-permute-done.11.refs_8_
  24.9 0.0 collective-permute-done.12.refs_9_
  24.9 1.9 %collective-permute-done.10.refs_6_ = bf16[1,8,2176]{2,1,0:T(8,128)(2,1)S(1)} collective-permute-done((bf16[1,8,2176]{2,1,0:T(8,128)(2,1)S(1)}, bf16[1,8,2176]{2,1,0:T(8,128)(2,1)S(1)}, u32[]{:S(2)}, u32[]{:S(2)}) %collective-permute-start.10) | collective-permute-done | bytes 34848 | tf_op jit(solution)/shard_map/ppermute | solution.py:312
  26.8 1.3 %finish.1 = (f32[4,1024]{1,0:T(4,128)}, bf16[256,1024]{1,0:T(8,128)(2,1)}, f32[2,2048]{1,0:T(2,128)}) custom-call(bf16[8,8,1536]{2,1,0:T(8,128)(2,1)S(1)} %order.1.slots_ref.refs_0_, bf16[8,8,1536]{2,1,0:T(8,128)(2,1)S(1)} %collective-permute-done.4.slots_ref.refs_1_, f32[32,256]{1,0:T(8,128)S(1)} %get-tuple-element.30.refs_2_, ...), custom_call_target="tpu_custom_call" | custom-call | tf_op jit(solution)/shard_map/finish/pallas_call | solution.py:368
  (4 shorter events, 0.0 us)
Async XLA Ops:
  0.6 0.7 %copy-start.4 = (bf16[2,2048]{1,0:T(2,128)(2,1)S(1)}, bf16[2,2048]{1,0:T(2,128)(2,1)}, u32[]{:S(2)}) copy-start(bf16[2,2048]{1,0:T(2,128)(2,1)} %grads_ref.1) | copy-start | bytes 24580
  0.6 0.7 %copy-start.3 = (bf16[2,2048]{1,0:T(2,128)(2,1)S(1)}, bf16[2,2048]{1,0:T(2,128)(2,1)}, u32[]{:S(2)}) copy-start(bf16[2,2048]{1,0:T(2,128)(2,1)} %outs_ref.1) | copy-start | bytes 24580
  0.7 0.7 %copy-start.2 = (bf16[4,1024]{1,0:T(4,128)(2,1)S(1)}, bf16[4,1024]{1,0:T(4,128)(2,1)}, u32[]{:S(2)}) copy-start(bf16[4,1024]{1,0:T(4,128)(2,1)} %params_ref.1) | copy-start | bytes 24580
  0.7 13.1 %collective-permute-start.5 = (bf16[256,1024]{1,0:T(8,128)(2,1)}, bf16[256,1024]{1,0:T(8,128)(2,1)S(1)}, u32[]{:S(2)}, u32[]{:S(2)}) collective-permute-start(bf16[256,1024]{1,0:T(8,128)(2,1)} %tokens_ref.1), channel_id=1, source_target_pairs={{0,1},{1,0},{2,3},{3,2},{4,5},{5,4},{6,7},{7,6},{8,9},{9,8},{10,11... | collective-permute-start | bytes 1572872 | tf_op jit(solution)/shard_map/ppermute | solution.py:322
  1.2 12.6 %collective-permute-start.6 = (bf16[256,1024]{1,0:T(8,128)(2,1)}, bf16[256,1024]{1,0:T(8,128)(2,1)S(1)}, u32[]{:S(2)}, u32[]{:S(2)}) collective-permute-start(bf16[256,1024]{1,0:T(8,128)(2,1)} %upstream_ref.1), channel_id=1, source_target_pairs={{0,1},{1,0},{2,3},{3,2},{4,5},{5,4},{6,7},{7,6},{8,9},{9,8},{10,11... | collective-permute-start | bytes 1572872 | tf_op jit(solution)/shard_map/ppermute | solution.py:322
  1.3 12.5 %copy-start.1 = (bf16[256,1024]{1,0:T(8,128)(2,1)S(1)}, bf16[256,1024]{1,0:T(8,128)(2,1)}, u32[]{:S(2)}) copy-start(bf16[256,1024]{1,0:T(8,128)(2,1)} %upstream_ref.1) | copy-start | bytes 1572868
  1.4 12.4 %copy-start = (bf16[256,1024]{1,0:T(8,128)(2,1)S(1)}, bf16[256,1024]{1,0:T(8,128)(2,1)}, u32[]{:S(2)}) copy-start(bf16[256,1024]{1,0:T(8,128)(2,1)} %tokens_ref.1) | copy-start | bytes 1572868
  1.4 5.2 %collective-permute-start = (bf16[1,8,1536]{2,1,0:T(8,128)(2,1)S(1)}, bf16[1,8,1536]{2,1,0:T(8,128)(2,1)S(1)}, u32[]{:S(2)}, u32[]{:S(2)}) collective-permute-start(bf16[1,8,1536]{2,1,0:T(8,128)(2,1)S(1)} %pack.1.mine_ref), channel_id=1, source_target_pairs={{0,9},{1,8},{2,11},{3,10},{4,13},{5,12},{6,15},{7,14},{8,1},{9,0},... | collective-permute-start | bytes 73736 | tf_op jit(solution)/shard_map/ppermute | solution.py:312
  6.6 4.8 %collective-permute-start.3 = (bf16[2,8,1536]{2,1,0:T(8,128)(2,1)S(1)}, bf16[2,8,1536]{2,1,0:T(8,128)(2,1)S(1)}, u32[]{:S(2)}, u32[]{:S(2)}) collective-permute-start(bf16[2,8,1536]{2,1,0:T(8,128)(2,1)S(1)} %pair.1.refs_0_), channel_id=1, source_target_pairs={{0,7},{1,6},{2,5},{3,4},{4,3},{5,2},{6,1},{7,0},{8,15},{9,14},{10,... | collective-permute-start | bytes 147464 | tf_op jit(solution)/shard_map/ppermute | solution.py:312
  9.3 3.5 %collective-permute-start.2 = (bf16[2,8,1536]{2,1,0:T(8,128)(2,1)S(1)}, bf16[2,8,1536]{2,1,0:T(8,128)(2,1)S(1)}, u32[]{:S(2)}, u32[]{:S(2)}) collective-permute-start(bf16[2,8,1536]{2,1,0:T(8,128)(2,1)S(1)} %pair.1.refs_0_), channel_id=1, source_target_pairs={{0,5},{1,4},{2,7},{3,6},{4,1},{5,0},{6,3},{7,2},{8,13},{9,12},{10,... | collective-permute-start | bytes 147464 | tf_op jit(solution)/shard_map/ppermute | solution.py:312
  9.8 3.8 %collective-permute-start.1 = (bf16[2,8,1536]{2,1,0:T(8,128)(2,1)S(1)}, bf16[2,8,1536]{2,1,0:T(8,128)(2,1)S(1)}, u32[]{:S(2)}, u32[]{:S(2)}) collective-permute-start(bf16[2,8,1536]{2,1,0:T(8,128)(2,1)S(1)} %pair.1.refs_0_), channel_id=1, source_target_pairs={{0,3},{1,2},{2,1},{3,0},{4,7},{5,6},{6,5},{7,4},{8,11},{9,10},{10,... | collective-permute-start | bytes 147464 | tf_op jit(solution)/shard_map/ppermute | solution.py:312
  13.6 1.5 %collective-permute-start.4 = (bf16[8,8,1536]{2,1,0:T(8,128)(2,1)S(1)}, bf16[8,8,1536]{2,1,0:T(8,128)(2,1)S(1)}, u32[]{:S(2)}, u32[]{:S(2)}) collective-permute-start(bf16[8,8,1536]{2,1,0:T(8,128)(2,1)S(1)} %order.1.slots_ref.refs_0_), channel_id=1, source_target_pairs={{0,1},{1,0},{2,3},{3,2},{4,5},{5,4},{6,7},{7,6},{8,9},{9,8},{10,11... | collective-permute-start | bytes 589832 | tf_op jit(solution)/shard_map/ppermute | solution.py:336
  16.1 6.1 %collective-permute-start.7 = (bf16[2,8,2176]{2,1,0:T(8,128)(2,1)S(1)}, bf16[2,8,2176]{2,1,0:T(8,128)(2,1)S(1)}, u32[]{:S(2)}, u32[]{:S(2)}) collective-permute-start(bf16[2,8,2176]{2,1,0:T(8,128)(2,1)S(1)} %get-tuple-element.35), channel_id=1, source_target_pairs={{0,7},{1,6},{2,5},{3,4},{4,3},{5,2},{6,1},{7,0},{8,15},{9,14},{10,... | collective-permute-start | bytes 208904 | tf_op jit(solution)/shard_map/ppermute | solution.py:312
  17.8 3.6 %collective-permute-start.8 = (bf16[1,8,2176]{2,1,0:T(8,128)(2,1)S(1)}, bf16[1,8,2176]{2,1,0:T(8,128)(2,1)S(1)}, u32[]{:S(2)}, u32[]{:S(2)}) collective-permute-start(bf16[1,8,2176]{2,1,0:T(8,128)(2,1)S(1)} %get-tuple-element.36), channel_id=1, source_target_pairs={{0,5},{1,4},{2,7},{3,6},{4,1},{5,0},{6,3},{7,2},{8,13},{9,12},{10,... | collective-permute-start | bytes 104456 | tf_op jit(solution)/shard_map/ppermute | solution.py:312
  18.3 3.9 %collective-permute-start.9 = (bf16[1,8,2176]{2,1,0:T(8,128)(2,1)S(1)}, bf16[1,8,2176]{2,1,0:T(8,128)(2,1)S(1)}, u32[]{:S(2)}, u32[]{:S(2)}) collective-permute-start(bf16[1,8,2176]{2,1,0:T(8,128)(2,1)S(1)} %get-tuple-element.37), channel_id=1, source_target_pairs={{0,3},{1,2},{2,1},{3,0},{4,7},{5,6},{6,5},{7,4},{8,11},{9,10},{10,... | collective-permute-start | bytes 104456 | tf_op jit(solution)/shard_map/ppermute | solution.py:312
  19.1 5.7 %collective-permute-start.11 = (bf16[1,8,2176]{2,1,0:T(8,128)(2,1)S(1)}, bf16[1,8,2176]{2,1,0:T(8,128)(2,1)S(1)}, u32[]{:S(2)}, u32[]{:S(2)}) collective-permute-start(bf16[1,8,2176]{2,1,0:T(8,128)(2,1)S(1)} %get-tuple-element.38), channel_id=1, source_target_pairs={{0,5},{1,4},{2,7},{3,6},{4,1},{5,0},{6,3},{7,2},{8,13},{9,12},{10,... | collective-permute-start | bytes 104456 | tf_op jit(solution)/shard_map/ppermute | solution.py:312
  20.7 4.2 %collective-permute-start.12 = (bf16[1,8,2176]{2,1,0:T(8,128)(2,1)S(1)}, bf16[1,8,2176]{2,1,0:T(8,128)(2,1)S(1)}, u32[]{:S(2)}, u32[]{:S(2)}) collective-permute-start(bf16[1,8,2176]{2,1,0:T(8,128)(2,1)S(1)} %get-tuple-element.39), channel_id=1, source_target_pairs={{0,3},{1,2},{2,1},{3,0},{4,7},{5,6},{6,5},{7,4},{8,11},{9,10},{10,... | collective-permute-start | bytes 104456 | tf_op jit(solution)/shard_map/ppermute | solution.py:312
  22.4 4.3 %collective-permute-start.10 = (bf16[1,8,2176]{2,1,0:T(8,128)(2,1)S(1)}, bf16[1,8,2176]{2,1,0:T(8,128)(2,1)S(1)}, u32[]{:S(2)}, u32[]{:S(2)}) collective-permute-start(bf16[1,8,2176]{2,1,0:T(8,128)(2,1)S(1)} %merge.1), channel_id=1, source_target_pairs={{0,9},{1,8},{2,11},{3,10},{4,13},{5,12},{6,15},{7,14},{8,1},{9,0},... | collective-permute-start | bytes 104456 | tf_op jit(solution)/shard_map/ppermute | solution.py:312
